TPU v7x, 128 devices: a whole 4x4x4 slice. The times are simulated.
128 devices in a mesh: row: 8 (over z_hi, x), col: 16 (over z_lo, y, core).
Axes of the slice: x: 4, y: 4, z: 4 (z_hi: 2, z_lo: 2; z = z_hi * 2 + z_lo), core: 2. Of those that a mesh axis runs over, the one named last changes fastest.
Arguments:
- ainv: float32 [24576, 24576], P('row', 'col'), may hold values from -0.0390625 to 0.0390625
- lpanel: float32 [24576, 1024], P(('row', 'col')), may hold values from -0.6 to 0.6
- dinv: float32 [1024, 512], P(('row', 'col')), may hold values from -6 to 6
- lmask: int32 [384, 2], P(('row', 'col')), may hold values 0 or 1
- hrows: float32 [24576, 1024], P(('row', 'col')), may hold values from -6 to 6
- hmask: int32 [384, 2], P(('row', 'col')), may hold values 0 or 1
- pole_weight: float32 [1], replicated, may hold values from 0.5 to 2
Outputs:
- offdiag: float32 [24576, 1024], P(('row', 'col'))
- diaginv: float32 [1024, 512], P(('row', 'col'))
- energy: float32 [24576], P(('row', 'col'))
All inputs are finite; a program needn't handle non-finite values. No bound on the sum of `lmask` or of `hmask` on one device may be relied on, other than what follows from the above.
Results may differ from a plain program's by a relative error of at most 0.00024.
Values sent between devices are 32-bit elements; how exact they have to be, the bound alone decides.
No kernel may reach another device: no remote copies, remote signals or barrier semaphores. Data moves between devices by JAX's collectives and lax.ppermute only.
A program may use at most 128 MiB of HBM per device.

v0:
```python
import jax
import jax.numpy as jnp
from jax import lax
from jax.sharding import Mesh
from jax.sharding import PartitionSpec as P

COL = ("col_0", "col_1", "col_2")
ROW = ("row_0", "row_1")
ROW_COL = ("row_0", "row_1", "col_0", "col_1", "col_2")


def from_root(block, axis, holder):
    block = jnp.where(lax.axis_index(axis) == holder, block, jnp.zeros_like(block))
    return lax.psum(block, axis)


def cut_along(array, dim, size):
    before, after = (array.shape[:dim], array.shape[dim + 1 :])
    return jnp.moveaxis(array.reshape(*before, size, -1, *after), dim, 0)


def sum_by_chip(array, chips, core, dim):
    sizes = (lax.axis_size(chips), lax.axis_size(core))
    parts = cut_along(array, dim, sizes[0] * sizes[1])
    inside = parts.shape[1:]
    parts = parts.reshape(*sizes, *inside).swapaxes(0, 1).reshape(-1, *inside)
    parts = lax.psum_scatter(parts, core, scatter_dimension=0, tiled=True)
    return lax.psum_scatter(parts, chips, scatter_dimension=0, tiled=True)[0]


def expand_local(mask, block_rows, supernode):
    count = mask.shape[0]
    full = jnp.broadcast_to(
        mask.astype(jnp.float32)[:, None, :, None], (count, block_rows, 2, supernode)
    )
    return full.reshape(count * block_rows, 2 * supernode)


def diag_blocks(left, right, supernode):
    total_rows = left.shape[0]
    blocks = jnp.einsum(
        "rsa,rsb->sab",
        left.reshape(total_rows, 2, supernode),
        right.reshape(total_rows, 2, supernode),
        precision=lax.Precision.HIGHEST,
    )
    return blocks.reshape(2 * supernode, supernode)


def local(ainv, lpanel, dinv, lmask, hrows, hmask, pole_weight):
    rows_local = lpanel.shape[0]
    supernode = lpanel.shape[1] // 2
    block_rows = rows_local // lmask.shape[0]
    pattern = expand_local(lmask, block_rows, supernode)
    lmasked = lpanel * pattern
    rowpanel = lax.all_gather(lmasked, COL, axis=0, tiled=True)
    ratio = lax.axis_size(COL) // lax.axis_size(ROW)
    colindex = lax.axis_index(COL)
    col_rows = ainv.shape[1]
    slab_piece = lax.dynamic_slice_in_dim(rowpanel, colindex % ratio * col_rows, col_rows, 0)
    colpanel = from_root(slab_piece, ROW, colindex // ratio)
    partial_value = jnp.dot(
        ainv, colpanel, precision=lax.Precision.HIGHEST, preferred_element_type=jnp.float32
    )
    owned = lax.psum_scatter(partial_value, COL, scatter_dimension=0, tiled=True)
    diag_term = diag_blocks(lmasked, owned, supernode)
    diag_sum = sum_by_chip(diag_term, ("row_0", "row_1", "col_0", "col_1"), "col_2", 0)
    offdiag = -owned * pattern
    diaginv = dinv + diag_sum
    hpattern = expand_local(hmask, block_rows, supernode)
    energy = pole_weight[0] * jnp.sum(hrows * hpattern * offdiag, axis=1)
    return (offdiag, diaginv, energy)


def solution(mesh):
    split = Mesh(mesh.devices.reshape(2, 4, 2, 4, 2), ("row_0", "row_1", "col_0", "col_1", "col_2"))
    placed = (
        P(ROW, COL),
        P(ROW_COL, None),
        P(ROW_COL, None),
        P(ROW_COL, None),
        P(ROW_COL, None),
        P(ROW_COL, None),
        P(),
    )
    return jax.shard_map(
        local,
        mesh=split,
        in_specs=placed,
        out_specs=(P(ROW_COL, None), P(ROW_COL, None), P(ROW_COL)),
        check_vma=False,
    )
```

profile of v0, /device:TPU:0, one launch (start us, length us, event | category | flops | bytes accessed | tf_op | source)
XLA Modules:
  0.0 835.3 jit_solution(6281680969533728642)
XLA Ops:
  7.2 0.7 convert_element_type.6
  7.9 0.1 copy.25
  8.0 0.3 broadcast_in_dim.6
  8.3 0.1 copy.35
  8.4 2.1 mul.33
  10.6 0.0 all-reduce.2.cloned.1.call-start
  10.7 74.4 %all-gather.2.cloned.1.call-done = f32[3072,1024]{1,0:T(8,128)} async-done(((f32[192,1024]{1,0:T(8,128)}), f32[3072,1024]{1,0:T(8,128)}) %all-gather.2.cloned.1.call-update) | async-done | bytes 12582928 | tf_op jit(solution)/shard_map/all_gather | solution.py:56
  85.1 6.7 dynamic-slice_select_fusion
  91.9 147.3 %all-reduce.2.cloned.1.call-done = f32[1536,1024]{1,0:T(8,128)} async-done(((f32[1536,1024]{1,0:T(8,128)}), f32[1536,1024]{1,0:T(8,128)}) %all-reduce.2.cloned.1.call-update) | async-done | bytes 6291472 | tf_op jit(solution)/shard_map/psum | solution.py:14
  239.2 122.8 %convolution_bitcast_fusion = f32[3072,1024]{0,1:T(8,128)} fusion(f32[1536,1024]{1,0:T(8,128)} %all-reduce.2.cloned.1.call-done, f32[3072,1536]{1,0:T(8,128)} %param.7), kind=kOutput, calls=%fused_computation | convolution fusion | flops 57982058496 | bytes 37748736 | tf_op jit(solution)/shard_map/dot_general | solution.py:62
  362.1 12.6 %copy.32 = f32[3072,1024]{1,0:T(8,128)} copy(f32[3072,1024]{0,1:T(8,128)} %convolution_bitcast_fusion) | data formatting | bytes 25165824
  374.7 0.0 reduce-scatter.6.cloned.1.call-start
  374.7 79.9 %reduce-scatter.10.cloned.1.call-done = f32[192,1024]{1,0:T(8,128)} async-done(((f32[3072,1024]{1,0:T(8,128)}), f32[192,1024]{1,0:T(8,128)}) %reduce-scatter.10.cloned.1.call-update) | async-done | bytes 786448 | tf_op jit(solution)/shard_map/reduce_scatter | solution.py:65
  454.6 1.5 copy.33
  456.1 3.5 fusion
  459.6 1.5 copy.29
  461.3 11.2 %reduce-scatter.6.cloned.1.call-done = f32[64,8,512]{2,1,0:T(8,128)} async-done(((f32[128,8,512]{2,1,0:T(8,128)}), f32[64,8,512]{2,1,0:T(8,128)}) %reduce-scatter.6.cloned.1.call-update) | async-done | bytes 1048592 | tf_op jit(solution)/shard_map/reduce_scatter | solution.py:27
  472.5 0.1 copy.30
  472.6 0.3 broadcast_in_dim.8
  472.8 0.1 copy.36
  473.7 1.1 multiply_reduce_fusion
  474.8 0.6 broadcast_multiply_fusion
  475.3 352.2 %reduce-scatter.8.cloned.1.call-done = f32[1,8,512]{2,1,0:T(8,128)} async-done(((f32[64,8,512]{2,1,0:T(8,128)}), f32[1,8,512]{2,1,0:T(8,128)}) %reduce-scatter.8.cloned.1.call-update) | async-done | bytes 16400 | tf_op jit(solution)/shard_map/reduce_scatter | solution.py:28
  827.5 1.3 bitcast_add_fusion
  (19 shorter events, 0.2 us)
Async XLA Ops:
  7.2 77.9 %all-gather.2.cloned.1.call-start = ((), (), s32[]{:S(2)}) async-start(), calls=%async_computation.3 | async-start | bytes 13369344 | tf_op jit(solution)/shard_map/all_gather | solution.py:56
  10.6 228.6 %all-reduce.2.cloned.1.call-start = ((), (), s32[]{:S(2)}) async-start(), calls=%async_computation.4 | async-start | bytes 12582912 | tf_op jit(solution)/shard_map/psum | solution.py:14
  91.9 362.7 %reduce-scatter.10.cloned.1.call-start = ((), (), s32[]{:S(2)}) async-start(), calls=%async_computation.7 | async-start | bytes 13369344 | tf_op jit(solution)/shard_map/reduce_scatter | solution.py:65
  374.6 81.4 %copy-start = (f32[192,1024]{1,0:T(8,128)S(1)}, f32[192,1024]{1,0:T(8,128)}, u32[]{:S(2)}) copy-start(f32[192,1024]{1,0:T(8,128)} %mul.33) | copy-start | bytes 2359300
  374.7 97.8 %copy-start.4 = (s32[3,2]{0,1:T(2,128)S(1)}, s32[3,2]{0,1:T(2,128)}, u32[]{:S(2)}) copy-start(s32[3,2]{0,1:T(2,128)} %param.12) | copy-start | bytes 76
  374.7 97.7 %reduce-scatter.6.cloned.1.call-start = ((), (), s32[]{:S(2)}) async-start(), calls=%async_computation.5 | async-start | bytes 3145728 | tf_op jit(solution)/shard_map/reduce_scatter | solution.py:27
  456.1 17.6 %copy-start.1 = (f32[192,1024]{1,0:T(8,128)S(1)}, f32[192,1024]{1,0:T(8,128)}, u32[]{:S(2)}) copy-start(f32[192,1024]{1,0:T(8,128)} %reduce-scatter.10.cloned.1.call-done) | copy-start | bytes 2359300
  459.6 14.1 %copy-start.2 = (f32[192,1024]{1,0:T(8,128)S(1)}, f32[192,1024]{1,0:T(8,128)}, u32[]{:S(2)}) copy-start(f32[192,1024]{1,0:T(8,128)} %param.11) | copy-start | bytes 2359300
  459.6 367.9 %copy-start.3 = (f32[8,512]{1,0:T(8,128)S(1)}, f32[8,512]{1,0:T(8,128)}, u32[]{:S(2)}) copy-start(f32[8,512]{1,0:T(8,128)} %param.9) | copy-start | bytes 49156
  461.2 366.3 %reduce-scatter.8.cloned.1.call-start = ((), (), s32[]{:S(2)}) async-start(), calls=%async_computation.6 | async-start | bytes 1064960 | tf_op jit(solution)/shard_map/reduce_scatter | solution.py:28
Sparse Core Ops, SparseCore 0:
  10.7 74.3 all-gather.1
  92.0 147.1 all-reduce.1
  374.8 79.7 reduce-scatter.9
  461.3 11.0 reduce-scatter.5
  474.7 352.7 reduce-scatter.7
where the time goes:
time: 836 us; the launch traced here: 835 us
  waiting for transfers between devices  665 us (80%)
  matrix products  126 us (15%)
  local copies, waits for them, and re-layouts  16.7 us (2%)
  between operations  14.6 us (2%)
  other arithmetic  12.5 us (1%)
    reduce_scatter x1, waiting for transfers between devices, sum_by_chip(): return lax.psum_scatter(parts, chips, scatter_dimension=0, tiled=True)[0]  352 us
    psum x1, waiting for transfers between devices, from_root(): return lax.psum(block, axis)  147 us
    dot_general x1, matrix products, local(): jnp.dot(ainv, colpanel, precision=lax.Precision.HIGHEST, preferred_elemen...  123 us
    reduce_scatter x1, waiting for transfers between devices, local(): lax.psum_scatter(partial_value, COL, scatter_dimension=0, tiled=True)  79.9 us
    all_gather x1, waiting for transfers between devices, local(): rowpanel = lax.all_gather(lmasked, COL, axis=0, tiled=True)  74.4 us
  transfers between devices with their start and end apart: 5, of which 5 were waited for; matrix products, arithmetic and copies ran while one was open for 0% of the time, Pallas kernels for 0%

commit v1 on v0

v1 whole, which is shorter than its diff:
```python
import functools

import jax
import jax.numpy as jnp
from jax import lax
from jax.experimental import pallas as pl
from jax.experimental.pallas import tpu as pltpu
from jax.sharding import Mesh
from jax.sharding import PartitionSpec as P

AXES = ("zh", "x", "zl", "y", "core")
SIZES = (2, 4, 2, 4, 2)


def shift(array, axis, by):
    size = lax.axis_size(axis)
    return lax.ppermute(array, axis, [(i, (i + by) % size) for i in range(size)])


def to_slabs(array):
    pairs = []
    for zh in range(2):
        for x in range(4):
            for zl in range(2):
                for y in range(4):
                    for core in range(2):
                        source = (((zh * 4 + x) * 2 + zl) * 4 + y) * 2 + core
                        target = (((core * 4 + y) * 2 + zh) * 4 + x) * 2 + zl
                        pairs.append((source, target))
    return lax.ppermute(array, AXES, pairs)


def split(value):
    high = value.astype(jnp.bfloat16)
    low = (value - high.astype(jnp.float32)).astype(jnp.bfloat16)
    return high, low


def product_kernel(where, a_ref, *refs):
    pieces, out_ref, high_ref, low_ref = refs[:8], refs[8], refs[9], refs[10]
    rows = pieces[0].shape[0]

    @pl.when((pl.program_id(0) == 0) & (pl.program_id(1) == 0))
    def _():
        for other in range(2):
            for by in range(4):
                place = lax.rem(where[1] + by, 4) * 2 + jnp.bitwise_xor(where[0], other)
                at = pl.ds(pl.multiple_of(place * rows, 64), rows)
                high, low = split(pieces[other * 4 + by][...])
                high_ref[at, :] = high
                low_ref[at, :] = low

    tiles, tile_rows, depth = a_ref.shape[1], a_ref.shape[3], a_ref.shape[4]
    a_high, a_low = split(a_ref[...].reshape(tiles * tile_rows, depth))
    dot = functools.partial(jnp.dot, preferred_element_type=jnp.float32)
    total = dot(a_low, high_ref[...]) + dot(a_high, low_ref[...]) + dot(a_high, high_ref[...])
    for tile in range(tiles):
        owner = pl.program_id(1) * tiles + tile
        by = lax.rem(owner - where[3] + 4, 4)
        out_ref[0, by] = total[tile * tile_rows : (tile + 1) * tile_rows]


def product(ainv, pieces, where, other_core):
    rows, width = pieces[0].shape
    depth = ainv.shape[1]
    tiles = 2
    blocks = ainv.reshape(2, 4, 2, rows, depth)

    def a_map(dz, part, where):
        return (
            jnp.bitwise_xor(where[2], dz),
            part,
            jnp.bitwise_xor(where[4], other_core),
            0,
            0,
        )

    flops = 2 * 8 * rows * depth * width * 3
    return pl.pallas_call(
        product_kernel,
        grid_spec=pltpu.PrefetchScalarGridSpec(
            num_scalar_prefetch=1,
            grid=(2, 4 // tiles),
            in_specs=[pl.BlockSpec((1, tiles, 1, rows, depth), a_map)]
            + [pl.BlockSpec((rows, width), lambda *_: (0, 0))] * 8,
            out_specs=pl.BlockSpec((1, 4, rows, width), lambda dz, part, where: (dz, 0, 0, 0)),
            scratch_shapes=[pltpu.VMEM((8 * rows, width), jnp.bfloat16)] * 2,
        ),
        out_shape=jax.ShapeDtypeStruct((2, 4, rows, width), jnp.float32),
        compiler_params=pltpu.CompilerParams(vmem_limit_bytes=44 * 1024 * 1024),
        cost_estimate=pl.CostEstimate(
            flops=flops, bytes_accessed=4 * (8 * rows * (depth + 2 * width)), transcendentals=0
        ),
    )(where, blocks, *pieces)


def gather_slab(piece):
    across = shift(piece, "zh", 1)
    from_left, from_right = shift(piece, "x", 1), shift(piece, "x", -1)
    across_left, across_right = shift(across, "x", 1), shift(across, "x", -1)
    opposite = shift(from_left, "x", 1)
    across_opposite = shift(across_right, "x", -1)
    return (
        piece,
        from_right,
        opposite,
        from_left,
        across,
        across_right,
        across_opposite,
        across_left,
    )


def reduce_to_owner(kept, came):
    part = lambda dz, by: kept[dz, by] + came[dz, by]
    up_far = shift(part(0, 2), "y", 1)
    down_far = shift(part(1, 2), "y", -1)
    up_second = shift(part(1, 1), "y", 1)
    down_first = shift(part(0, 3), "y", -1)
    up_first = shift(part(0, 1) + up_far, "y", 1)
    down_second = shift(part(1, 3) + down_far, "y", -1)
    second = part(1, 0) + up_second + down_second
    across = shift(second, "zl", 1)
    return part(0, 0) + up_first + down_first + across


def sum_diag(terms, index):
    at = lambda array, axis, i: lax.dynamic_index_in_dim(array, i, axis, keepdims=False)
    terms = at(terms, 4, index["core"]) + shift(at(terms, 4, 1 - index["core"]), "core", 1)
    for axis, dim in (("y", 3), ("x", 1)):
        total = at(terms, dim, index[axis])
        for by in (1, 3, 2):
            total = total + shift(at(terms, dim, (index[axis] + by) % 4), axis, by)
        terms = total
    own_high, own_low = terms[index["zh"]], terms[1 - index["zh"]]
    own = own_high[index["zl"]]
    near = shift(own_high[1 - index["zl"]], "zl", 1)
    far = shift(own_low[index["zl"]], "zh", 1)
    pairs = [(i, 3 - i) for i in range(4)]
    both = lax.ppermute(own_low[1 - index["zl"]], ("zh", "zl"), pairs)
    return own + near + far + both


def expand_local(mask, block_rows, supernode):
    count = mask.shape[0]
    full = jnp.broadcast_to(
        mask.astype(jnp.float32)[:, None, :, None], (count, block_rows, 2, supernode)
    )
    return full.reshape(count * block_rows, 2 * supernode)


def local(ainv, lpanel, dinv, lmask, hrows, hmask, pole_weight):
    rows_local = lpanel.shape[0]
    supernode = lpanel.shape[1] // 2
    block_rows = rows_local // lmask.shape[0]
    index = {axis: lax.axis_index(axis) for axis in AXES}
    where = jnp.stack([index[axis] for axis in AXES]).astype(jnp.int32)
    pattern = expand_local(lmask, block_rows, supernode)
    lmasked = lpanel * pattern
    owned, terms = [], []
    halves = [lmasked[:, :supernode], lmasked[:, supernode:]]
    for half in halves:
        pieces = gather_slab(to_slabs(half))
        came = shift(product(ainv, pieces, where, 1), "core", 1)
        kept = product(ainv, pieces, where, 0)
        mine = reduce_to_owner(kept, came)
        owned.append(mine)
        terms.append(
            lax.dot_general(
                half,
                mine,
                (((0,), (0,)), ((), ())),
                precision=lax.Precision.HIGHEST,
                preferred_element_type=jnp.float32,
            )
        )
    diag_rows = dinv.shape[0]
    diag = jnp.stack(terms).reshape(*SIZES, diag_rows, supernode)
    diaginv = dinv + sum_diag(diag, index)
    offdiag = -jnp.concatenate(owned, axis=1) * pattern
    hpattern = expand_local(hmask, block_rows, supernode)
    energy = pole_weight[0] * jnp.sum(hrows * hpattern * offdiag, axis=1)
    return (offdiag, diaginv, energy)


def solution(mesh):
    split_mesh = Mesh(mesh.devices.reshape(*SIZES), AXES)
    rows = P(AXES, None)
    return jax.shard_map(
        local,
        mesh=split_mesh,
        in_specs=(P(("zh", "x"), ("zl", "y", "core")), rows, rows, rows, rows, rows, P()),
        out_specs=(rows, rows, P(AXES)),
        check_vma=False,
    )
```

time: 836 us -> 240 us (0.29)
  waiting for transfers between devices: 665 us -> 57.7 us
  matrix products: 126 us -> 2.19 us
  starting transfers between devices: 0.2 us -> 109 us
  Pallas kernels: 0 us -> 43.9 us
  local copies, waits for them, and re-layouts: 16.7 us -> 3.07 us
  between operations: 14.6 us -> 1.85 us
  other arithmetic: 12.5 us -> 21.4 us
    reduce_scatter x3 -> x0, waiting for transfers between devices: 443 us -> none  [the longest x1 352 us: sum_by_chip(): return lax.psum_scatter(parts, chips, scatter_dimension=0, tiled=True)[0]]
    psum x1 -> x0, waiting for transfers between devices: 147 us -> none  [from_root(): return lax.psum(block, axis)]
    dot_general x2, matrix products: 126 us -> 2.19 us  [local(): lax.dot_general(half, mine, (((0,), (0,)), ((), ())), precision=lax.Preci...]
    ppermute x0 -> x42, starting transfers between devices: none -> 109 us  [the longest x39 107 us: shift(): lax.ppermute(array, axis, [(i, (i + by) % size) for i in range(size)])]
    all_gather x1 -> x0, waiting for transfers between devices: 74.4 us -> none  [local(): rowpanel = lax.all_gather(lmasked, COL, axis=0, tiled=True)]
    ppermute x0 -> x42, waiting for transfers between devices: none -> 57.7 us  [the longest x39 57.4 us: shift(): lax.ppermute(array, axis, [(i, (i + by) % size) for i in range(size)])]
    pallas_call x0 -> x4, Pallas kernels: none -> 43.9 us  [product(): pl.pallas_call(product_kernel, grid_spec=pltpu.PrefetchScalarGridSpec(num...]
    add x1 -> x12, other arithmetic: 1.33 us -> 16 us  [the longest x2 4.08 us: reduce_to_owner(): part = lambda dz, by: kept[dz, by] + came[dz, by]]
  transfers between devices with their start and end apart: 5 -> 42, of which waited for: 5 -> 21; matrix products, arithmetic and copies ran while one was open for 0% -> 7% of each run, Pallas kernels for 0% -> 18%
where the time goes in v1:
time: 240 us
  starting transfers between devices  109 us (45%)
  waiting for transfers between devices  57.7 us (24%)
  Pallas kernels  43.9 us (18%)
  other arithmetic  21.4 us (9%)
  local copies, waits for them, and re-layouts  3.07 us (1%)
    ppermute x39, starting transfers between devices, shift(): lax.ppermute(array, axis, [(i, (i + by) % size) for i in range(size)])  107 us
    ppermute x39, waiting for transfers between devices, shift(): lax.ppermute(array, axis, [(i, (i + by) % size) for i in range(size)])  57.4 us
    pallas_call x4, Pallas kernels, product(): pl.pallas_call(product_kernel, grid_spec=pltpu.PrefetchScalarGridSpec(num...  43.9 us
  transfers between devices with their start and end apart: 42, of which 21 were waited for; matrix products, arithmetic and copies ran while one was open for 7% of the time, Pallas kernels for 18%

profile of v1, /device:TPU:0, one launch (start us, length us, event | category | flops | bytes accessed | tf_op | source)
XLA Modules:
  0.0 239.6 jit_solution(18150410681943994300)
XLA Ops:
  4.9 18.3 %collective-permute-start.4 = (f32[192,512]{1,0:T(8,128)S(1)}, f32[192,512]{1,0:T(8,128)S(1)}, u32[]{:S(2)}, u32[]{:S(2)}) collective-permute-start(f32[192,512]{1,0:T(8,128)S(1)} %collective-permute-done.refs_0_), channel_id=1, source_target_pairs={{0,64},{64,0},{1,65},{65,1},{2,66},{66,2},{3,67},{67,3},{4,68},{68... | collective-permute-start | bytes 1179656 | tf_op jit(solution)/shard_map/ppermute | solution.py:17
  23.1 12.6 %collective-permute-start.20 = (f32[192,512]{1,0:T(8,128)S(1)}, f32[192,512]{1,0:T(8,128)S(1)}, u32[]{:S(2)}, u32[]{:S(2)}) collective-permute-start(f32[192,512]{1,0:T(8,128)S(1)} %collective-permute-done.16.refs_0_), channel_id=1, source_target_pairs={{0,64},{64,0},{1,65},{65,1},{2,66},{66,2},{3,67},{67,3},{4,68},{68... | collective-permute-start | bytes 1179656 | tf_op jit(solution)/shard_map/ppermute | solution.py:17
  35.8 12.2 %collective-permute-start.2 = (f32[192,512]{1,0:T(8,128)S(1)}, f32[192,512]{1,0:T(8,128)S(1)}, u32[]{:S(2)}, u32[]{:S(2)}) collective-permute-start(f32[192,512]{1,0:T(8,128)S(1)} %collective-permute-done.refs_0_), channel_id=1, source_target_pairs={{0,16},{16,32},{32,48},{48,0},{1,17},{17,33},{33,49},{49,1},{2,18}... | collective-permute-start | bytes 1179656 | tf_op jit(solution)/shard_map/ppermute | solution.py:17
  50.0 8.0 %collective-permute-start.5 = (f32[192,512]{1,0:T(8,128)S(1)}, f32[192,512]{1,0:T(8,128)S(1)}, u32[]{:S(2)}, u32[]{:S(2)}) collective-permute-start(f32[192,512]{1,0:T(8,128)S(1)} %collective-permute-done.4.refs_4_), channel_id=1, source_target_pairs={{0,48},{16,0},{32,16},{48,32},{1,49},{17,1},{33,17},{49,33},{2,50}... | collective-permute-start | bytes 1179656 | tf_op jit(solution)/shard_map/ppermute | solution.py:17
  58.0 7.6 %collective-permute-start.21 = (f32[192,512]{1,0:T(8,128)S(1)}, f32[192,512]{1,0:T(8,128)S(1)}, u32[]{:S(2)}, u32[]{:S(2)}) collective-permute-start(f32[192,512]{1,0:T(8,128)S(1)} %collective-permute-done.20.refs_4_), channel_id=1, source_target_pairs={{0,48},{16,0},{32,16},{48,32},{1,49},{17,1},{33,17},{49,33},{2,50}... | collective-permute-start | bytes 1179656 | tf_op jit(solution)/shard_map/ppermute | solution.py:17
  65.7 5.9 %collective-permute-done.18.refs_3_ = f32[192,512]{1,0:T(8,128)S(1)} collective-permute-done((f32[192,512]{1,0:T(8,128)S(1)}, f32[192,512]{1,0:T(8,128)S(1)}, u32[]{:S(2)}, u32[]{:S(2)}) %collective-permute-start.18) | collective-permute-done | bytes 393248 | tf_op jit(solution)/shard_map/ppermute | solution.py:17
  71.6 3.3 %collective-permute-start.6 = (f32[192,512]{1,0:T(8,128)S(1)}, f32[192,512]{1,0:T(8,128)}, u32[]{:S(2)}, u32[]{:S(2)}) collective-permute-start(f32[192,512]{1,0:T(8,128)S(1)} %collective-permute-done.5.refs_5_), channel_id=1, source_target_pairs={{0,48},{16,0},{32,16},{48,32},{1,49},{17,1},{33,17},{49,33},{2,50}... | collective-permute-start | bytes 1179656 | tf_op jit(solution)/shard_map/ppermute | solution.py:17
  76.0 3.7 %collective-permute-start.17 = (f32[192,512]{1,0:T(8,128)S(1)}, f32[192,512]{1,0:T(8,128)S(1)}, u32[]{:S(2)}, u32[]{:S(2)}) collective-permute-start(f32[192,512]{1,0:T(8,128)S(1)} %collective-permute-done.16.refs_0_), channel_id=1, source_target_pairs={{0,48},{16,0},{32,16},{48,32},{1,49},{17,1},{33,17},{49,33},{2,50}... | collective-permute-start | bytes 1179656 | tf_op jit(solution)/shard_map/ppermute | solution.py:17
  79.7 4.7 %collective-permute-done.21.refs_5_ = f32[192,512]{1,0:T(8,128)S(1)} collective-permute-done((f32[192,512]{1,0:T(8,128)S(1)}, f32[192,512]{1,0:T(8,128)S(1)}, u32[]{:S(2)}, u32[]{:S(2)}) %collective-permute-start.21) | collective-permute-done | bytes 393248 | tf_op jit(solution)/shard_map/ppermute | solution.py:17
  92.8 11.1 %shard_map.95 = f32[2,4,192,512]{3,2,1,0:T(8,128)S(1)} custom-call(s32[5]{0:T(128)S(1)} %stack.32.where, f32[2,4,2,192,1536]{4,3,2,1,0:T(8,128)} %bitcast.129, f32[192,512]{1,0:T(8,128)S(1)} %collective-permute-done.refs_0_, f32[192,512]{1,0:T(8,128)S(1)} %collective-permute-done.1.refs_1_, f32[192,512]{1,0:T(8,128)} %collective-permute-done.3.refs_2_, ...), custom_call_target="tpu_custom_call" | custom-call | flops 7247757312 | bytes 15728640 | tf_op jit(solution)/shard_map/pallas_call | solution.py:79
  107.3 10.8 %shard_map.97 = f32[2,4,192,512]{3,2,1,0:T(8,128)S(1)} custom-call(s32[5]{0:T(128)S(1)} %stack.32.where, f32[2,4,2,192,1536]{4,3,2,1,0:T(8,128)} %bitcast.130, f32[192,512]{1,0:T(8,128)S(1)} %collective-permute-done.16.refs_0_, f32[192,512]{1,0:T(8,128)S(1)} %collective-permute-done.17.refs_1_, f32[192,512]{1,0:T(8,128)S(1)} %collective-permute-done.19.refs_2_, ...), custom_call_target="tpu_custom_call" | custom-call | flops 7247757312 | bytes 15728640 | tf_op jit(solution)/shard_map/pallas_call | solution.py:79
  118.4 11.1 %shard_map.94 = f32[2,4,192,512]{3,2,1,0:T(8,128)S(1)} custom-call(s32[5]{0:T(128)S(1)} %stack.32.where, f32[2,4,2,192,1536]{4,3,2,1,0:T(8,128)} %bitcast.131, f32[192,512]{1,0:T(8,128)S(1)} %copy-done.4, f32[192,512]{1,0:T(8,128)S(1)} %copy-done.16, f32[192,512]{1,0:T(8,128)} %collective-permute-done.3.refs_2_, f32[192,512]{1,0:T(8,128)S(1)} %copy-done.12, ...), custom_call_target="tpu_custom_call" | custom-call | flops 7247757312 | bytes 15728640 | tf_op jit(solution)/shard_map/pallas_call | solution.py:79
  132.1 3.2 %collective-permute-start.13 = (f32[192,512]{1,0:T(8,128)S(1)}, f32[192,512]{1,0:T(8,128)S(1)}, u32[]{:S(2)}, u32[]{:S(2)}) collective-permute-start(f32[192,512]{1,0:T(8,128)S(1)} %get-tuple-element.8), channel_id=1, source_target_pairs={{0,6},{2,0},{4,2},{6,4},{1,7},{3,1},{5,3},{7,5},{8,14},{10,8},{12,... | collective-permute-start | bytes 1179656 | tf_op jit(solution)/shard_map/ppermute | solution.py:17
  135.4 10.8 %shard_map.96 = f32[2,4,192,512]{3,2,1,0:T(8,128)S(1)} custom-call(s32[5]{0:T(128)S(1)} %stack.32.where, f32[2,4,2,192,1536]{4,3,2,1,0:T(8,128)} %bitcast.132, f32[192,512]{1,0:T(8,128)S(1)} %collective-permute-done.16.refs_0_, f32[192,512]{1,0:T(8,128)S(1)} %collective-permute-done.17.refs_1_, f32[192,512]{1,0:T(8,128)S(1)} %collective-permute-done.19.refs_2_, ...), custom_call_target="tpu_custom_call" | custom-call | flops 7247757312 | bytes 15728640 | tf_op jit(solution)/shard_map/pallas_call | solution.py:79
  147.8 3.2 %collective-permute-start.29 = (f32[192,512]{1,0:T(8,128)S(1)}, f32[192,512]{1,0:T(8,128)S(1)}, u32[]{:S(2)}, u32[]{:S(2)}) collective-permute-start(f32[192,512]{1,0:T(8,128)S(1)} %get-tuple-element.14), channel_id=1, source_target_pairs={{0,6},{2,0},{4,2},{6,4},{1,7},{3,1},{5,3},{7,5},{8,14},{10,8},{12,... | collective-permute-start | bytes 1179656 | tf_op jit(solution)/shard_map/ppermute | solution.py:17
  152.4 3.3 %collective-permute-start.14 = (f32[192,512]{1,0:T(8,128)S(1)}, f32[192,512]{1,0:T(8,128)S(1)}, u32[]{:S(2)}, u32[]{:S(2)}) collective-permute-start(f32[192,512]{1,0:T(8,128)S(1)} %get-tuple-element.6), channel_id=1, source_target_pairs={{0,6},{2,0},{4,2},{6,4},{1,7},{3,1},{5,3},{7,5},{8,14},{10,8},{12,... | collective-permute-start | bytes 1179656 | tf_op jit(solution)/shard_map/ppermute | solution.py:17
  155.7 5.3 %collective-permute-done.25 = f32[192,512]{1,0:T(8,128)S(1)} collective-permute-done((f32[192,512]{1,0:T(8,128)S(1)}, f32[192,512]{1,0:T(8,128)S(1)}, u32[]{:S(2)}, u32[]{:S(2)}) %collective-permute-start.25) | collective-permute-done | bytes 393248 | tf_op jit(solution)/shard_map/ppermute | solution.py:17
  162.2 3.3 %collective-permute-start.30 = (f32[192,512]{1,0:T(8,128)}, f32[192,512]{1,0:T(8,128)}, u32[]{:S(2)}, u32[]{:S(2)}) collective-permute-start(f32[192,512]{1,0:T(8,128)} %get-tuple-element.12), channel_id=1, source_target_pairs={{0,6},{2,0},{4,2},{6,4},{1,7},{3,1},{5,3},{7,5},{8,14},{10,8},{12,... | collective-permute-start | bytes 1179656 | tf_op jit(solution)/shard_map/ppermute | solution.py:17
  165.5 3.9 %collective-permute-done.12 = f32[192,512]{1,0:T(8,128)S(1)} collective-permute-done((f32[192,512]{1,0:T(8,128)S(1)}, f32[192,512]{1,0:T(8,128)S(1)}, u32[]{:S(2)}, u32[]{:S(2)}) %collective-permute-start.12) | collective-permute-done | bytes 393248 | tf_op jit(solution)/shard_map/ppermute | solution.py:17
  171.3 3.5 %collective-permute-start.15 = (f32[192,512]{1,0:T(8,128)}, f32[192,512]{1,0:T(8,128)}, u32[]{:S(2)}, u32[]{:S(2)}) collective-permute-start(f32[192,512]{1,0:T(8,128)} %fusion.24), channel_id=1, source_target_pairs={{0,8},{8,0},{1,9},{9,1},{2,10},{10,2},{3,11},{11,3},{4,12},{12,4},... | collective-permute-start | bytes 1179656 | tf_op jit(solution)/shard_map/ppermute | solution.py:17
  181.5 4.5 %collective-permute-done.11 = f32[192,512]{1,0:T(8,128)} collective-permute-done((f32[192,512]{1,0:T(8,128)}, f32[192,512]{1,0:T(8,128)}, u32[]{:S(2)}, u32[]{:S(2)}) %collective-permute-start.11) | collective-permute-done | bytes 393248 | tf_op jit(solution)/shard_map/ppermute | solution.py:17
  186.0 3.5 %collective-permute-start.31 = (f32[192,512]{1,0:T(8,128)S(1)}, f32[192,512]{1,0:T(8,128)S(1)}, u32[]{:S(2)}, u32[]{:S(2)}) collective-permute-start(f32[192,512]{1,0:T(8,128)S(1)} %fusion.9), channel_id=1, source_target_pairs={{0,8},{8,0},{1,9},{9,1},{2,10},{10,2},{3,11},{11,3},{4,12},{12,4},... | collective-permute-start | bytes 1179656 | tf_op jit(solution)/shard_map/ppermute | solution.py:17
  210.7 4.3 %collective-permute-done.35 = f32[2,4,2,8,512]{4,3,2,1,0:T(8,128)S(1)} collective-permute-done((f32[2,4,2,8,512]{4,3,2,1,0:T(8,128)}, f32[2,4,2,8,512]{4,3,2,1,0:T(8,128)S(1)}, u32[]{:S(2)}, u32[]{:S(2)}) %collective-permute-start.35) | collective-permute-done | bytes 262176 | tf_op jit(solution)/shard_map/ppermute | solution.py:17
  215.0 5.9 %collective-permute-done.34 = f32[2,4,2,8,512]{4,3,2,1,0:T(8,128)} collective-permute-done((f32[2,4,2,8,512]{4,3,2,1,0:T(8,128)S(1)}, f32[2,4,2,8,512]{4,3,2,1,0:T(8,128)}, u32[]{:S(2)}, u32[]{:S(2)}) %collective-permute-start.34) | collective-permute-done | bytes 262176 | tf_op jit(solution)/shard_map/ppermute | solution.py:17
  (144 shorter events, 73.6 us)
Async XLA Ops:
  4.2 19.0 %collective-permute-start.16 = (f32[192,512]{1,0:T(8,128)S(1)}, f32[192,512]{1,0:T(8,128)S(1)}, u32[]{:S(2)}, u32[]{:S(2)}) collective-permute-start(f32[192,512]{1,0:T(8,128)S(1)} %get-tuple-element.23), channel_id=1, source_target_pairs={{0,0},{1,64},{2,16},{3,80},{4,32},{5,96},{6,48},{7,112},{8,1},{9,6... | collective-permute-start | bytes 1179656 | tf_op jit(solution)/shard_map/ppermute | solution.py:30
  4.9 45.1 %collective-permute-start.4 = (f32[192,512]{1,0:T(8,128)S(1)}, f32[192,512]{1,0:T(8,128)S(1)}, u32[]{:S(2)}, u32[]{:S(2)}) collective-permute-start(f32[192,512]{1,0:T(8,128)S(1)} %collective-permute-done.refs_0_), channel_id=1, source_target_pairs={{0,64},{64,0},{1,65},{65,1},{2,66},{66,2},{3,67},{67,3},{4,68},{68... | collective-permute-start | bytes 1179656 | tf_op jit(solution)/shard_map/ppermute | solution.py:17
  23.1 34.9 %collective-permute-start.20 = (f32[192,512]{1,0:T(8,128)S(1)}, f32[192,512]{1,0:T(8,128)S(1)}, u32[]{:S(2)}, u32[]{:S(2)}) collective-permute-start(f32[192,512]{1,0:T(8,128)S(1)} %collective-permute-done.16.refs_0_), channel_id=1, source_target_pairs={{0,64},{64,0},{1,65},{65,1},{2,66},{66,2},{3,67},{67,3},{4,68},{68... | collective-permute-start | bytes 1179656 | tf_op jit(solution)/shard_map/ppermute | solution.py:17
  35.8 29.9 %collective-permute-start.2 = (f32[192,512]{1,0:T(8,128)S(1)}, f32[192,512]{1,0:T(8,128)S(1)}, u32[]{:S(2)}, u32[]{:S(2)}) collective-permute-start(f32[192,512]{1,0:T(8,128)S(1)} %collective-permute-done.refs_0_), channel_id=1, source_target_pairs={{0,16},{16,32},{32,48},{48,0},{1,17},{17,33},{33,49},{49,1},{2,18}... | collective-permute-start | bytes 1179656 | tf_op jit(solution)/shard_map/ppermute | solution.py:17
  48.0 23.6 %collective-permute-start.18 = (f32[192,512]{1,0:T(8,128)S(1)}, f32[192,512]{1,0:T(8,128)S(1)}, u32[]{:S(2)}, u32[]{:S(2)}) collective-permute-start(f32[192,512]{1,0:T(8,128)S(1)} %collective-permute-done.16.refs_0_), channel_id=1, source_target_pairs={{0,16},{16,32},{32,48},{48,0},{1,17},{17,33},{33,49},{49,1},{2,18}... | collective-permute-start | bytes 1179656 | tf_op jit(solution)/shard_map/ppermute | solution.py:17
  50.0 21.6 %collective-permute-start.5 = (f32[192,512]{1,0:T(8,128)S(1)}, f32[192,512]{1,0:T(8,128)S(1)}, u32[]{:S(2)}, u32[]{:S(2)}) collective-permute-start(f32[192,512]{1,0:T(8,128)S(1)} %collective-permute-done.4.refs_4_), channel_id=1, source_target_pairs={{0,48},{16,0},{32,16},{48,32},{1,49},{17,1},{33,17},{49,33},{2,50}... | collective-permute-start | bytes 1179656 | tf_op jit(solution)/shard_map/ppermute | solution.py:17
  58.0 18.0 %collective-permute-start.1 = (f32[192,512]{1,0:T(8,128)S(1)}, f32[192,512]{1,0:T(8,128)S(1)}, u32[]{:S(2)}, u32[]{:S(2)}) collective-permute-start(f32[192,512]{1,0:T(8,128)S(1)} %collective-permute-done.refs_0_), channel_id=1, source_target_pairs={{0,48},{16,0},{32,16},{48,32},{1,49},{17,1},{33,17},{49,33},{2,50}... | collective-permute-start | bytes 1179656 | tf_op jit(solution)/shard_map/ppermute | solution.py:17
  58.0 26.4 %collective-permute-start.21 = (f32[192,512]{1,0:T(8,128)S(1)}, f32[192,512]{1,0:T(8,128)S(1)}, u32[]{:S(2)}, u32[]{:S(2)}) collective-permute-start(f32[192,512]{1,0:T(8,128)S(1)} %collective-permute-done.20.refs_4_), channel_id=1, source_target_pairs={{0,48},{16,0},{32,16},{48,32},{1,49},{17,1},{33,17},{49,33},{2,50}... | collective-permute-start | bytes 1179656 | tf_op jit(solution)/shard_map/ppermute | solution.py:17
  65.7 18.7 %collective-permute-start.3 = (f32[192,512]{1,0:T(8,128)S(1)}, f32[192,512]{1,0:T(8,128)}, u32[]{:S(2)}, u32[]{:S(2)}) collective-permute-start(f32[192,512]{1,0:T(8,128)S(1)} %collective-permute-done.2.refs_3_), channel_id=1, source_target_pairs={{0,16},{16,32},{32,48},{48,0},{1,17},{17,33},{33,49},{49,1},{2,18}... | collective-permute-start | bytes 1179656 | tf_op jit(solution)/shard_map/ppermute | solution.py:17
  71.6 21.2 %collective-permute-start.6 = (f32[192,512]{1,0:T(8,128)S(1)}, f32[192,512]{1,0:T(8,128)}, u32[]{:S(2)}, u32[]{:S(2)}) collective-permute-start(f32[192,512]{1,0:T(8,128)S(1)} %collective-permute-done.5.refs_5_), channel_id=1, source_target_pairs={{0,48},{16,0},{32,16},{48,32},{1,49},{17,1},{33,17},{49,33},{2,50}... | collective-permute-start | bytes 1179656 | tf_op jit(solution)/shard_map/ppermute | solution.py:17
  76.0 28.2 %collective-permute-start.17 = (f32[192,512]{1,0:T(8,128)S(1)}, f32[192,512]{1,0:T(8,128)S(1)}, u32[]{:S(2)}, u32[]{:S(2)}) collective-permute-start(f32[192,512]{1,0:T(8,128)S(1)} %collective-permute-done.16.refs_0_), channel_id=1, source_target_pairs={{0,48},{16,0},{32,16},{48,32},{1,49},{17,1},{33,17},{49,33},{2,50}... | collective-permute-start | bytes 1179656 | tf_op jit(solution)/shard_map/ppermute | solution.py:17
  84.4 19.8 %collective-permute-start.23 = (f32[192,512]{1,0:T(8,128)S(1)}, f32[192,512]{1,0:T(8,128)S(1)}, u32[]{:S(2)}, u32[]{:S(2)}) collective-permute-start(f32[192,512]{1,0:T(8,128)S(1)} %collective-permute-done.20.refs_4_), channel_id=1, source_target_pairs={{0,16},{16,32},{32,48},{48,0},{1,17},{17,33},{33,49},{49,1},{2,18}... | collective-permute-start | bytes 1179656 | tf_op jit(solution)/shard_map/ppermute | solution.py:17
  84.4 19.8 %collective-permute-start.19 = (f32[192,512]{1,0:T(8,128)S(1)}, f32[192,512]{1,0:T(8,128)S(1)}, u32[]{:S(2)}, u32[]{:S(2)}) collective-permute-start(f32[192,512]{1,0:T(8,128)S(1)} %collective-permute-done.18.refs_3_), channel_id=1, source_target_pairs={{0,16},{16,32},{32,48},{48,0},{1,17},{17,33},{33,49},{49,1},{2,18}... | collective-permute-start | bytes 1179656 | tf_op jit(solution)/shard_map/ppermute | solution.py:17
  88.5 18.7 %collective-permute-start.22 = (f32[192,512]{1,0:T(8,128)S(1)}, f32[192,512]{1,0:T(8,128)S(1)}, u32[]{:S(2)}, u32[]{:S(2)}) collective-permute-start(f32[192,512]{1,0:T(8,128)S(1)} %collective-permute-done.21.refs_5_), channel_id=1, source_target_pairs={{0,48},{16,0},{32,16},{48,32},{1,49},{17,1},{33,17},{49,33},{2,50}... | collective-permute-start | bytes 1179656 | tf_op jit(solution)/shard_map/ppermute | solution.py:17
  104.0 25.6 %collective-permute-start.8 = (f32[2,4,192,512]{3,2,1,0:T(8,128)S(1)}, f32[2,4,192,512]{3,2,1,0:T(8,128)}, u32[]{:S(2)}, u32[]{:S(2)}) collective-permute-start(f32[2,4,192,512]{3,2,1,0:T(8,128)S(1)} %shard_map.95), channel_id=1, source_target_pairs={{0,1},{1,0},{2,3},{3,2},{4,5},{5,4},{6,7},{7,6},{8,9},{9,8},{10,11... | collective-permute-start | bytes 9437192 | tf_op jit(solution)/shard_map/ppermute | solution.py:17
  118.1 28.1 %collective-permute-start.24 = (f32[2,4,192,512]{3,2,1,0:T(8,128)S(1)}, f32[2,4,192,512]{3,2,1,0:T(8,128)S(1)}, u32[]{:S(2)}, u32[]{:S(2)}) collective-permute-start(f32[2,4,192,512]{3,2,1,0:T(8,128)S(1)} %shard_map.97), channel_id=1, source_target_pairs={{0,1},{1,0},{2,3},{3,2},{4,5},{5,4},{6,7},{7,6},{8,9},{9,8},{10,11... | collective-permute-start | bytes 9437192 | tf_op jit(solution)/shard_map/ppermute | solution.py:17
  132.1 18.9 %collective-permute-start.9 = (f32[192,512]{1,0:T(8,128)S(1)}, f32[192,512]{1,0:T(8,128)S(1)}, u32[]{:S(2)}, u32[]{:S(2)}) collective-permute-start(f32[192,512]{1,0:T(8,128)S(1)} %get-tuple-element.7), channel_id=1, source_target_pairs={{0,2},{2,4},{4,6},{6,0},{1,3},{3,5},{5,7},{7,1},{8,10},{10,12},{12... | collective-permute-start | bytes 1179656 | tf_op jit(solution)/shard_map/ppermute | solution.py:17
  132.1 18.9 %collective-permute-start.13 = (f32[192,512]{1,0:T(8,128)S(1)}, f32[192,512]{1,0:T(8,128)S(1)}, u32[]{:S(2)}, u32[]{:S(2)}) collective-permute-start(f32[192,512]{1,0:T(8,128)S(1)} %get-tuple-element.8), channel_id=1, source_target_pairs={{0,6},{2,0},{4,2},{6,4},{1,7},{3,1},{5,3},{7,5},{8,14},{10,8},{12,... | collective-permute-start | bytes 1179656 | tf_op jit(solution)/shard_map/ppermute | solution.py:17
  151.0 18.4 %collective-permute-start.12 = (f32[192,512]{1,0:T(8,128)S(1)}, f32[192,512]{1,0:T(8,128)S(1)}, u32[]{:S(2)}, u32[]{:S(2)}) collective-permute-start(f32[192,512]{1,0:T(8,128)S(1)} %get-tuple-element.9), channel_id=1, source_target_pairs={{0,2},{2,4},{4,6},{6,0},{1,3},{3,5},{5,7},{7,1},{8,10},{10,12},{12... | collective-permute-start | bytes 1179656 | tf_op jit(solution)/shard_map/ppermute | solution.py:17
  152.4 17.0 %collective-permute-start.14 = (f32[192,512]{1,0:T(8,128)S(1)}, f32[192,512]{1,0:T(8,128)S(1)}, u32[]{:S(2)}, u32[]{:S(2)}) collective-permute-start(f32[192,512]{1,0:T(8,128)S(1)} %get-tuple-element.6), channel_id=1, source_target_pairs={{0,6},{2,0},{4,2},{6,4},{1,7},{3,1},{5,3},{7,5},{8,14},{10,8},{12,... | collective-permute-start | bytes 1179656 | tf_op jit(solution)/shard_map/ppermute | solution.py:17
  155.7 22.2 %collective-permute-start.28 = (f32[192,512]{1,0:T(8,128)}, f32[192,512]{1,0:T(8,128)}, u32[]{:S(2)}, u32[]{:S(2)}) collective-permute-start(f32[192,512]{1,0:T(8,128)} %get-tuple-element.15), channel_id=1, source_target_pairs={{0,2},{2,4},{4,6},{6,0},{1,3},{3,5},{5,7},{7,1},{8,10},{10,12},{12... | collective-permute-start | bytes 1179656 | tf_op jit(solution)/shard_map/ppermute | solution.py:17
  165.4 20.5 %collective-permute-start.11 = (f32[192,512]{1,0:T(8,128)}, f32[192,512]{1,0:T(8,128)}, u32[]{:S(2)}, u32[]{:S(2)}) collective-permute-start(f32[192,512]{1,0:T(8,128)} %get-tuple-element.10), channel_id=1, source_target_pairs={{0,6},{2,0},{4,2},{6,4},{1,7},{3,1},{5,3},{7,5},{8,14},{10,8},{12,... | collective-permute-start | bytes 1179656 | tf_op jit(solution)/shard_map/ppermute | solution.py:17
  169.4 20.1 %collective-permute-start.10 = (f32[192,512]{1,0:T(8,128)S(1)}, f32[192,512]{1,0:T(8,128)}, u32[]{:S(2)}, u32[]{:S(2)}) collective-permute-start(f32[192,512]{1,0:T(8,128)S(1)} %get-tuple-element.5), channel_id=1, source_target_pairs={{0,2},{2,4},{4,6},{6,0},{1,3},{3,5},{5,7},{7,1},{8,10},{10,12},{12... | collective-permute-start | bytes 1179656 | tf_op jit(solution)/shard_map/ppermute | solution.py:17
  171.3 18.2 %collective-permute-start.15 = (f32[192,512]{1,0:T(8,128)}, f32[192,512]{1,0:T(8,128)}, u32[]{:S(2)}, u32[]{:S(2)}) collective-permute-start(f32[192,512]{1,0:T(8,128)} %fusion.24), channel_id=1, source_target_pairs={{0,8},{8,0},{1,9},{9,1},{2,10},{10,2},{3,11},{11,3},{4,12},{12,4},... | collective-permute-start | bytes 1179656 | tf_op jit(solution)/shard_map/ppermute | solution.py:17
  (42 other events, 873.5 us)

commit v2 on v1

v2 whole, which is shorter than its diff:
```python
import functools

import jax
import jax.numpy as jnp
from jax import lax
from jax.experimental import pallas as pl
from jax.experimental.pallas import tpu as pltpu
from jax.sharding import Mesh
from jax.sharding import PartitionSpec as P

AXES = ("zh", "x", "zl", "y", "core")
SIZES = (2, 4, 2, 4, 2)


def shift(array, axis, by):
    size = lax.axis_size(axis)
    return lax.ppermute(array, axis, [(i, (i + by) % size) for i in range(size)])


def to_slabs(array):
    pairs = []
    for zh in range(2):
        for x in range(4):
            for zl in range(2):
                for y in range(4):
                    for core in range(2):
                        source = (((zh * 4 + x) * 2 + zl) * 4 + y) * 2 + core
                        to_x = (x + y % 2 * 2 + core) % 4
                        target = (((y // 2 * 4 + to_x) * 2 + zh) * 4 + x) * 2 + zl
                        pairs.append((source, target))
    return lax.ppermute(array, AXES, pairs)


def split(value):
    high = value.astype(jnp.bfloat16)
    low = (value - high.astype(jnp.float32)).astype(jnp.bfloat16)
    return high, low


def load_pieces(where, pieces, columns, high_ref, low_ref):
    rows = pieces[0].shape[0]
    start = lambda by: lax.rem(where[1] + by - where[3] + 4, 4) * rows
    places = (start(0), start(1), start(3), start(2), start(2) + rows // 2)
    for piece, place in zip(pieces, places):
        at = pl.ds(pl.multiple_of(place, 32), piece.shape[0])
        high_ref[at, :], low_ref[at, :] = split(piece[:, columns])


def three_products(a, high_ref, low_ref):
    high, low = split(a)
    dot = functools.partial(jnp.dot, preferred_element_type=jnp.float32)
    return dot(low, high_ref[...]) + dot(high, low_ref[...]) + dot(high, high_ref[...])


def near_kernel(where, a_ref, *refs):
    pieces, out_ref, high_ref, low_ref = refs[:5], *refs[5:]

    @pl.when(pl.program_id(0) == 0)
    def _():
        load_pieces(where, pieces, slice(None), high_ref, low_ref)

    out_ref[...] = three_products(a_ref[...], high_ref, low_ref)


def near_product(ainv, pieces, where):
    total, depth = ainv.shape
    rows, width = pieces[0].shape
    tile = 2 * rows
    return pl.pallas_call(
        near_kernel,
        grid_spec=pltpu.PrefetchScalarGridSpec(
            num_scalar_prefetch=1,
            grid=(total // tile,),
            in_specs=[pl.BlockSpec((tile, depth // 2), lambda i, where: (i, where[0]))]
            + [pl.BlockSpec(memory_space=pltpu.VMEM)] * 5,
            out_specs=pl.BlockSpec((tile, width), lambda i, where: (i, 0)),
            scratch_shapes=[pltpu.VMEM((depth // 2, width), jnp.bfloat16)] * 2,
        ),
        out_shape=jax.ShapeDtypeStruct((total, width), jnp.float32),
        compiler_params=pltpu.CompilerParams(vmem_limit_bytes=36 * 1024 * 1024),
        cost_estimate=pl.CostEstimate(
            flops=3 * total * depth * width,
            bytes_accessed=4 * total * (depth // 2 + width),
            transcendentals=0,
        ),
    )(where, ainv, *pieces)


def far_kernel(columns, where, a_ref, near_ref, *refs):
    pieces, given_ref, kept_ref, high_ref, low_ref = refs[:5], *refs[5:]
    half, part = pl.program_id(0), pl.program_id(2)

    @pl.when((half == 0) & (pl.program_id(1) == 0) & (part == 0))
    def _():
        load_pieces(where, pieces, columns, high_ref, low_ref)

    tiles, tile_rows, depth = a_ref.shape[1], a_ref.shape[3], a_ref.shape[4]
    total = three_products(a_ref[...].reshape(tiles * tile_rows, depth), high_ref, low_ref)
    total = total + near_ref[...].reshape(total.shape)
    for which, out_ref in enumerate((given_ref, kept_ref)):

        @pl.when(half == which)
        def _():
            for tile in range(tiles):
                by = lax.rem(part * tiles + tile - where[3] + 4, 4)
                out_ref[0, by] = total[tile * tile_rows : (tile + 1) * tile_rows]


def far_product(ainv, near, pieces, where, supernode):
    total, depth = ainv.shape
    rows, width = pieces[0].shape[0], pieces[0].shape[1] // 2
    tiles = 2

    def rows_of(half, dz, part, where):
        core = jnp.bitwise_xor(where[4], 1 - half)
        return jnp.bitwise_xor(where[2], dz), part, core, 0

    def a_map(half, dz, part, where):
        return *rows_of(half, dz, part, where), 1 - where[0]

    def near_map(half, dz, part, where):
        return *rows_of(half, dz, part, where), supernode

    def given_map(half, dz, part, where):
        return jnp.maximum(half, dz), 0, 0, 0

    def kept_map(half, dz, part, where):
        return half * dz, 0, 0, 0

    columns = slice(supernode * width, (supernode + 1) * width)
    return pl.pallas_call(
        functools.partial(far_kernel, columns),
        grid_spec=pltpu.PrefetchScalarGridSpec(
            num_scalar_prefetch=1,
            grid=(2, 2, 4 // tiles),
            in_specs=[
                pl.BlockSpec((1, tiles, 1, rows, depth // 2), a_map),
                pl.BlockSpec((1, tiles, 1, rows, width), near_map),
            ]
            + [pl.BlockSpec(memory_space=pltpu.VMEM)] * 5,
            out_specs=[
                pl.BlockSpec((1, 4, rows, width), given_map),
                pl.BlockSpec((1, 4, rows, width), kept_map),
            ],
            scratch_shapes=[pltpu.VMEM((depth // 2, width), jnp.bfloat16)] * 2,
        ),
        out_shape=[jax.ShapeDtypeStruct((2, 4, rows, width), jnp.float32)] * 2,
        compiler_params=pltpu.CompilerParams(vmem_limit_bytes=36 * 1024 * 1024),
        cost_estimate=pl.CostEstimate(
            flops=3 * total * depth * width,
            bytes_accessed=4 * total * (depth // 2 + 2 * width),
            transcendentals=0,
        ),
    )(
        where,
        ainv.reshape(2, 4, 2, rows, depth),
        near.reshape(2, 4, 2, rows, 2 * width),
        *pieces,
    )


def fence(*arrays):
    return lax.optimization_barrier(arrays)


def reduce_to_owner(kept, came):
    part = lambda dz, by: kept[dz, by] + came[dz, by]
    up_far = shift(part(0, 2), "y", 1)
    down_far = shift(part(1, 2), "y", -1)
    up_second = shift(part(1, 1), "y", 1)
    down_first = shift(part(0, 3), "y", -1)
    up_first = shift(part(0, 1) + up_far, "y", 1)
    down_second = shift(part(1, 3) + down_far, "y", -1)
    second = part(1, 0) + up_second + down_second
    across = shift(second, "zl", 1)
    return part(0, 0) + up_first + down_first + across


def sum_diag(terms, index):
    rows, width = terms.shape[0] // 128, terms.shape[1]
    terms = terms.reshape(16, 4, 2, rows, width)
    at = lambda array, axis, i: lax.dynamic_index_in_dim(array, i, axis, keepdims=False)
    terms = at(terms, 2, index["core"]) + shift(at(terms, 2, 1 - index["core"]), "core", 1)
    total = at(terms, 1, index["y"])
    for by in (1, 3, 2):
        total = total + shift(at(terms, 1, (index["y"] + by) % 4), "y", by)
    return jnp.sum(lax.all_to_all(total, ("zh", "x", "zl"), 0, 0, tiled=True), axis=0)


def expand_local(mask, block_rows, supernode):
    count = mask.shape[0]
    full = jnp.broadcast_to(
        mask.astype(jnp.float32)[:, None, :, None], (count, block_rows, 2, supernode)
    )
    return full.reshape(count * block_rows, 2 * supernode)


def local(ainv, lpanel, dinv, lmask, hrows, hmask, pole_weight):
    rows_local = lpanel.shape[0]
    supernode = lpanel.shape[1] // 2
    block_rows = rows_local // lmask.shape[0]
    index = {axis: lax.axis_index(axis) for axis in AXES}
    where = jnp.stack([index[axis] for axis in AXES]).astype(jnp.int32)
    pattern = expand_local(lmask, block_rows, supernode)
    lmasked = lpanel * pattern
    half = rows_local // 2
    (mine,) = fence(to_slabs(lmasked))
    left, right, across = fence(shift(mine, "x", 1), shift(mine, "x", -1), shift(mine, "zh", 1))
    top, bottom = fence(shift(left[:half], "x", 1), shift(right[half:], "x", -1))
    near = near_product(ainv, (mine, right, left, top, bottom), where)
    near, *others = fence(
        near,
        shift(across, "x", -1),
        shift(across, "x", 1),
        shift(top, "zh", 1),
        shift(bottom, "zh", 1),
    )
    others = (across, *others)
    given0, kept0 = fence(*far_product(ainv, near, others, where, 0))
    given1, kept1, came0 = fence(
        *far_product(ainv, near, others, where, 1), shift(given0, "core", 1)
    )
    owned = (reduce_to_owner(kept0, came0), reduce_to_owner(kept1, shift(given1, "core", 1)))
    terms = [
        lax.dot_general(
            lmasked[:, s * supernode : (s + 1) * supernode],
            owned[s],
            (((0,), (0,)), ((), ())),
            precision=lax.Precision.HIGHEST,
            preferred_element_type=jnp.float32,
        )
        for s in range(2)
    ]
    diaginv = dinv + sum_diag(jnp.concatenate(terms, axis=0), index)
    offdiag = -jnp.concatenate(owned, axis=1) * pattern
    hpattern = expand_local(hmask, block_rows, supernode)
    energy = pole_weight[0] * jnp.sum(hrows * hpattern * offdiag, axis=1)
    return (offdiag, diaginv, energy)


def solution(mesh):
    split_mesh = Mesh(mesh.devices.reshape(*SIZES), AXES)
    rows = P(AXES, None)
    return jax.shard_map(
        local,
        mesh=split_mesh,
        in_specs=(P(("zh", "x"), ("zl", "y", "core")), rows, rows, rows, rows, rows, P()),
        out_specs=(rows, rows, P(AXES)),
        check_vma=False,
    )
```

time: 240 us -> 225 us (0.938)
  starting transfers between devices: 109 us -> 75.3 us
  waiting for transfers between devices: 57.7 us -> 70.2 us
  local copies, waits for them, and re-layouts: 3.07 us -> 11.6 us
  other arithmetic: 21.4 us -> 18.6 us
    ppermute x39 -> x29, starting transfers between devices: 107 us -> 69.4 us  [shift(): lax.ppermute(array, axis, [(i, (i + by) % size) for i in range(size)])]
    ppermute x39 -> x29, waiting for transfers between devices: 57.4 us -> 64.7 us  [shift(): lax.ppermute(array, axis, [(i, (i + by) % size) for i in range(size)])]
    unnamed x50 -> x30, local copies, waits for them, and re-layouts: 1.27 us -> 8.21 us
    all_to_all x0 -> x1, waiting for transfers between devices: none -> 5.53 us  [sum_diag(): lax.all_to_all(total, ('zh', 'x', 'zl'), 0, 0, tiled=True)]
    all_to_all x0 -> x1, starting transfers between devices: none -> 5.24 us  [sum_diag(): lax.all_to_all(total, ('zh', 'x', 'zl'), 0, 0, tiled=True)]
    pallas_call x4 -> x3, Pallas kernels: 43.9 us -> 44.3 us  [the longest x2 25.8 us: far_product(): pl.pallas_call(functools.partial(far_kernel, columns), grid_spec=pltpu.Pr...]
  transfers between devices with their start and end apart: 42 -> 31, of which waited for: 21 -> 19; matrix products, arithmetic and copies ran while one was open for 7% -> 6% of each run, Pallas kernels for 18% -> 14%
where the time goes in v2:
time: 225 us; the launch traced here: 224 us
  starting transfers between devices  75.3 us (33%)
  waiting for transfers between devices  70.2 us (31%)
  Pallas kernels  44.3 us (20%)
  other arithmetic  18.6 us (8%)
  local copies, waits for them, and re-layouts  11.6 us (5%)
    ppermute x29, starting transfers between devices, shift(): lax.ppermute(array, axis, [(i, (i + by) % size) for i in range(size)])  69.4 us
    ppermute x29, waiting for transfers between devices, shift(): lax.ppermute(array, axis, [(i, (i + by) % size) for i in range(size)])  64.7 us
    pallas_call x2, Pallas kernels, far_product(): pl.pallas_call(functools.partial(far_kernel, columns), grid_spec=pltpu.Pr...  25.8 us
    pallas_call x1, Pallas kernels, near_product(): pl.pallas_call(near_kernel, grid_spec=pltpu.PrefetchScalarGridSpec(num_sc...  18.5 us
    unnamed x30, local copies, waits for them, and re-layouts  8.21 us
    all_to_all x1, waiting for transfers between devices, sum_diag(): lax.all_to_all(total, ('zh', 'x', 'zl'), 0, 0, tiled=True)  5.53 us
    all_to_all x1, starting transfers between devices, sum_diag(): lax.all_to_all(total, ('zh', 'x', 'zl'), 0, 0, tiled=True)  5.24 us
  transfers between devices with their start and end apart: 31, of which 19 were waited for; matrix products, arithmetic and copies ran while one was open for 6% of the time, Pallas kernels for 14%

profile of v2, /device:TPU:0, one launch (start us, length us, event | category | flops | bytes accessed | tf_op | source)
XLA Modules:
  0.0 223.9 jit_solution(3350127679617430931)
XLA Ops:
  4.1 14.2 %collective-permute-start.1 = (f32[192,1024]{1,0:T(8,128)S(1)}, f32[192,1024]{1,0:T(8,128)S(1)}, u32[]{:S(2)}, u32[]{:S(2)}) collective-permute-start(f32[192,1024]{1,0:T(8,128)S(1)} %collective-permute-done.refs_0_), channel_id=1, source_target_pairs={{0,16},{16,32},{32,48},{48,0},{1,17},{17,33},{33,49},{49,1},{2,18}... | collective-permute-start | bytes 2359304 | tf_op jit(solution)/shard_map/ppermute | solution.py:17
  18.3 11.8 %collective-permute-start.2 = (f32[192,1024]{1,0:T(8,128)S(1)}, f32[192,1024]{1,0:T(8,128)S(1)}, u32[]{:S(2)}, u32[]{:S(2)}) collective-permute-start(f32[192,1024]{1,0:T(8,128)S(1)} %collective-permute-done.refs_0_), channel_id=1, source_target_pairs={{0,48},{16,0},{32,16},{48,32},{1,49},{17,1},{33,17},{49,33},{2,50}... | collective-permute-start | bytes 2359304 | tf_op jit(solution)/shard_map/ppermute | solution.py:17
  30.1 6.6 %collective-permute-start.3 = (f32[192,1024]{1,0:T(8,128)S(1)}, f32[192,1024]{1,0:T(8,128)S(1)}, u32[]{:S(2)}, u32[]{:S(2)}) collective-permute-start(f32[192,1024]{1,0:T(8,128)S(1)} %collective-permute-done.refs_0_), channel_id=1, source_target_pairs={{0,64},{64,0},{1,65},{65,1},{2,66},{66,2},{3,67},{67,3},{4,68},{68... | collective-permute-start | bytes 2359304 | tf_op jit(solution)/shard_map/ppermute | solution.py:17
  36.7 11.2 %collective-permute-done.1.refs_2_ = f32[192,1024]{1,0:T(8,128)S(1)} collective-permute-done((f32[192,1024]{1,0:T(8,128)S(1)}, f32[192,1024]{1,0:T(8,128)S(1)}, u32[]{:S(2)}, u32[]{:S(2)}) %collective-permute-start.1) | collective-permute-done | bytes 786464 | tf_op jit(solution)/shard_map/ppermute | solution.py:17
  47.9 4.1 %collective-permute-done.3.refs_0_ = f32[192,1024]{1,0:T(8,128)S(1)} collective-permute-done((f32[192,1024]{1,0:T(8,128)S(1)}, f32[192,1024]{1,0:T(8,128)S(1)}, u32[]{:S(2)}, u32[]{:S(2)}) %collective-permute-start.3) | collective-permute-done | bytes 786464 | tf_op jit(solution)/shard_map/ppermute | solution.py:17
  53.6 3.2 %collective-permute-start.5 = (f32[96,1024]{1,0:T(8,128)}, f32[96,1024]{1,0:T(8,128)}, u32[]{:S(2)}, u32[]{:S(2)}) collective-permute-start(f32[96,1024]{1,0:T(8,128)} %slice.109), channel_id=1, source_target_pairs={{0,48},{16,0},{32,16},{48,32},{1,49},{17,1},{33,17},{49,33},{2,50}... | collective-permute-start | bytes 1179656 | tf_op jit(solution)/shard_map/ppermute | solution.py:17
  58.9 7.4 %collective-permute-done.4.refs_3_ = f32[96,1024]{1,0:T(8,128)S(1)} collective-permute-done((f32[96,1024]{1,0:T(8,128)}, f32[96,1024]{1,0:T(8,128)S(1)}, u32[]{:S(2)}, u32[]{:S(2)}) %collective-permute-start.4) | collective-permute-done | bytes 393248 | tf_op jit(solution)/shard_map/ppermute | solution.py:17
  66.7 3.2 %collective-permute-start.8 = (f32[96,1024]{1,0:T(8,128)S(1)}, f32[96,1024]{1,0:T(8,128)S(1)}, u32[]{:S(2)}, u32[]{:S(2)}) collective-permute-start(f32[96,1024]{1,0:T(8,128)S(1)} %collective-permute-done.4.refs_3_), channel_id=1, source_target_pairs={{0,64},{64,0},{1,65},{65,1},{2,66},{66,2},{3,67},{67,3},{4,68},{68... | collective-permute-start | bytes 1179656 | tf_op jit(solution)/shard_map/ppermute | solution.py:17
  70.2 18.5 %shard_map.94 = f32[3072,1024]{1,0:T(8,128)S(1)} custom-call(s32[5]{0:T(128)S(1)} %stack.23.where, f32[3072,1536]{1,0:T(8,128)} %a_ref.1, f32[192,1024]{1,0:T(8,128)S(1)} %collective-permute-done.refs_0_, f32[192,1024]{1,0:T(8,128)S(1)} %collective-permute-done.2.refs_1_, f32[192,1024]{1,0:T(8,128)S(1)} %collective-permute-done.1.refs_2_, ...), custom_call_target="tpu_custom_call" | custom-call | flops 14495514624 | bytes 22020096 | tf_op jit(solution)/shard_map/pallas_call | solution.py:69
  88.7 4.5 %copy-done = f32[3072,1024]{1,0:T(8,128)} copy-done((f32[3072,1024]{1,0:T(8,128)}, f32[3072,1024]{1,0:T(8,128)S(1)}, u32[]{:S(2)}) %copy-start) | copy-done | bytes 12582936
  93.3 12.9 %shard_map.95 = (f32[2,4,192,512]{3,2,1,0:T(8,128)S(1)}, f32[2,4,192,512]{3,2,1,0:T(8,128)S(1)}) custom-call(s32[5]{0:T(128)S(1)} %stack.23.where, f32[2,4,2,192,1536]{4,3,2,1,0:T(8,128)} %bitcast.88, f32[2,4,2,192,1024]{4,3,2,1,0:T(8,128)} %bitcast.86, f32[192,1024]{1,0:T(8,128)S(1)} %collective-permute-done.3.refs_0_, ...), custom_call_target="tpu_custom_call" | custom-call | flops 7247757312 | bytes 22020096 | tf_op jit(solution)/shard_map/pallas_call | solution.py:131
  108.0 12.9 %shard_map.96 = (f32[2,4,192,512]{3,2,1,0:T(8,128)S(1)}, f32[2,4,192,512]{3,2,1,0:T(8,128)S(1)}) custom-call(s32[5]{0:T(128)S(1)} %stack.23.where, f32[2,4,2,192,1536]{4,3,2,1,0:T(8,128)} %bitcast.89, f32[2,4,2,192,1024]{4,3,2,1,0:T(8,128)} %bitcast.87, f32[192,1024]{1,0:T(8,128)S(1)} %copy-done.3, f32[192,1024]{1,0:T(8,128)S(1)} %collective-permute-done.6.refs_1_, ...), custom_call_target="tpu_custom_call" | custom-call | flops 7247757312 | bytes 22020096 | tf_op jit(solution)/shard_map/pallas_call | solution.py:131
  121.4 4.0 %collective-permute-start.11 = (f32[192,512]{1,0:T(8,128)S(1)}, f32[192,512]{1,0:T(8,128)S(1)}, u32[]{:S(2)}, u32[]{:S(2)}) collective-permute-start(f32[192,512]{1,0:T(8,128)S(1)} %get-tuple-element.41), channel_id=1, source_target_pairs={{0,2},{2,4},{4,6},{6,0},{1,3},{3,5},{5,7},{7,1},{8,10},{10,12},{12... | collective-permute-start | bytes 1179656 | tf_op jit(solution)/shard_map/ppermute | solution.py:17
  128.2 3.9 %collective-permute-start.19 = (f32[192,512]{1,0:T(8,128)S(1)}, f32[192,512]{1,0:T(8,128)S(1)}, u32[]{:S(2)}, u32[]{:S(2)}) collective-permute-start(f32[192,512]{1,0:T(8,128)S(1)} %get-tuple-element.47), channel_id=1, source_target_pairs={{0,2},{2,4},{4,6},{6,0},{1,3},{3,5},{5,7},{7,1},{8,10},{10,12},{12... | collective-permute-start | bytes 1179656 | tf_op jit(solution)/shard_map/ppermute | solution.py:17
  140.4 3.8 %collective-permute-done.19 = f32[192,512]{1,0:T(8,128)S(1)} collective-permute-done((f32[192,512]{1,0:T(8,128)S(1)}, f32[192,512]{1,0:T(8,128)S(1)}, u32[]{:S(2)}, u32[]{:S(2)}) %collective-permute-start.19) | collective-permute-done | bytes 393248 | tf_op jit(solution)/shard_map/ppermute | solution.py:17
  149.4 3.2 %collective-permute-done.14 = f32[192,512]{1,0:T(8,128)S(1)} collective-permute-done((f32[192,512]{1,0:T(8,128)S(1)}, f32[192,512]{1,0:T(8,128)S(1)}, u32[]{:S(2)}, u32[]{:S(2)}) %collective-permute-start.14) | collective-permute-done | bytes 393248 | tf_op jit(solution)/shard_map/ppermute | solution.py:17
  157.4 3.7 %collective-permute-done.22 = f32[192,512]{1,0:T(8,128)} collective-permute-done((f32[192,512]{1,0:T(8,128)}, f32[192,512]{1,0:T(8,128)}, u32[]{:S(2)}, u32[]{:S(2)}) %collective-permute-start.22) | collective-permute-done | bytes 393248 | tf_op jit(solution)/shard_map/ppermute | solution.py:17
  164.6 6.6 %collective-permute-done.13 = f32[192,512]{1,0:T(8,128)} collective-permute-done((f32[192,512]{1,0:T(8,128)S(1)}, f32[192,512]{1,0:T(8,128)}, u32[]{:S(2)}, u32[]{:S(2)}) %collective-permute-start.13) | collective-permute-done | bytes 393248 | tf_op jit(solution)/shard_map/ppermute | solution.py:17
  175.7 3.1 %collective-permute-done.21 = f32[192,512]{1,0:T(8,128)S(1)} collective-permute-done((f32[192,512]{1,0:T(8,128)}, f32[192,512]{1,0:T(8,128)S(1)}, u32[]{:S(2)}, u32[]{:S(2)}) %collective-permute-start.21) | collective-permute-done | bytes 393248 | tf_op jit(solution)/shard_map/ppermute | solution.py:17
  185.0 2.7 %collective-permute-done.26 = f32[16,4,8,512]{3,2,1,0:T(8,128)} collective-permute-done((f32[16,4,8,512]{3,2,1,0:T(8,128)S(1)}, f32[16,4,8,512]{3,2,1,0:T(8,128)}, u32[]{:S(2)}, u32[]{:S(2)}) %collective-permute-start.26) | collective-permute-done | bytes 1048608 | tf_op jit(solution)/shard_map/ppermute | solution.py:17
  197.6 3.2 %collective-permute-done.27 = f32[16,8,512]{2,1,0:T(8,128)} collective-permute-done((f32[16,8,512]{2,1,0:T(8,128)}, f32[16,8,512]{2,1,0:T(8,128)}, u32[]{:S(2)}, u32[]{:S(2)}) %collective-permute-start.27) | collective-permute-done | bytes 262176 | tf_op jit(solution)/shard_map/ppermute | solution.py:17
  200.8 4.9 %collective-permute-done.28 = f32[16,8,512]{2,1,0:T(8,128)} collective-permute-done((f32[16,8,512]{2,1,0:T(8,128)}, f32[16,8,512]{2,1,0:T(8,128)}, u32[]{:S(2)}, u32[]{:S(2)}) %collective-permute-start.28) | collective-permute-done | bytes 262176 | tf_op jit(solution)/shard_map/ppermute | solution.py:17
  209.5 5.2 %all-to-all-start = ((f32[16,8,512]{2,1,0:T(8,128)}), f32[16,8,512]{2,1,0:T(8,128)S(1)}, u32[]{:S(2)}, u32[]{:S(2)}) async-start(f32[16,8,512]{2,1,0:T(8,128)} %fusion.24), calls=%async_computation | async-start | bytes 524288 | tf_op jit(solution)/shard_map/all_to_all | solution.py:187
  217.7 5.5 %all-to-all-done = f32[16,8,512]{2,1,0:T(8,128)S(1)} async-done(((f32[16,8,512]{2,1,0:T(8,128)}), f32[16,8,512]{2,1,0:T(8,128)S(1)}, u32[]{:S(2)}, u32[]{:S(2)}) %all-to-all-start) | async-done | bytes 262176 | tf_op jit(solution)/shard_map/all_to_all | solution.py:187
  (100 shorter events, 61.6 us)
Async XLA Ops:
  4.1 43.8 %collective-permute-start.1 = (f32[192,1024]{1,0:T(8,128)S(1)}, f32[192,1024]{1,0:T(8,128)S(1)}, u32[]{:S(2)}, u32[]{:S(2)}) collective-permute-start(f32[192,1024]{1,0:T(8,128)S(1)} %collective-permute-done.refs_0_), channel_id=1, source_target_pairs={{0,16},{16,32},{32,48},{48,0},{1,17},{17,33},{33,49},{49,1},{2,18}... | collective-permute-start | bytes 2359304 | tf_op jit(solution)/shard_map/ppermute | solution.py:17
  18.3 29.7 %collective-permute-start.2 = (f32[192,1024]{1,0:T(8,128)S(1)}, f32[192,1024]{1,0:T(8,128)S(1)}, u32[]{:S(2)}, u32[]{:S(2)}) collective-permute-start(f32[192,1024]{1,0:T(8,128)S(1)} %collective-permute-done.refs_0_), channel_id=1, source_target_pairs={{0,48},{16,0},{32,16},{48,32},{1,49},{17,1},{33,17},{49,33},{2,50}... | collective-permute-start | bytes 2359304 | tf_op jit(solution)/shard_map/ppermute | solution.py:17
  30.1 21.9 %collective-permute-start.3 = (f32[192,1024]{1,0:T(8,128)S(1)}, f32[192,1024]{1,0:T(8,128)S(1)}, u32[]{:S(2)}, u32[]{:S(2)}) collective-permute-start(f32[192,1024]{1,0:T(8,128)S(1)} %collective-permute-done.refs_0_), channel_id=1, source_target_pairs={{0,64},{64,0},{1,65},{65,1},{2,66},{66,2},{3,67},{67,3},{4,68},{68... | collective-permute-start | bytes 2359304 | tf_op jit(solution)/shard_map/ppermute | solution.py:17
  52.8 13.5 %collective-permute-start.4 = (f32[96,1024]{1,0:T(8,128)}, f32[96,1024]{1,0:T(8,128)S(1)}, u32[]{:S(2)}, u32[]{:S(2)}) collective-permute-start(f32[96,1024]{1,0:T(8,128)} %slice.108), channel_id=1, source_target_pairs={{0,16},{16,32},{32,48},{48,0},{1,17},{17,33},{33,49},{49,1},{2,18}... | collective-permute-start | bytes 1179656 | tf_op jit(solution)/shard_map/ppermute | solution.py:17
  56.9 36.4 %collective-permute-start.6 = (f32[192,1024]{1,0:T(8,128)S(1)}, f32[192,1024]{1,0:T(8,128)S(1)}, u32[]{:S(2)}, u32[]{:S(2)}) collective-permute-start(f32[192,1024]{1,0:T(8,128)S(1)} %collective-permute-done.3.refs_0_), channel_id=1, source_target_pairs={{0,48},{16,0},{32,16},{48,32},{1,49},{17,1},{33,17},{49,33},{2,50}... | collective-permute-start | bytes 2359304 | tf_op jit(solution)/shard_map/ppermute | solution.py:17
  56.9 36.4 %collective-permute-start.7 = (f32[192,1024]{1,0:T(8,128)S(1)}, f32[192,1024]{1,0:T(8,128)S(1)}, u32[]{:S(2)}, u32[]{:S(2)}) collective-permute-start(f32[192,1024]{1,0:T(8,128)S(1)} %collective-permute-done.3.refs_0_), channel_id=1, source_target_pairs={{0,16},{16,32},{32,48},{48,0},{1,17},{17,33},{33,49},{49,1},{2,18}... | collective-permute-start | bytes 2359304 | tf_op jit(solution)/shard_map/ppermute | solution.py:17
  66.7 26.6 %collective-permute-start.8 = (f32[96,1024]{1,0:T(8,128)S(1)}, f32[96,1024]{1,0:T(8,128)S(1)}, u32[]{:S(2)}, u32[]{:S(2)}) collective-permute-start(f32[96,1024]{1,0:T(8,128)S(1)} %collective-permute-done.4.refs_3_), channel_id=1, source_target_pairs={{0,64},{64,0},{1,65},{65,1},{2,66},{66,2},{3,67},{67,3},{4,68},{68... | collective-permute-start | bytes 1179656 | tf_op jit(solution)/shard_map/ppermute | solution.py:17
  70.0 23.3 %collective-permute-start.9 = (f32[96,1024]{1,0:T(8,128)}, f32[96,1024]{1,0:T(8,128)S(1)}, u32[]{:S(2)}, u32[]{:S(2)}) collective-permute-start(f32[96,1024]{1,0:T(8,128)} %collective-permute-done.5.refs_4_), channel_id=1, source_target_pairs={{0,64},{64,0},{1,65},{65,1},{2,66},{66,2},{3,67},{67,3},{4,68},{68... | collective-permute-start | bytes 1179656 | tf_op jit(solution)/shard_map/ppermute | solution.py:17
  106.2 14.7 %collective-permute-start.10 = (f32[2,4,192,512]{3,2,1,0:T(8,128)S(1)}, f32[2,4,192,512]{3,2,1,0:T(8,128)S(1)}, u32[]{:S(2)}, u32[]{:S(2)}) collective-permute-start(f32[2,4,192,512]{3,2,1,0:T(8,128)S(1)} %get-tuple-element.33), channel_id=1, source_target_pairs={{0,1},{1,0},{2,3},{3,2},{4,5},{5,4},{6,7},{7,6},{8,9},{9,8},{10,11... | collective-permute-start | bytes 9437192 | tf_op jit(solution)/shard_map/ppermute | solution.py:17
  121.4 14.3 %collective-permute-start.11 = (f32[192,512]{1,0:T(8,128)S(1)}, f32[192,512]{1,0:T(8,128)S(1)}, u32[]{:S(2)}, u32[]{:S(2)}) collective-permute-start(f32[192,512]{1,0:T(8,128)S(1)} %get-tuple-element.41), channel_id=1, source_target_pairs={{0,2},{2,4},{4,6},{6,0},{1,3},{3,5},{5,7},{7,1},{8,10},{10,12},{12... | collective-permute-start | bytes 1179656 | tf_op jit(solution)/shard_map/ppermute | solution.py:17
  128.2 16.0 %collective-permute-start.19 = (f32[192,512]{1,0:T(8,128)S(1)}, f32[192,512]{1,0:T(8,128)S(1)}, u32[]{:S(2)}, u32[]{:S(2)}) collective-permute-start(f32[192,512]{1,0:T(8,128)S(1)} %get-tuple-element.47), channel_id=1, source_target_pairs={{0,2},{2,4},{4,6},{6,0},{1,3},{3,5},{5,7},{7,1},{8,10},{10,12},{12... | collective-permute-start | bytes 1179656 | tf_op jit(solution)/shard_map/ppermute | solution.py:17
  132.2 13.7 %collective-permute-start.23 = (f32[192,512]{1,0:T(8,128)S(1)}, f32[192,512]{1,0:T(8,128)S(1)}, u32[]{:S(2)}, u32[]{:S(2)}) collective-permute-start(f32[192,512]{1,0:T(8,128)S(1)} %get-tuple-element.48), channel_id=1, source_target_pairs={{0,6},{2,0},{4,2},{6,4},{1,7},{3,1},{5,3},{7,5},{8,14},{10,8},{12,... | collective-permute-start | bytes 1179656 | tf_op jit(solution)/shard_map/ppermute | solution.py:17
  132.5 20.1 %collective-permute-start.14 = (f32[192,512]{1,0:T(8,128)S(1)}, f32[192,512]{1,0:T(8,128)S(1)}, u32[]{:S(2)}, u32[]{:S(2)}) collective-permute-start(f32[192,512]{1,0:T(8,128)S(1)} %get-tuple-element.43), channel_id=1, source_target_pairs={{0,2},{2,4},{4,6},{6,0},{1,3},{3,5},{5,7},{7,1},{8,10},{10,12},{12... | collective-permute-start | bytes 1179656 | tf_op jit(solution)/shard_map/ppermute | solution.py:17
  138.4 15.9 %collective-permute-start.16 = (f32[192,512]{1,0:T(8,128)S(1)}, f32[192,512]{1,0:T(8,128)S(1)}, u32[]{:S(2)}, u32[]{:S(2)}) collective-permute-start(f32[192,512]{1,0:T(8,128)S(1)} %get-tuple-element.40), channel_id=1, source_target_pairs={{0,6},{2,0},{4,2},{6,4},{1,7},{3,1},{5,3},{7,5},{8,14},{10,8},{12,... | collective-permute-start | bytes 1179656 | tf_op jit(solution)/shard_map/ppermute | solution.py:17
  140.0 21.1 %collective-permute-start.22 = (f32[192,512]{1,0:T(8,128)}, f32[192,512]{1,0:T(8,128)}, u32[]{:S(2)}, u32[]{:S(2)}) collective-permute-start(f32[192,512]{1,0:T(8,128)} %get-tuple-element.49), channel_id=1, source_target_pairs={{0,2},{2,4},{4,6},{6,0},{1,3},{3,5},{5,7},{7,1},{8,10},{10,12},{12... | collective-permute-start | bytes 1179656 | tf_op jit(solution)/shard_map/ppermute | solution.py:17
  147.0 16.1 %collective-permute-start.24 = (f32[192,512]{1,0:T(8,128)}, f32[192,512]{1,0:T(8,128)}, u32[]{:S(2)}, u32[]{:S(2)}) collective-permute-start(f32[192,512]{1,0:T(8,128)} %get-tuple-element.46), channel_id=1, source_target_pairs={{0,6},{2,0},{4,2},{6,4},{1,7},{3,1},{5,3},{7,5},{8,14},{10,8},{12,... | collective-permute-start | bytes 1179656 | tf_op jit(solution)/shard_map/ppermute | solution.py:17
  148.6 22.6 %collective-permute-start.13 = (f32[192,512]{1,0:T(8,128)S(1)}, f32[192,512]{1,0:T(8,128)}, u32[]{:S(2)}, u32[]{:S(2)}) collective-permute-start(f32[192,512]{1,0:T(8,128)S(1)} %get-tuple-element.44), channel_id=1, source_target_pairs={{0,6},{2,0},{4,2},{6,4},{1,7},{3,1},{5,3},{7,5},{8,14},{10,8},{12,... | collective-permute-start | bytes 1179656 | tf_op jit(solution)/shard_map/ppermute | solution.py:17
  152.6 20.2 %collective-permute-start.12 = (f32[192,512]{1,0:T(8,128)}, f32[192,512]{1,0:T(8,128)}, u32[]{:S(2)}, u32[]{:S(2)}) collective-permute-start(f32[192,512]{1,0:T(8,128)} %get-tuple-element.39), channel_id=1, source_target_pairs={{0,2},{2,4},{4,6},{6,0},{1,3},{3,5},{5,7},{7,1},{8,10},{10,12},{12... | collective-permute-start | bytes 1179656 | tf_op jit(solution)/shard_map/ppermute | solution.py:17
  155.2 17.7 %collective-permute-start.17 = (f32[192,512]{1,0:T(8,128)}, f32[192,512]{1,0:T(8,128)}, u32[]{:S(2)}, u32[]{:S(2)}) collective-permute-start(f32[192,512]{1,0:T(8,128)} %fusion.20), channel_id=1, source_target_pairs={{0,8},{8,0},{1,9},{9,1},{2,10},{10,2},{3,11},{11,3},{4,12},{12,4},... | collective-permute-start | bytes 1179656 | tf_op jit(solution)/shard_map/ppermute | solution.py:17
  161.2 17.7 %collective-permute-start.21 = (f32[192,512]{1,0:T(8,128)}, f32[192,512]{1,0:T(8,128)S(1)}, u32[]{:S(2)}, u32[]{:S(2)}) collective-permute-start(f32[192,512]{1,0:T(8,128)} %get-tuple-element.50), channel_id=1, source_target_pairs={{0,6},{2,0},{4,2},{6,4},{1,7},{3,1},{5,3},{7,5},{8,14},{10,8},{12,... | collective-permute-start | bytes 1179656 | tf_op jit(solution)/shard_map/ppermute | solution.py:17
  163.1 15.7 %collective-permute-start.20 = (f32[192,512]{1,0:T(8,128)}, f32[192,512]{1,0:T(8,128)S(1)}, u32[]{:S(2)}, u32[]{:S(2)}) collective-permute-start(f32[192,512]{1,0:T(8,128)} %get-tuple-element.45), channel_id=1, source_target_pairs={{0,2},{2,4},{4,6},{6,0},{1,3},{3,5},{5,7},{7,1},{8,10},{10,12},{12... | collective-permute-start | bytes 1179656 | tf_op jit(solution)/shard_map/ppermute | solution.py:17
  192.0 13.7 %collective-permute-start.28 = (f32[16,8,512]{2,1,0:T(8,128)}, f32[16,8,512]{2,1,0:T(8,128)}, u32[]{:S(2)}, u32[]{:S(2)}) collective-permute-start(f32[16,8,512]{2,1,0:T(8,128)} %get-tuple-element.53), channel_id=1, source_target_pairs={{0,6},{2,0},{4,2},{6,4},{1,7},{3,1},{5,3},{7,5},{8,14},{10,8},{12,... | collective-permute-start | bytes 786440 | tf_op jit(solution)/shard_map/ppermute | solution.py:17
  193.9 13.7 %collective-permute-start.29 = (f32[16,8,512]{2,1,0:T(8,128)}, f32[16,8,512]{2,1,0:T(8,128)}, u32[]{:S(2)}, u32[]{:S(2)}) collective-permute-start(f32[16,8,512]{2,1,0:T(8,128)} %get-tuple-element.52), channel_id=1, source_target_pairs={{0,4},{2,6},{4,0},{6,2},{1,5},{3,7},{5,1},{7,3},{8,12},{10,14},{12... | collective-permute-start | bytes 786440 | tf_op jit(solution)/shard_map/ppermute | solution.py:17
  209.5 13.8 %all-to-all-start = ((f32[16,8,512]{2,1,0:T(8,128)}), f32[16,8,512]{2,1,0:T(8,128)S(1)}, u32[]{:S(2)}, u32[]{:S(2)}) async-start(f32[16,8,512]{2,1,0:T(8,128)} %fusion.24), calls=%async_computation | async-start | bytes 524288 | tf_op jit(solution)/shard_map/all_to_all | solution.py:187
  (21 other events, 409.3 us)

commit v3 on v2

--- a/solution.py
+++ b/solution.py
@@ -76,7 +76,7 @@
             out_specs=pl.BlockSpec((tile, width), lambda i, where: (i, 0)),
             scratch_shapes=[pltpu.VMEM((depth // 2, width), jnp.bfloat16)] * 2,
         ),
-        out_shape=jax.ShapeDtypeStruct((total, width), jnp.float32),
+        out_shape=pltpu.HBM((total, width), jnp.float32),
         compiler_params=pltpu.CompilerParams(vmem_limit_bytes=36 * 1024 * 1024),
         cost_estimate=pl.CostEstimate(
             flops=3 * total * depth * width,
@@ -163,28 +163,32 @@
     return lax.optimization_barrier(arrays)
 
 
-def reduce_to_owner(kept, came):
-    part = lambda dz, by: kept[dz, by] + came[dz, by]
-    up_far = shift(part(0, 2), "y", 1)
-    down_far = shift(part(1, 2), "y", -1)
-    up_second = shift(part(1, 1), "y", 1)
-    down_first = shift(part(0, 3), "y", -1)
-    up_first = shift(part(0, 1) + up_far, "y", 1)
-    down_second = shift(part(1, 3) + down_far, "y", -1)
-    second = part(1, 0) + up_second + down_second
-    across = shift(second, "zl", 1)
-    return part(0, 0) + up_first + down_first + across
+def both_ways(up, down):
+    return shift(up, "y", 1), shift(down, "y", -1)
+
+
+def reduce_y_first(part):
+    up_far, down_far = both_ways(part[0, 2], part[1, 2])
+    up_second, down_first = both_ways(part[1, 1], part[0, 3])
+    up_first, down_second = both_ways(part[0, 1] + up_far, part[1, 3] + down_far)
+    return part[0, 0] + up_first + down_first, part[1, 0] + up_second + down_second
+
+
+def diag_term(panel, rows):
+    return lax.dot_general(
+        panel,
+        rows,
+        (((0,), (0,)), ((), ())),
+        precision=lax.Precision.HIGHEST,
+        preferred_element_type=jnp.float32,
+    )
 
 
 def sum_diag(terms, index):
-    rows, width = terms.shape[0] // 128, terms.shape[1]
-    terms = terms.reshape(16, 4, 2, rows, width)
-    at = lambda array, axis, i: lax.dynamic_index_in_dim(array, i, axis, keepdims=False)
-    terms = at(terms, 2, index["core"]) + shift(at(terms, 2, 1 - index["core"]), "core", 1)
-    total = at(terms, 1, index["y"])
-    for by in (1, 3, 2):
-        total = total + shift(at(terms, 1, (index["y"] + by) % 4), "y", by)
-    return jnp.sum(lax.all_to_all(total, ("zh", "x", "zl"), 0, 0, tiled=True), axis=0)
+    terms = terms.reshape(64, 2, terms.shape[0] // 128, terms.shape[1])
+    at = lambda i: lax.dynamic_index_in_dim(terms, i, 1, keepdims=False)
+    terms = at(index["core"]) + shift(at(1 - index["core"]), "core", 1)
+    return jnp.sum(lax.all_to_all(terms, ("zh", "x", "zl", "y"), 0, 0, tiled=True), axis=0)
 
 
 def expand_local(mask, block_rows, supernode):
@@ -216,21 +220,18 @@
         shift(bottom, "zh", 1),
     )
     others = (across, *others)
-    given0, kept0 = fence(*far_product(ainv, near, others, where, 0))
+    given0, kept0, over = fence(*far_product(ainv, near, others, where, 0), lmasked)
+    over = shift(over, "zl", 1)
     given1, kept1, came0 = fence(
         *far_product(ainv, near, others, where, 1), shift(given0, "core", 1)
     )
-    owned = (reduce_to_owner(kept0, came0), reduce_to_owner(kept1, shift(given1, "core", 1)))
-    terms = [
-        lax.dot_general(
-            lmasked[:, s * supernode : (s + 1) * supernode],
-            owned[s],
-            (((0,), (0,)), ((), ())),
-            precision=lax.Precision.HIGHEST,
-            preferred_element_type=jnp.float32,
-        )
-        for s in range(2)
-    ]
+    panels = jnp.concatenate([lmasked, over])
+    owned, terms = [], []
+    for s, (kept, came) in enumerate(((kept0, came0), (kept1, shift(given1, "core", 1)))):
+        here, there = reduce_y_first(kept + came)
+        owned.append(here + shift(there, "zl", 1))
+        panel = panels[:, s * supernode : (s + 1) * supernode]
+        terms.append(diag_term(panel, jnp.concatenate([here, there])))
     diaginv = dinv + sum_diag(jnp.concatenate(terms, axis=0), index)
     offdiag = -jnp.concatenate(owned, axis=1) * pattern
     hpattern = expand_local(hmask, block_rows, supernode)

time: 225 us -> 220 us (0.978)
  waiting for transfers between devices: 70.2 us -> 61.3 us
  starting transfers between devices: 75.3 us -> 81.4 us
  local copies, waits for them, and re-layouts: 11.6 us -> 6.48 us
  matrix products: 2.19 us -> 6.03 us
    ppermute x29 -> x27, waiting for transfers between devices: 64.7 us -> 46.5 us  [shift(): lax.ppermute(array, axis, [(i, (i + by) % size) for i in range(size)])]
    all_to_all x1, waiting for transfers between devices: 5.53 us -> 14.7 us  [sum_diag(): lax.all_to_all(terms, ('zh', 'x', 'zl', 'y'), 0, 0, tiled=True)]
    unnamed x30 -> x16, local copies, waits for them, and re-layouts: 8.21 us -> 1.09 us
    dot_general x2, matrix products: 2.19 us -> 6.03 us  [diag_term(): lax.dot_general(panel, rows, (((0,), (0,)), ((), ())), precision=lax.Prec...]
    all_to_all x1, starting transfers between devices: 5.24 us -> 8.78 us  [sum_diag(): lax.all_to_all(terms, ('zh', 'x', 'zl', 'y'), 0, 0, tiled=True)]
    add x10 -> x9, other arithmetic: 12.6 us -> 9.79 us  [the longest x2 2.42 us: local(): owned.append(here + shift(there, 'zl', 1))]
    ppermute x29 -> x27, starting transfers between devices: 69.4 us -> 70.8 us  [shift(): lax.ppermute(array, axis, [(i, (i + by) % size) for i in range(size)])]
  transfers between devices with their start and end apart: 31 -> 29, of which waited for: 19 -> 14; matrix products, arithmetic and copies ran while one was open for 6% -> 7% of each run, Pallas kernels for 14% -> 15%
where the time goes in v3:
time: 220 us; the launch traced here: 219 us
  starting transfers between devices  81.4 us (37%)
  waiting for transfers between devices  61.3 us (28%)
  Pallas kernels  45.5 us (21%)
  other arithmetic  16.7 us (8%)
  local copies, waits for them, and re-layouts  6.48 us (3%)
  matrix products  6.03 us (3%)
    ppermute x27, starting transfers between devices, shift(): lax.ppermute(array, axis, [(i, (i + by) % size) for i in range(size)])  70.8 us
    ppermute x27, waiting for transfers between devices, shift(): lax.ppermute(array, axis, [(i, (i + by) % size) for i in range(size)])  46.5 us
    pallas_call x2, Pallas kernels, far_product(): pl.pallas_call(functools.partial(far_kernel, columns), grid_spec=pltpu.Pr...  25.8 us
    pallas_call x1, Pallas kernels, near_product(): pl.pallas_call(near_kernel, grid_spec=pltpu.PrefetchScalarGridSpec(num_sc...  19.7 us
    all_to_all x1, waiting for transfers between devices, sum_diag(): lax.all_to_all(terms, ('zh', 'x', 'zl', 'y'), 0, 0, tiled=True)  14.7 us
    all_to_all x1, starting transfers between devices, sum_diag(): lax.all_to_all(terms, ('zh', 'x', 'zl', 'y'), 0, 0, tiled=True)  8.78 us
    dot_general x2, matrix products, diag_term(): lax.dot_general(panel, rows, (((0,), (0,)), ((), ())), precision=lax.Prec...  6.03 us
  transfers between devices with their start and end apart: 29, of which 14 were waited for; matrix products, arithmetic and copies ran while one was open for 7% of the time, Pallas kernels for 15%

profile of v3, /device:TPU:0, one launch (start us, length us, event | category | flops | bytes accessed | tf_op | source)
XLA Modules:
  0.0 218.9 jit_solution(6122078503275622500)
XLA Ops:
  6.1 13.3 %collective-permute-start.1 = (f32[192,1024]{1,0:T(8,128)S(1)}, f32[192,1024]{1,0:T(8,128)S(1)}, u32[]{:S(2)}, u32[]{:S(2)}) collective-permute-start(f32[192,1024]{1,0:T(8,128)S(1)} %collective-permute-done.refs_0_), channel_id=1, source_target_pairs={{0,16},{16,32},{32,48},{48,0},{1,17},{17,33},{33,49},{49,1},{2,18}... | collective-permute-start | bytes 2359304 | tf_op jit(solution)/shard_map/ppermute | solution.py:17
  19.4 11.8 %collective-permute-start.2 = (f32[192,1024]{1,0:T(8,128)S(1)}, f32[192,1024]{1,0:T(8,128)S(1)}, u32[]{:S(2)}, u32[]{:S(2)}) collective-permute-start(f32[192,1024]{1,0:T(8,128)S(1)} %collective-permute-done.refs_0_), channel_id=1, source_target_pairs={{0,48},{16,0},{32,16},{48,32},{1,49},{17,1},{33,17},{49,33},{2,50}... | collective-permute-start | bytes 2359304 | tf_op jit(solution)/shard_map/ppermute | solution.py:17
  31.2 6.6 %collective-permute-start.3 = (f32[192,1024]{1,0:T(8,128)S(1)}, f32[192,1024]{1,0:T(8,128)S(1)}, u32[]{:S(2)}, u32[]{:S(2)}) collective-permute-start(f32[192,1024]{1,0:T(8,128)S(1)} %collective-permute-done.refs_0_), channel_id=1, source_target_pairs={{0,64},{64,0},{1,65},{65,1},{2,66},{66,2},{3,67},{67,3},{4,68},{68... | collective-permute-start | bytes 2359304 | tf_op jit(solution)/shard_map/ppermute | solution.py:17
  37.8 11.2 %collective-permute-done.1.refs_2_ = f32[192,1024]{1,0:T(8,128)S(1)} collective-permute-done((f32[192,1024]{1,0:T(8,128)S(1)}, f32[192,1024]{1,0:T(8,128)S(1)}, u32[]{:S(2)}, u32[]{:S(2)}) %collective-permute-start.1) | collective-permute-done | bytes 786464 | tf_op jit(solution)/shard_map/ppermute | solution.py:17
  49.0 4.1 %collective-permute-done.3.refs_0_ = f32[192,1024]{1,0:T(8,128)S(1)} collective-permute-done((f32[192,1024]{1,0:T(8,128)S(1)}, f32[192,1024]{1,0:T(8,128)S(1)}, u32[]{:S(2)}, u32[]{:S(2)}) %collective-permute-start.3) | collective-permute-done | bytes 786464 | tf_op jit(solution)/shard_map/ppermute | solution.py:17
  54.7 3.2 %collective-permute-start.5 = (f32[96,1024]{1,0:T(8,128)}, f32[96,1024]{1,0:T(8,128)}, u32[]{:S(2)}, u32[]{:S(2)}) collective-permute-start(f32[96,1024]{1,0:T(8,128)} %slice.61), channel_id=1, source_target_pairs={{0,48},{16,0},{32,16},{48,32},{1,49},{17,1},{33,17},{49,33},{2,50}... | collective-permute-start | bytes 1179656 | tf_op jit(solution)/shard_map/ppermute | solution.py:17
  60.0 7.3 %collective-permute-done.4.refs_3_ = f32[96,1024]{1,0:T(8,128)S(1)} collective-permute-done((f32[96,1024]{1,0:T(8,128)}, f32[96,1024]{1,0:T(8,128)S(1)}, u32[]{:S(2)}, u32[]{:S(2)}) %collective-permute-start.4) | collective-permute-done | bytes 393248 | tf_op jit(solution)/shard_map/ppermute | solution.py:17
  67.8 3.2 %collective-permute-start.8 = (f32[96,1024]{1,0:T(8,128)S(1)}, f32[96,1024]{1,0:T(8,128)S(1)}, u32[]{:S(2)}, u32[]{:S(2)}) collective-permute-start(f32[96,1024]{1,0:T(8,128)S(1)} %collective-permute-done.4.refs_3_), channel_id=1, source_target_pairs={{0,64},{64,0},{1,65},{65,1},{2,66},{66,2},{3,67},{67,3},{4,68},{68... | collective-permute-start | bytes 1179656 | tf_op jit(solution)/shard_map/ppermute | solution.py:17
  71.3 19.7 %shard_map.94 = f32[3072,1024]{1,0:T(8,128)} custom-call(s32[5]{0:T(128)S(1)} %stack.23.where, f32[3072,1536]{1,0:T(8,128)} %a_ref.1, f32[192,1024]{1,0:T(8,128)S(1)} %collective-permute-done.refs_0_, f32[192,1024]{1,0:T(8,128)S(1)} %collective-permute-done.2.refs_1_, f32[192,1024]{1,0:T(8,128)S(1)} %collective-permute-done.1.refs_2_, ...), custom_call_target="tpu_custom_call" | custom-call | flops 14495514624 | bytes 22020096 | tf_op jit(solution)/shard_map/pallas_call | solution.py:69
  91.1 12.9 %shard_map.95 = (f32[2,4,192,512]{3,2,1,0:T(8,128)S(1)}, f32[2,4,192,512]{3,2,1,0:T(8,128)S(1)}) custom-call(s32[5]{0:T(128)S(1)} %stack.23.where, f32[2,4,2,192,1536]{4,3,2,1,0:T(8,128)} %bitcast.78, f32[2,4,2,192,1024]{4,3,2,1,0:T(8,128)} %bitcast.80, f32[192,1024]{1,0:T(8,128)S(1)} %collective-permute-done.3.refs_0_, ...), custom_call_target="tpu_custom_call" | custom-call | flops 7247757312 | bytes 22020096 | tf_op jit(solution)/shard_map/pallas_call | solution.py:131
  104.1 12.9 %shard_map.96 = (f32[2,4,192,512]{3,2,1,0:T(8,128)S(1)}, f32[2,4,192,512]{3,2,1,0:T(8,128)S(1)}) custom-call(s32[5]{0:T(128)S(1)} %stack.23.where, f32[2,4,2,192,1536]{4,3,2,1,0:T(8,128)} %bitcast.79, f32[2,4,2,192,1024]{4,3,2,1,0:T(8,128)} %bitcast.81, f32[192,1024]{1,0:T(8,128)S(1)} %collective-permute-done.3.refs_0_, ...), custom_call_target="tpu_custom_call" | custom-call | flops 7247757312 | bytes 22020096 | tf_op jit(solution)/shard_map/pallas_call | solution.py:131
  119.3 3.9 %collective-permute-start.11 = (f32[192,512]{1,0:T(8,128)S(1)}, f32[192,512]{1,0:T(8,128)S(1)}, u32[]{:S(2)}, u32[]{:S(2)}) collective-permute-start(f32[192,512]{1,0:T(8,128)S(1)} %get-tuple-element.51), channel_id=1, source_target_pairs={{0,2},{2,4},{4,6},{6,0},{1,3},{3,5},{5,7},{7,1},{8,10},{10,12},{12... | collective-permute-start | bytes 1179656 | tf_op jit(solution)/shard_map/ppermute | solution.py:17
  125.6 3.2 %collective-permute-start.19 = (f32[192,512]{1,0:T(8,128)S(1)}, f32[192,512]{1,0:T(8,128)S(1)}, u32[]{:S(2)}, u32[]{:S(2)}) collective-permute-start(f32[192,512]{1,0:T(8,128)S(1)} %get-tuple-element.57), channel_id=1, source_target_pairs={{0,2},{2,4},{4,6},{6,0},{1,3},{3,5},{5,7},{7,1},{8,10},{10,12},{12... | collective-permute-start | bytes 1179656 | tf_op jit(solution)/shard_map/ppermute | solution.py:17
  130.7 2.8 %collective-permute-done.11 = f32[192,512]{1,0:T(8,128)S(1)} collective-permute-done((f32[192,512]{1,0:T(8,128)S(1)}, f32[192,512]{1,0:T(8,128)S(1)}, u32[]{:S(2)}, u32[]{:S(2)}) %collective-permute-start.11) | collective-permute-done | bytes 393248 | tf_op jit(solution)/shard_map/ppermute | solution.py:17
  137.7 3.9 %collective-permute-start.26 = (f32[192,1024]{1,0:T(8,128)}, f32[192,1024]{1,0:T(8,128)}, u32[]{:S(2)}, u32[]{:S(2)}) collective-permute-start(f32[192,1024]{1,0:T(8,128)} %mul.18), channel_id=1, source_target_pairs={{0,8},{8,0},{1,9},{9,1},{2,10},{10,2},{3,11},{11,3},{4,12},{12,4},... | collective-permute-start | bytes 2359304 | tf_op jit(solution)/shard_map/ppermute | solution.py:17
  146.3 4.1 %collective-permute-done.14 = f32[192,512]{1,0:T(8,128)S(1)} collective-permute-done((f32[192,512]{1,0:T(8,128)S(1)}, f32[192,512]{1,0:T(8,128)S(1)}, u32[]{:S(2)}, u32[]{:S(2)}) %collective-permute-start.14) | collective-permute-done | bytes 393248 | tf_op jit(solution)/shard_map/ppermute | solution.py:17
  152.6 6.2 %collective-permute-done.22 = f32[192,512]{1,0:T(8,128)S(1)} collective-permute-done((f32[192,512]{1,0:T(8,128)S(1)}, f32[192,512]{1,0:T(8,128)S(1)}, u32[]{:S(2)}, u32[]{:S(2)}) %collective-permute-start.22) | collective-permute-done | bytes 393248 | tf_op jit(solution)/shard_map/ppermute | solution.py:17
  159.6 3.9 %collective-permute-start.17 = (f32[192,512]{1,0:T(8,128)S(1)}, f32[192,512]{1,0:T(8,128)}, u32[]{:S(2)}, u32[]{:S(2)}) collective-permute-start(f32[192,512]{1,0:T(8,128)S(1)} %fusion.20), channel_id=1, source_target_pairs={{0,8},{8,0},{1,9},{9,1},{2,10},{10,2},{3,11},{11,3},{4,12},{12,4},... | collective-permute-start | bytes 1179656 | tf_op jit(solution)/shard_map/ppermute | solution.py:17
  169.1 3.6 %collective-permute-start.25 = (f32[192,512]{1,0:T(8,128)S(1)}, f32[192,512]{1,0:T(8,128)S(1)}, u32[]{:S(2)}, u32[]{:S(2)}) collective-permute-start(f32[192,512]{1,0:T(8,128)S(1)} %fusion.14), channel_id=1, source_target_pairs={{0,8},{8,0},{1,9},{9,1},{2,10},{10,2},{3,11},{11,3},{4,12},{12,4},... | collective-permute-start | bytes 1179656 | tf_op jit(solution)/shard_map/ppermute | solution.py:17
  174.2 3.1 %fusion.1 = f32[512,512]{1,0:T(8,128)S(1)} fusion(f32[192,1024]{1,0:T(8,128)} %mul.18, f32[192,1024]{1,0:T(8,128)} %collective-permute-done.26, f32[192,512]{1,0:T(8,128)} %copy-done.3, f32[192,512]{1,0:T(8,128)S(1)} %get-tuple-element.46), kind=kOutput, calls=%fused_computation.6 | convolution fusion | flops 1208352768 | bytes 3407872 | tf_op jit(solution)/shard_map/dot_general | solution.py:178
  181.0 3.0 %fusion.3 = f32[512,512]{1,0:T(8,128)S(1)} fusion(f32[192,1024]{1,0:T(8,128)} %collective-permute-done.26, f32[192,1024]{1,0:T(8,128)} %mul.18, f32[192,512]{1,0:T(8,128)S(1)} %fusion.14, f32[192,512]{1,0:T(8,128)S(1)} %get-tuple-element.48), kind=kOutput, calls=%fused_computation.8 | convolution fusion | flops 1208352768 | bytes 3407872 | tf_op jit(solution)/shard_map/dot_general | solution.py:178
  185.2 3.0 %collective-permute-done.27 = f32[64,8,512]{2,1,0:T(8,128)} collective-permute-done((f32[64,8,512]{2,1,0:T(8,128)}, f32[64,8,512]{2,1,0:T(8,128)}, u32[]{:S(2)}, u32[]{:S(2)}) %collective-permute-start.27) | collective-permute-done | bytes 1048608 | tf_op jit(solution)/shard_map/ppermute | solution.py:17
  190.6 8.8 %all-to-all-start = ((f32[64,8,512]{2,1,0:T(8,128)}), f32[64,8,512]{2,1,0:T(8,128)S(1)}, u32[]{:S(2)}, u32[]{:S(2)}) async-start(f32[64,8,512]{2,1,0:T(8,128)} %bitcast_add_fusion), calls=%async_computation | async-start | bytes 2097152 | tf_op jit(solution)/shard_map/all_to_all | solution.py:191
  203.5 14.7 %all-to-all-done = f32[64,8,512]{2,1,0:T(8,128)S(1)} async-done(((f32[64,8,512]{2,1,0:T(8,128)}), f32[64,8,512]{2,1,0:T(8,128)S(1)}, u32[]{:S(2)}, u32[]{:S(2)}) %all-to-all-start) | async-done | bytes 1048608 | tf_op jit(solution)/shard_map/all_to_all | solution.py:191
  (82 shorter events, 47.0 us)
Async XLA Ops:
  6.1 43.0 %collective-permute-start.1 = (f32[192,1024]{1,0:T(8,128)S(1)}, f32[192,1024]{1,0:T(8,128)S(1)}, u32[]{:S(2)}, u32[]{:S(2)}) collective-permute-start(f32[192,1024]{1,0:T(8,128)S(1)} %collective-permute-done.refs_0_), channel_id=1, source_target_pairs={{0,16},{16,32},{32,48},{48,0},{1,17},{17,33},{33,49},{49,1},{2,18}... | collective-permute-start | bytes 2359304 | tf_op jit(solution)/shard_map/ppermute | solution.py:17
  19.4 29.7 %collective-permute-start.2 = (f32[192,1024]{1,0:T(8,128)S(1)}, f32[192,1024]{1,0:T(8,128)S(1)}, u32[]{:S(2)}, u32[]{:S(2)}) collective-permute-start(f32[192,1024]{1,0:T(8,128)S(1)} %collective-permute-done.refs_0_), channel_id=1, source_target_pairs={{0,48},{16,0},{32,16},{48,32},{1,49},{17,1},{33,17},{49,33},{2,50}... | collective-permute-start | bytes 2359304 | tf_op jit(solution)/shard_map/ppermute | solution.py:17
  31.2 21.9 %collective-permute-start.3 = (f32[192,1024]{1,0:T(8,128)S(1)}, f32[192,1024]{1,0:T(8,128)S(1)}, u32[]{:S(2)}, u32[]{:S(2)}) collective-permute-start(f32[192,1024]{1,0:T(8,128)S(1)} %collective-permute-done.refs_0_), channel_id=1, source_target_pairs={{0,64},{64,0},{1,65},{65,1},{2,66},{66,2},{3,67},{67,3},{4,68},{68... | collective-permute-start | bytes 2359304 | tf_op jit(solution)/shard_map/ppermute | solution.py:17
  53.9 13.5 %collective-permute-start.4 = (f32[96,1024]{1,0:T(8,128)}, f32[96,1024]{1,0:T(8,128)S(1)}, u32[]{:S(2)}, u32[]{:S(2)}) collective-permute-start(f32[96,1024]{1,0:T(8,128)} %slice.60), channel_id=1, source_target_pairs={{0,16},{16,32},{32,48},{48,0},{1,17},{17,33},{33,49},{49,1},{2,18}... | collective-permute-start | bytes 1179656 | tf_op jit(solution)/shard_map/ppermute | solution.py:17
  54.7 13.1 %collective-permute-start.5 = (f32[96,1024]{1,0:T(8,128)}, f32[96,1024]{1,0:T(8,128)}, u32[]{:S(2)}, u32[]{:S(2)}) collective-permute-start(f32[96,1024]{1,0:T(8,128)} %slice.61), channel_id=1, source_target_pairs={{0,48},{16,0},{32,16},{48,32},{1,49},{17,1},{33,17},{49,33},{2,50}... | collective-permute-start | bytes 1179656 | tf_op jit(solution)/shard_map/ppermute | solution.py:17
  58.0 33.1 %collective-permute-start.6 = (f32[192,1024]{1,0:T(8,128)S(1)}, f32[192,1024]{1,0:T(8,128)S(1)}, u32[]{:S(2)}, u32[]{:S(2)}) collective-permute-start(f32[192,1024]{1,0:T(8,128)S(1)} %collective-permute-done.3.refs_0_), channel_id=1, source_target_pairs={{0,48},{16,0},{32,16},{48,32},{1,49},{17,1},{33,17},{49,33},{2,50}... | collective-permute-start | bytes 2359304 | tf_op jit(solution)/shard_map/ppermute | solution.py:17
  58.0 33.1 %collective-permute-start.7 = (f32[192,1024]{1,0:T(8,128)S(1)}, f32[192,1024]{1,0:T(8,128)S(1)}, u32[]{:S(2)}, u32[]{:S(2)}) collective-permute-start(f32[192,1024]{1,0:T(8,128)S(1)} %collective-permute-done.3.refs_0_), channel_id=1, source_target_pairs={{0,16},{16,32},{32,48},{48,0},{1,17},{17,33},{33,49},{49,1},{2,18}... | collective-permute-start | bytes 2359304 | tf_op jit(solution)/shard_map/ppermute | solution.py:17
  67.8 23.3 %collective-permute-start.8 = (f32[96,1024]{1,0:T(8,128)S(1)}, f32[96,1024]{1,0:T(8,128)S(1)}, u32[]{:S(2)}, u32[]{:S(2)}) collective-permute-start(f32[96,1024]{1,0:T(8,128)S(1)} %collective-permute-done.4.refs_3_), channel_id=1, source_target_pairs={{0,64},{64,0},{1,65},{65,1},{2,66},{66,2},{3,67},{67,3},{4,68},{68... | collective-permute-start | bytes 1179656 | tf_op jit(solution)/shard_map/ppermute | solution.py:17
  71.0 20.0 %collective-permute-start.9 = (f32[96,1024]{1,0:T(8,128)}, f32[96,1024]{1,0:T(8,128)S(1)}, u32[]{:S(2)}, u32[]{:S(2)}) collective-permute-start(f32[96,1024]{1,0:T(8,128)} %collective-permute-done.5.refs_4_), channel_id=1, source_target_pairs={{0,64},{64,0},{1,65},{65,1},{2,66},{66,2},{3,67},{67,3},{4,68},{68... | collective-permute-start | bytes 1179656 | tf_op jit(solution)/shard_map/ppermute | solution.py:17
  104.0 13.0 %collective-permute-start.10 = (f32[2,4,192,512]{3,2,1,0:T(8,128)S(1)}, f32[2,4,192,512]{3,2,1,0:T(8,128)S(1)}, u32[]{:S(2)}, u32[]{:S(2)}) collective-permute-start(f32[2,4,192,512]{3,2,1,0:T(8,128)S(1)} %get-tuple-element.38), channel_id=1, source_target_pairs={{0,1},{1,0},{2,3},{3,2},{4,5},{5,4},{6,7},{7,6},{8,9},{9,8},{10,11... | collective-permute-start | bytes 9437192 | tf_op jit(solution)/shard_map/ppermute | solution.py:17
  119.3 14.2 %collective-permute-start.11 = (f32[192,512]{1,0:T(8,128)S(1)}, f32[192,512]{1,0:T(8,128)S(1)}, u32[]{:S(2)}, u32[]{:S(2)}) collective-permute-start(f32[192,512]{1,0:T(8,128)S(1)} %get-tuple-element.51), channel_id=1, source_target_pairs={{0,2},{2,4},{4,6},{6,0},{1,3},{3,5},{5,7},{7,1},{8,10},{10,12},{12... | collective-permute-start | bytes 1179656 | tf_op jit(solution)/shard_map/ppermute | solution.py:17
  123.3 12.0 %collective-permute-start.15 = (f32[192,512]{1,0:T(8,128)S(1)}, f32[192,512]{1,0:T(8,128)S(1)}, u32[]{:S(2)}, u32[]{:S(2)}) collective-permute-start(f32[192,512]{1,0:T(8,128)S(1)} %get-tuple-element.52), channel_id=1, source_target_pairs={{0,6},{2,0},{4,2},{6,4},{1,7},{3,1},{5,3},{7,5},{8,14},{10,8},{12,... | collective-permute-start | bytes 1179656 | tf_op jit(solution)/shard_map/ppermute | solution.py:17
  125.6 16.4 %collective-permute-start.19 = (f32[192,512]{1,0:T(8,128)S(1)}, f32[192,512]{1,0:T(8,128)S(1)}, u32[]{:S(2)}, u32[]{:S(2)}) collective-permute-start(f32[192,512]{1,0:T(8,128)S(1)} %get-tuple-element.57), channel_id=1, source_target_pairs={{0,2},{2,4},{4,6},{6,0},{1,3},{3,5},{5,7},{7,1},{8,10},{10,12},{12... | collective-permute-start | bytes 1179656 | tf_op jit(solution)/shard_map/ppermute | solution.py:17
  128.7 15.0 %collective-permute-start.23 = (f32[192,512]{1,0:T(8,128)S(1)}, f32[192,512]{1,0:T(8,128)S(1)}, u32[]{:S(2)}, u32[]{:S(2)}) collective-permute-start(f32[192,512]{1,0:T(8,128)S(1)} %get-tuple-element.58), channel_id=1, source_target_pairs={{0,6},{2,0},{4,2},{6,4},{1,7},{3,1},{5,3},{7,5},{8,14},{10,8},{12,... | collective-permute-start | bytes 1179656 | tf_op jit(solution)/shard_map/ppermute | solution.py:17
  129.1 21.3 %collective-permute-start.14 = (f32[192,512]{1,0:T(8,128)S(1)}, f32[192,512]{1,0:T(8,128)S(1)}, u32[]{:S(2)}, u32[]{:S(2)}) collective-permute-start(f32[192,512]{1,0:T(8,128)S(1)} %get-tuple-element.53), channel_id=1, source_target_pairs={{0,2},{2,4},{4,6},{6,0},{1,3},{3,5},{5,7},{7,1},{8,10},{10,12},{12... | collective-permute-start | bytes 1179656 | tf_op jit(solution)/shard_map/ppermute | solution.py:17
  136.2 16.3 %collective-permute-start.16 = (f32[192,512]{1,0:T(8,128)S(1)}, f32[192,512]{1,0:T(8,128)S(1)}, u32[]{:S(2)}, u32[]{:S(2)}) collective-permute-start(f32[192,512]{1,0:T(8,128)S(1)} %get-tuple-element.50), channel_id=1, source_target_pairs={{0,6},{2,0},{4,2},{6,4},{1,7},{3,1},{5,3},{7,5},{8,14},{10,8},{12,... | collective-permute-start | bytes 1179656 | tf_op jit(solution)/shard_map/ppermute | solution.py:17
  137.7 36.5 %collective-permute-start.26 = (f32[192,1024]{1,0:T(8,128)}, f32[192,1024]{1,0:T(8,128)}, u32[]{:S(2)}, u32[]{:S(2)}) collective-permute-start(f32[192,1024]{1,0:T(8,128)} %mul.18), channel_id=1, source_target_pairs={{0,8},{8,0},{1,9},{9,1},{2,10},{10,2},{3,11},{11,3},{4,12},{12,4},... | collective-permute-start | bytes 2359304 | tf_op jit(solution)/shard_map/ppermute | solution.py:17
  142.0 16.9 %collective-permute-start.22 = (f32[192,512]{1,0:T(8,128)S(1)}, f32[192,512]{1,0:T(8,128)S(1)}, u32[]{:S(2)}, u32[]{:S(2)}) collective-permute-start(f32[192,512]{1,0:T(8,128)S(1)} %get-tuple-element.59), channel_id=1, source_target_pairs={{0,2},{2,4},{4,6},{6,0},{1,3},{3,5},{5,7},{7,1},{8,10},{10,12},{12... | collective-permute-start | bytes 1179656 | tf_op jit(solution)/shard_map/ppermute | solution.py:17
  144.8 18.7 %collective-permute-start.24 = (f32[192,512]{1,0:T(8,128)}, f32[192,512]{1,0:T(8,128)}, u32[]{:S(2)}, u32[]{:S(2)}) collective-permute-start(f32[192,512]{1,0:T(8,128)} %get-tuple-element.56), channel_id=1, source_target_pairs={{0,6},{2,0},{4,2},{6,4},{1,7},{3,1},{5,3},{7,5},{8,14},{10,8},{12,... | collective-permute-start | bytes 1179656 | tf_op jit(solution)/shard_map/ppermute | solution.py:17
  150.4 18.7 %collective-permute-start.13 = (f32[192,512]{1,0:T(8,128)}, f32[192,512]{1,0:T(8,128)}, u32[]{:S(2)}, u32[]{:S(2)}) collective-permute-start(f32[192,512]{1,0:T(8,128)} %get-tuple-element.54), channel_id=1, source_target_pairs={{0,6},{2,0},{4,2},{6,4},{1,7},{3,1},{5,3},{7,5},{8,14},{10,8},{12,... | collective-permute-start | bytes 1179656 | tf_op jit(solution)/shard_map/ppermute | solution.py:17
  152.5 16.6 %collective-permute-start.12 = (f32[192,512]{1,0:T(8,128)}, f32[192,512]{1,0:T(8,128)}, u32[]{:S(2)}, u32[]{:S(2)}) collective-permute-start(f32[192,512]{1,0:T(8,128)} %get-tuple-element.49), channel_id=1, source_target_pairs={{0,2},{2,4},{4,6},{6,0},{1,3},{3,5},{5,7},{7,1},{8,10},{10,12},{12... | collective-permute-start | bytes 1179656 | tf_op jit(solution)/shard_map/ppermute | solution.py:17
  159.6 13.1 %collective-permute-start.17 = (f32[192,512]{1,0:T(8,128)S(1)}, f32[192,512]{1,0:T(8,128)}, u32[]{:S(2)}, u32[]{:S(2)}) collective-permute-start(f32[192,512]{1,0:T(8,128)S(1)} %fusion.20), channel_id=1, source_target_pairs={{0,8},{8,0},{1,9},{9,1},{2,10},{10,2},{3,11},{11,3},{4,12},{12,4},... | collective-permute-start | bytes 1179656 | tf_op jit(solution)/shard_map/ppermute | solution.py:17
  163.5 13.8 %collective-permute-start.21 = (f32[192,512]{1,0:T(8,128)}, f32[192,512]{1,0:T(8,128)S(1)}, u32[]{:S(2)}, u32[]{:S(2)}) collective-permute-start(f32[192,512]{1,0:T(8,128)} %get-tuple-element.60), channel_id=1, source_target_pairs={{0,6},{2,0},{4,2},{6,4},{1,7},{3,1},{5,3},{7,5},{8,14},{10,8},{12,... | collective-permute-start | bytes 1179656 | tf_op jit(solution)/shard_map/ppermute | solution.py:17
  190.6 27.6 %all-to-all-start = ((f32[64,8,512]{2,1,0:T(8,128)}), f32[64,8,512]{2,1,0:T(8,128)S(1)}, u32[]{:S(2)}, u32[]{:S(2)}) async-start(f32[64,8,512]{2,1,0:T(8,128)} %bitcast_add_fusion), calls=%async_computation | async-start | bytes 2097152 | tf_op jit(solution)/shard_map/all_to_all | solution.py:191
  (12 other events, 186.9 us)

commit v4 on v3

--- a/solution.py
+++ b/solution.py
@@ -38,12 +38,14 @@
 
 
 def load_pieces(where, pieces, columns, high_ref, low_ref):
-    rows = pieces[0].shape[0]
-    start = lambda by: lax.rem(where[1] + by - where[3] + 4, 4) * rows
-    places = (start(0), start(1), start(3), start(2), start(2) + rows // 2)
-    for piece, place in zip(pieces, places):
+    rows = high_ref.shape[0] // 4
+    done = 0
+    for piece in pieces:
+        by, part = (0, 1, 3, 2)[done // rows], done % rows
+        place = lax.rem(where[1] + by - where[3] + 4, 4) * rows + part
         at = pl.ds(pl.multiple_of(place, 32), piece.shape[0])
         high_ref[at, :], low_ref[at, :] = split(piece[:, columns])
+        done += piece.shape[0]
 
 
 def three_products(a, high_ref, low_ref):
@@ -53,7 +55,7 @@
 
 
 def near_kernel(where, a_ref, *refs):
-    pieces, out_ref, high_ref, low_ref = refs[:5], *refs[5:]
+    pieces, out_ref, high_ref, low_ref = refs[:-3], *refs[-3:]
 
     @pl.when(pl.program_id(0) == 0)
     def _():
@@ -64,15 +66,15 @@
 
 def near_product(ainv, pieces, where):
     total, depth = ainv.shape
-    rows, width = pieces[0].shape
-    tile = 2 * rows
+    width = pieces[0].shape[1]
+    tile = total // 8
     return pl.pallas_call(
         near_kernel,
         grid_spec=pltpu.PrefetchScalarGridSpec(
             num_scalar_prefetch=1,
             grid=(total // tile,),
             in_specs=[pl.BlockSpec((tile, depth // 2), lambda i, where: (i, where[0]))]
-            + [pl.BlockSpec(memory_space=pltpu.VMEM)] * 5,
+            + [pl.BlockSpec(memory_space=pltpu.VMEM)] * len(pieces),
             out_specs=pl.BlockSpec((tile, width), lambda i, where: (i, 0)),
             scratch_shapes=[pltpu.VMEM((depth // 2, width), jnp.bfloat16)] * 2,
         ),
@@ -208,10 +210,17 @@
     pattern = expand_local(lmask, block_rows, supernode)
     lmasked = lpanel * pattern
     half = rows_local // 2
-    (mine,) = fence(to_slabs(lmasked))
-    left, right, across = fence(shift(mine, "x", 1), shift(mine, "x", -1), shift(mine, "zh", 1))
-    top, bottom = fence(shift(left[:half], "x", 1), shift(right[half:], "x", -1))
-    near = near_product(ainv, (mine, right, left, top, bottom), where)
+    mine_top, mine_low = to_slabs(lmasked[:half]), to_slabs(lmasked[half:])
+    (mine_top,) = fence(mine_top)
+    left_top, right_top, mine_low = fence(
+        shift(mine_top, "x", 1), shift(mine_top, "x", -1), mine_low
+    )
+    left_low, right_low = shift(mine_low, "x", 1), shift(mine_low, "x", -1)
+    across = shift(jnp.concatenate([mine_top, mine_low]), "zh", 1)
+    left_low, right_low = fence(left_low, right_low)
+    top, bottom, across = fence(shift(left_top, "x", 1), shift(right_low, "x", -1), across)
+    own = (mine_top, mine_low, right_top, right_low, left_top, left_low, top, bottom)
+    near = near_product(ainv, own, where)
     near, *others = fence(
         near,
         shift(across, "x", -1),

time: 220 us -> 215 us (0.977)
  starting transfers between devices: 81.4 us -> 69.2 us
  waiting for transfers between devices: 61.3 us -> 67.8 us
    ppermute x27 -> x29, starting transfers between devices: 70.8 us -> 61.2 us  [shift(): lax.ppermute(array, axis, [(i, (i + by) % size) for i in range(size)])]
    ppermute x27 -> x29, waiting for transfers between devices: 46.5 us -> 53 us  [shift(): lax.ppermute(array, axis, [(i, (i + by) % size) for i in range(size)])]
  transfers between devices with their start and end apart: 29 -> 32, of which waited for: 14 -> 16; matrix products, arithmetic and copies ran while one was open for 7% -> 7% of each run, Pallas kernels for 15% -> 15%
where the time goes in v4:
time: 215 us; the launch traced here: 214 us
  starting transfers between devices  69.2 us (32%)
  waiting for transfers between devices  67.8 us (32%)
  Pallas kernels  45.6 us (21%)
  other arithmetic  17.6 us (8%)
  local copies, waits for them, and re-layouts  6.09 us (3%)
  matrix products  6.03 us (3%)
    ppermute x29, starting transfers between devices, shift(): lax.ppermute(array, axis, [(i, (i + by) % size) for i in range(size)])  61.2 us
    ppermute x29, waiting for transfers between devices, shift(): lax.ppermute(array, axis, [(i, (i + by) % size) for i in range(size)])  53 us
    pallas_call x2, Pallas kernels, far_product(): pl.pallas_call(functools.partial(far_kernel, columns), grid_spec=pltpu.Pr...  25.8 us
    pallas_call x1, Pallas kernels, near_product(): pl.pallas_call(near_kernel, grid_spec=pltpu.PrefetchScalarGridSpec(num_sc...  19.8 us
    all_to_all x1, waiting for transfers between devices, sum_diag(): lax.all_to_all(terms, ('zh', 'x', 'zl', 'y'), 0, 0, tiled=True)  14.7 us
    all_to_all x1, starting transfers between devices, sum_diag(): lax.all_to_all(terms, ('zh', 'x', 'zl', 'y'), 0, 0, tiled=True)  6.66 us
    dot_general x2, matrix products, diag_term(): lax.dot_general(panel, rows, (((0,), (0,)), ((), ())), precision=lax.Prec...  6.03 us
  transfers between devices with their start and end apart: 32, of which 16 were waited for; matrix products, arithmetic and copies ran while one was open for 7% of the time, Pallas kernels for 15%

profile of v4, /device:TPU:0, one launch (start us, length us, event | category | flops | bytes accessed | tf_op | source)
XLA Modules:
  0.0 213.9 jit_solution(14078110031769461492)
XLA Ops:
  6.8 9.3 %collective-permute-start.1 = (f32[96,1024]{1,0:T(8,128)S(1)}, f32[96,1024]{1,0:T(8,128)S(1)}, u32[]{:S(2)}, u32[]{:S(2)}) collective-permute-start(f32[96,1024]{1,0:T(8,128)S(1)} %collective-permute-done.refs_0_), channel_id=1, source_target_pairs={{0,16},{16,32},{32,48},{48,0},{1,17},{17,33},{33,49},{49,1},{2,18}... | collective-permute-start | bytes 1179656 | tf_op jit(solution)/shard_map/ppermute | solution.py:17
  16.1 6.5 %collective-permute-start.2 = (f32[96,1024]{1,0:T(8,128)S(1)}, f32[96,1024]{1,0:T(8,128)S(1)}, u32[]{:S(2)}, u32[]{:S(2)}) collective-permute-start(f32[96,1024]{1,0:T(8,128)S(1)} %collective-permute-done.refs_0_), channel_id=1, source_target_pairs={{0,48},{16,0},{32,16},{48,32},{1,49},{17,1},{33,17},{49,33},{2,50}... | collective-permute-start | bytes 1179656 | tf_op jit(solution)/shard_map/ppermute | solution.py:17
  22.7 10.0 %collective-permute-done.1.refs_4_ = f32[96,1024]{1,0:T(8,128)S(1)} collective-permute-done((f32[96,1024]{1,0:T(8,128)S(1)}, f32[96,1024]{1,0:T(8,128)S(1)}, u32[]{:S(2)}, u32[]{:S(2)}) %collective-permute-start.1) | collective-permute-done | bytes 393248 | tf_op jit(solution)/shard_map/ppermute | solution.py:17
  37.5 4.7 %collective-permute-start.8 = (f32[192,1024]{1,0:T(8,128)}, f32[192,1024]{1,0:T(8,128)S(1)}, u32[]{:S(2)}, u32[]{:S(2)}) collective-permute-start(f32[192,1024]{1,0:T(8,128)} %pad_maximum_fusion.3), channel_id=1, source_target_pairs={{0,64},{64,0},{1,65},{65,1},{2,66},{66,2},{3,67},{67,3},{4,68},{68... | collective-permute-start | bytes 2359304 | tf_op jit(solution)/shard_map/ppermute | solution.py:17
  46.2 3.4 %collective-permute-start.7 = (f32[96,1024]{1,0:T(8,128)S(1)}, f32[96,1024]{1,0:T(8,128)}, u32[]{:S(2)}, u32[]{:S(2)}) collective-permute-start(f32[96,1024]{1,0:T(8,128)S(1)} %collective-permute-done.5.refs_3_), channel_id=1, source_target_pairs={{0,48},{16,0},{32,16},{48,32},{1,49},{17,1},{33,17},{49,33},{2,50}... | collective-permute-start | bytes 1179656 | tf_op jit(solution)/shard_map/ppermute | solution.py:17
  49.7 5.2 %collective-permute-done.6.refs_6_ = f32[96,1024]{1,0:T(8,128)S(1)} collective-permute-done((f32[96,1024]{1,0:T(8,128)S(1)}, f32[96,1024]{1,0:T(8,128)S(1)}, u32[]{:S(2)}, u32[]{:S(2)}) %collective-permute-start.6) | collective-permute-done | bytes 393248 | tf_op jit(solution)/shard_map/ppermute | solution.py:17
  54.9 3.4 %collective-permute-done.7.refs_7_ = f32[96,1024]{1,0:T(8,128)} collective-permute-done((f32[96,1024]{1,0:T(8,128)S(1)}, f32[96,1024]{1,0:T(8,128)}, u32[]{:S(2)}, u32[]{:S(2)}) %collective-permute-start.7) | collective-permute-done | bytes 393248 | tf_op jit(solution)/shard_map/ppermute | solution.py:17
  59.3 3.2 %collective-permute-start.9 = (f32[192,1024]{1,0:T(8,128)S(1)}, f32[192,1024]{1,0:T(8,128)S(1)}, u32[]{:S(2)}, u32[]{:S(2)}) collective-permute-start(f32[192,1024]{1,0:T(8,128)S(1)} %collective-permute-done.8.refs_0_), channel_id=1, source_target_pairs={{0,48},{16,0},{32,16},{48,32},{1,49},{17,1},{33,17},{49,33},{2,50}... | collective-permute-start | bytes 2359304 | tf_op jit(solution)/shard_map/ppermute | solution.py:17
  66.0 19.8 %shard_map.94 = f32[3072,1024]{1,0:T(8,128)} custom-call(s32[5]{0:T(128)S(1)} %stack.23.where, f32[3072,1536]{1,0:T(8,128)} %a_ref.1, f32[96,1024]{1,0:T(8,128)S(1)} %collective-permute-done.refs_0_, f32[96,1024]{1,0:T(8,128)S(1)} %collective-permute-done.3.refs_1_, f32[96,1024]{1,0:T(8,128)S(1)} %collective-permute-done.2.refs_2_, ...), custom_call_target="tpu_custom_call" | custom-call | flops 14495514624 | bytes 22020096 | tf_op jit(solution)/shard_map/pallas_call | solution.py:71
  85.8 12.9 %shard_map.95 = (f32[2,4,192,512]{3,2,1,0:T(8,128)S(1)}, f32[2,4,192,512]{3,2,1,0:T(8,128)S(1)}) custom-call(s32[5]{0:T(128)S(1)} %stack.23.where, f32[2,4,2,192,1536]{4,3,2,1,0:T(8,128)} %bitcast.78, f32[2,4,2,192,1024]{4,3,2,1,0:T(8,128)} %bitcast.80, f32[192,1024]{1,0:T(8,128)S(1)} %collective-permute-done.8.refs_0_, ...), custom_call_target="tpu_custom_call" | custom-call | flops 7247757312 | bytes 22020096 | tf_op jit(solution)/shard_map/pallas_call | solution.py:133
  98.8 12.9 %shard_map.96 = (f32[2,4,192,512]{3,2,1,0:T(8,128)S(1)}, f32[2,4,192,512]{3,2,1,0:T(8,128)S(1)}) custom-call(s32[5]{0:T(128)S(1)} %stack.23.where, f32[2,4,2,192,1536]{4,3,2,1,0:T(8,128)} %bitcast.79, f32[2,4,2,192,1024]{4,3,2,1,0:T(8,128)} %bitcast.81, f32[192,1024]{1,0:T(8,128)S(1)} %collective-permute-done.8.refs_0_, ...), custom_call_target="tpu_custom_call" | custom-call | flops 7247757312 | bytes 22020096 | tf_op jit(solution)/shard_map/pallas_call | solution.py:133
  114.1 3.5 %collective-permute-start.14 = (f32[192,512]{1,0:T(8,128)S(1)}, f32[192,512]{1,0:T(8,128)S(1)}, u32[]{:S(2)}, u32[]{:S(2)}) collective-permute-start(f32[192,512]{1,0:T(8,128)S(1)} %get-tuple-element.57), channel_id=1, source_target_pairs={{0,2},{2,4},{4,6},{6,0},{1,3},{3,5},{5,7},{7,1},{8,10},{10,12},{12... | collective-permute-start | bytes 1179656 | tf_op jit(solution)/shard_map/ppermute | solution.py:17
  117.6 4.7 %collective-permute-start.18 = (f32[192,512]{1,0:T(8,128)S(1)}, f32[192,512]{1,0:T(8,128)S(1)}, u32[]{:S(2)}, u32[]{:S(2)}) collective-permute-start(f32[192,512]{1,0:T(8,128)S(1)} %get-tuple-element.58), channel_id=1, source_target_pairs={{0,6},{2,0},{4,2},{6,4},{1,7},{3,1},{5,3},{7,5},{8,14},{10,8},{12,... | collective-permute-start | bytes 1179656 | tf_op jit(solution)/shard_map/ppermute | solution.py:17
  124.3 3.5 %collective-permute-start.26 = (f32[192,512]{1,0:T(8,128)S(1)}, f32[192,512]{1,0:T(8,128)S(1)}, u32[]{:S(2)}, u32[]{:S(2)}) collective-permute-start(f32[192,512]{1,0:T(8,128)S(1)} %get-tuple-element.64), channel_id=1, source_target_pairs={{0,6},{2,0},{4,2},{6,4},{1,7},{3,1},{5,3},{7,5},{8,14},{10,8},{12,... | collective-permute-start | bytes 1179656 | tf_op jit(solution)/shard_map/ppermute | solution.py:17
  127.8 4.5 %collective-permute-done.14 = f32[192,512]{1,0:T(8,128)S(1)} collective-permute-done((f32[192,512]{1,0:T(8,128)S(1)}, f32[192,512]{1,0:T(8,128)S(1)}, u32[]{:S(2)}, u32[]{:S(2)}) %collective-permute-start.14) | collective-permute-done | bytes 393248 | tf_op jit(solution)/shard_map/ppermute | solution.py:17
  133.2 3.3 %collective-permute-start.19 = (f32[192,512]{1,0:T(8,128)S(1)}, f32[192,512]{1,0:T(8,128)S(1)}, u32[]{:S(2)}, u32[]{:S(2)}) collective-permute-start(f32[192,512]{1,0:T(8,128)S(1)} %get-tuple-element.56), channel_id=1, source_target_pairs={{0,6},{2,0},{4,2},{6,4},{1,7},{3,1},{5,3},{7,5},{8,14},{10,8},{12,... | collective-permute-start | bytes 1179656 | tf_op jit(solution)/shard_map/ppermute | solution.py:17
  136.9 3.8 %collective-permute-done.22 = f32[192,512]{1,0:T(8,128)S(1)} collective-permute-done((f32[192,512]{1,0:T(8,128)S(1)}, f32[192,512]{1,0:T(8,128)S(1)}, u32[]{:S(2)}, u32[]{:S(2)}) %collective-permute-start.22) | collective-permute-done | bytes 393248 | tf_op jit(solution)/shard_map/ppermute | solution.py:17
  141.7 3.3 %collective-permute-start.27 = (f32[192,512]{1,0:T(8,128)}, f32[192,512]{1,0:T(8,128)}, u32[]{:S(2)}, u32[]{:S(2)}) collective-permute-start(f32[192,512]{1,0:T(8,128)} %get-tuple-element.62), channel_id=1, source_target_pairs={{0,6},{2,0},{4,2},{6,4},{1,7},{3,1},{5,3},{7,5},{8,14},{10,8},{12,... | collective-permute-start | bytes 1179656 | tf_op jit(solution)/shard_map/ppermute | solution.py:17
  145.0 4.1 %collective-permute-done.17 = f32[192,512]{1,0:T(8,128)S(1)} collective-permute-done((f32[192,512]{1,0:T(8,128)S(1)}, f32[192,512]{1,0:T(8,128)S(1)}, u32[]{:S(2)}, u32[]{:S(2)}) %collective-permute-start.17) | collective-permute-done | bytes 393248 | tf_op jit(solution)/shard_map/ppermute | solution.py:17
  151.3 6.2 %collective-permute-done.25 = f32[192,512]{1,0:T(8,128)S(1)} collective-permute-done((f32[192,512]{1,0:T(8,128)S(1)}, f32[192,512]{1,0:T(8,128)S(1)}, u32[]{:S(2)}, u32[]{:S(2)}) %collective-permute-start.25) | collective-permute-done | bytes 393248 | tf_op jit(solution)/shard_map/ppermute | solution.py:17
  162.2 3.5 %collective-permute-done.16 = f32[192,512]{1,0:T(8,128)} collective-permute-done((f32[192,512]{1,0:T(8,128)}, f32[192,512]{1,0:T(8,128)}, u32[]{:S(2)}, u32[]{:S(2)}) %collective-permute-start.16) | collective-permute-done | bytes 393248 | tf_op jit(solution)/shard_map/ppermute | solution.py:17
  173.2 3.9 %collective-permute-done.23 = f32[192,512]{1,0:T(8,128)S(1)} collective-permute-done((f32[192,512]{1,0:T(8,128)}, f32[192,512]{1,0:T(8,128)S(1)}, u32[]{:S(2)}, u32[]{:S(2)}) %collective-permute-start.23) | collective-permute-done | bytes 393248 | tf_op jit(solution)/shard_map/ppermute | solution.py:17
  187.7 6.7 %all-to-all-start = ((f32[64,8,512]{2,1,0:T(8,128)}), f32[64,8,512]{2,1,0:T(8,128)S(1)}, u32[]{:S(2)}, u32[]{:S(2)}) async-start(f32[64,8,512]{2,1,0:T(8,128)} %bitcast_add_fusion), calls=%async_computation | async-start | bytes 2097152 | tf_op jit(solution)/shard_map/all_to_all | solution.py:193
  198.5 14.7 %all-to-all-done = f32[64,8,512]{2,1,0:T(8,128)S(1)} async-done(((f32[64,8,512]{2,1,0:T(8,128)}), f32[64,8,512]{2,1,0:T(8,128)S(1)}, u32[]{:S(2)}, u32[]{:S(2)}) %all-to-all-start) | async-done | bytes 1048608 | tf_op jit(solution)/shard_map/all_to_all | solution.py:193
  (88 shorter events, 55.2 us)
Async XLA Ops:
  6.1 16.5 %collective-permute-start.3 = (f32[96,1024]{1,0:T(8,128)S(1)}, f32[96,1024]{1,0:T(8,128)S(1)}, u32[]{:S(2)}, u32[]{:S(2)}) collective-permute-start(f32[96,1024]{1,0:T(8,128)S(1)} %get-tuple-element.67), channel_id=1, source_target_pairs={{0,0},{1,16},{2,32},{3,48},{4,64},{5,80},{6,96},{7,112},{8,1},{9,1... | collective-permute-start | bytes 1179656 | tf_op jit(solution)/shard_map/ppermute | solution.py:31
  6.8 25.8 %collective-permute-start.1 = (f32[96,1024]{1,0:T(8,128)S(1)}, f32[96,1024]{1,0:T(8,128)S(1)}, u32[]{:S(2)}, u32[]{:S(2)}) collective-permute-start(f32[96,1024]{1,0:T(8,128)S(1)} %collective-permute-done.refs_0_), channel_id=1, source_target_pairs={{0,16},{16,32},{32,48},{48,0},{1,17},{17,33},{33,49},{49,1},{2,18}... | collective-permute-start | bytes 1179656 | tf_op jit(solution)/shard_map/ppermute | solution.py:17
  16.1 17.1 %collective-permute-start.2 = (f32[96,1024]{1,0:T(8,128)S(1)}, f32[96,1024]{1,0:T(8,128)S(1)}, u32[]{:S(2)}, u32[]{:S(2)}) collective-permute-start(f32[96,1024]{1,0:T(8,128)S(1)} %collective-permute-done.refs_0_), channel_id=1, source_target_pairs={{0,48},{16,0},{32,16},{48,32},{1,49},{17,1},{33,17},{49,33},{2,50}... | collective-permute-start | bytes 1179656 | tf_op jit(solution)/shard_map/ppermute | solution.py:17
  33.3 13.0 %collective-permute-start.4 = (f32[96,1024]{1,0:T(8,128)S(1)}, f32[96,1024]{1,0:T(8,128)S(1)}, u32[]{:S(2)}, u32[]{:S(2)}) collective-permute-start(f32[96,1024]{1,0:T(8,128)S(1)} %collective-permute-done.3.refs_1_), channel_id=1, source_target_pairs={{0,16},{16,32},{32,48},{48,0},{1,17},{17,33},{33,49},{49,1},{2,18}... | collective-permute-start | bytes 1179656 | tf_op jit(solution)/shard_map/ppermute | solution.py:17
  37.5 21.8 %collective-permute-start.8 = (f32[192,1024]{1,0:T(8,128)}, f32[192,1024]{1,0:T(8,128)S(1)}, u32[]{:S(2)}, u32[]{:S(2)}) collective-permute-start(f32[192,1024]{1,0:T(8,128)} %pad_maximum_fusion.3), channel_id=1, source_target_pairs={{0,64},{64,0},{1,65},{65,1},{2,66},{66,2},{3,67},{67,3},{4,68},{68... | collective-permute-start | bytes 2359304 | tf_op jit(solution)/shard_map/ppermute | solution.py:17
  42.2 12.7 %collective-permute-start.6 = (f32[96,1024]{1,0:T(8,128)S(1)}, f32[96,1024]{1,0:T(8,128)S(1)}, u32[]{:S(2)}, u32[]{:S(2)}) collective-permute-start(f32[96,1024]{1,0:T(8,128)S(1)} %collective-permute-done.1.refs_4_), channel_id=1, source_target_pairs={{0,16},{16,32},{32,48},{48,0},{1,17},{17,33},{33,49},{49,1},{2,18}... | collective-permute-start | bytes 1179656 | tf_op jit(solution)/shard_map/ppermute | solution.py:17
  59.2 26.6 %collective-permute-start.10 = (f32[192,1024]{1,0:T(8,128)S(1)}, f32[192,1024]{1,0:T(8,128)S(1)}, u32[]{:S(2)}, u32[]{:S(2)}) collective-permute-start(f32[192,1024]{1,0:T(8,128)S(1)} %collective-permute-done.8.refs_0_), channel_id=1, source_target_pairs={{0,16},{16,32},{32,48},{48,0},{1,17},{17,33},{33,49},{49,1},{2,18}... | collective-permute-start | bytes 2359304 | tf_op jit(solution)/shard_map/ppermute | solution.py:17
  59.3 26.6 %collective-permute-start.9 = (f32[192,1024]{1,0:T(8,128)S(1)}, f32[192,1024]{1,0:T(8,128)S(1)}, u32[]{:S(2)}, u32[]{:S(2)}) collective-permute-start(f32[192,1024]{1,0:T(8,128)S(1)} %collective-permute-done.8.refs_0_), channel_id=1, source_target_pairs={{0,48},{16,0},{32,16},{48,32},{1,49},{17,1},{33,17},{49,33},{2,50}... | collective-permute-start | bytes 2359304 | tf_op jit(solution)/shard_map/ppermute | solution.py:17
  62.5 23.3 %collective-permute-start.11 = (f32[96,1024]{1,0:T(8,128)S(1)}, f32[96,1024]{1,0:T(8,128)S(1)}, u32[]{:S(2)}, u32[]{:S(2)}) collective-permute-start(f32[96,1024]{1,0:T(8,128)S(1)} %collective-permute-done.6.refs_6_), channel_id=1, source_target_pairs={{0,64},{64,0},{1,65},{65,1},{2,66},{66,2},{3,67},{67,3},{4,68},{68... | collective-permute-start | bytes 1179656 | tf_op jit(solution)/shard_map/ppermute | solution.py:17
  64.1 21.7 %collective-permute-start.12 = (f32[96,1024]{1,0:T(8,128)}, f32[96,1024]{1,0:T(8,128)S(1)}, u32[]{:S(2)}, u32[]{:S(2)}) collective-permute-start(f32[96,1024]{1,0:T(8,128)} %collective-permute-done.7.refs_7_), channel_id=1, source_target_pairs={{0,64},{64,0},{1,65},{65,1},{2,66},{66,2},{3,67},{67,3},{4,68},{68... | collective-permute-start | bytes 1179656 | tf_op jit(solution)/shard_map/ppermute | solution.py:17
  98.8 13.0 %collective-permute-start.13 = (f32[2,4,192,512]{3,2,1,0:T(8,128)S(1)}, f32[2,4,192,512]{3,2,1,0:T(8,128)S(1)}, u32[]{:S(2)}, u32[]{:S(2)}) collective-permute-start(f32[2,4,192,512]{3,2,1,0:T(8,128)S(1)} %get-tuple-element.44), channel_id=1, source_target_pairs={{0,1},{1,0},{2,3},{3,2},{4,5},{5,4},{6,7},{7,6},{8,9},{9,8},{10,11... | collective-permute-start | bytes 9437192 | tf_op jit(solution)/shard_map/ppermute | solution.py:17
  114.1 18.2 %collective-permute-start.14 = (f32[192,512]{1,0:T(8,128)S(1)}, f32[192,512]{1,0:T(8,128)S(1)}, u32[]{:S(2)}, u32[]{:S(2)}) collective-permute-start(f32[192,512]{1,0:T(8,128)S(1)} %get-tuple-element.57), channel_id=1, source_target_pairs={{0,2},{2,4},{4,6},{6,0},{1,3},{3,5},{5,7},{7,1},{8,10},{10,12},{12... | collective-permute-start | bytes 1179656 | tf_op jit(solution)/shard_map/ppermute | solution.py:17
  117.6 14.7 %collective-permute-start.18 = (f32[192,512]{1,0:T(8,128)S(1)}, f32[192,512]{1,0:T(8,128)S(1)}, u32[]{:S(2)}, u32[]{:S(2)}) collective-permute-start(f32[192,512]{1,0:T(8,128)S(1)} %get-tuple-element.58), channel_id=1, source_target_pairs={{0,6},{2,0},{4,2},{6,4},{1,7},{3,1},{5,3},{7,5},{8,14},{10,8},{12,... | collective-permute-start | bytes 1179656 | tf_op jit(solution)/shard_map/ppermute | solution.py:17
  124.3 16.4 %collective-permute-start.22 = (f32[192,512]{1,0:T(8,128)S(1)}, f32[192,512]{1,0:T(8,128)S(1)}, u32[]{:S(2)}, u32[]{:S(2)}) collective-permute-start(f32[192,512]{1,0:T(8,128)S(1)} %get-tuple-element.63), channel_id=1, source_target_pairs={{0,2},{2,4},{4,6},{6,0},{1,3},{3,5},{5,7},{7,1},{8,10},{10,12},{12... | collective-permute-start | bytes 1179656 | tf_op jit(solution)/shard_map/ppermute | solution.py:17
  124.3 16.4 %collective-permute-start.26 = (f32[192,512]{1,0:T(8,128)S(1)}, f32[192,512]{1,0:T(8,128)S(1)}, u32[]{:S(2)}, u32[]{:S(2)}) collective-permute-start(f32[192,512]{1,0:T(8,128)S(1)} %get-tuple-element.64), channel_id=1, source_target_pairs={{0,6},{2,0},{4,2},{6,4},{1,7},{3,1},{5,3},{7,5},{8,14},{10,8},{12,... | collective-permute-start | bytes 1179656 | tf_op jit(solution)/shard_map/ppermute | solution.py:17
  127.8 21.3 %collective-permute-start.17 = (f32[192,512]{1,0:T(8,128)S(1)}, f32[192,512]{1,0:T(8,128)S(1)}, u32[]{:S(2)}, u32[]{:S(2)}) collective-permute-start(f32[192,512]{1,0:T(8,128)S(1)} %get-tuple-element.59), channel_id=1, source_target_pairs={{0,2},{2,4},{4,6},{6,0},{1,3},{3,5},{5,7},{7,1},{8,10},{10,12},{12... | collective-permute-start | bytes 1179656 | tf_op jit(solution)/shard_map/ppermute | solution.py:17
  133.2 18.0 %collective-permute-start.19 = (f32[192,512]{1,0:T(8,128)S(1)}, f32[192,512]{1,0:T(8,128)S(1)}, u32[]{:S(2)}, u32[]{:S(2)}) collective-permute-start(f32[192,512]{1,0:T(8,128)S(1)} %get-tuple-element.56), channel_id=1, source_target_pairs={{0,6},{2,0},{4,2},{6,4},{1,7},{3,1},{5,3},{7,5},{8,14},{10,8},{12,... | collective-permute-start | bytes 1179656 | tf_op jit(solution)/shard_map/ppermute | solution.py:17
  136.5 33.4 %collective-permute-start.29 = (f32[192,1024]{1,0:T(8,128)}, f32[192,1024]{1,0:T(8,128)}, u32[]{:S(2)}, u32[]{:S(2)}) collective-permute-start(f32[192,1024]{1,0:T(8,128)} %mul.18), channel_id=1, source_target_pairs={{0,8},{8,0},{1,9},{9,1},{2,10},{10,2},{3,11},{11,3},{4,12},{12,4},... | collective-permute-start | bytes 2359304 | tf_op jit(solution)/shard_map/ppermute | solution.py:17
  140.7 16.9 %collective-permute-start.25 = (f32[192,512]{1,0:T(8,128)S(1)}, f32[192,512]{1,0:T(8,128)S(1)}, u32[]{:S(2)}, u32[]{:S(2)}) collective-permute-start(f32[192,512]{1,0:T(8,128)S(1)} %get-tuple-element.65), channel_id=1, source_target_pairs={{0,2},{2,4},{4,6},{6,0},{1,3},{3,5},{5,7},{7,1},{8,10},{10,12},{12... | collective-permute-start | bytes 1179656 | tf_op jit(solution)/shard_map/ppermute | solution.py:17
  141.7 17.0 %collective-permute-start.27 = (f32[192,512]{1,0:T(8,128)}, f32[192,512]{1,0:T(8,128)}, u32[]{:S(2)}, u32[]{:S(2)}) collective-permute-start(f32[192,512]{1,0:T(8,128)} %get-tuple-element.62), channel_id=1, source_target_pairs={{0,6},{2,0},{4,2},{6,4},{1,7},{3,1},{5,3},{7,5},{8,14},{10,8},{12,... | collective-permute-start | bytes 1179656 | tf_op jit(solution)/shard_map/ppermute | solution.py:17
  149.1 16.5 %collective-permute-start.16 = (f32[192,512]{1,0:T(8,128)}, f32[192,512]{1,0:T(8,128)}, u32[]{:S(2)}, u32[]{:S(2)}) collective-permute-start(f32[192,512]{1,0:T(8,128)} %get-tuple-element.60), channel_id=1, source_target_pairs={{0,6},{2,0},{4,2},{6,4},{1,7},{3,1},{5,3},{7,5},{8,14},{10,8},{12,... | collective-permute-start | bytes 1179656 | tf_op jit(solution)/shard_map/ppermute | solution.py:17
  151.2 16.4 %collective-permute-start.15 = (f32[192,512]{1,0:T(8,128)}, f32[192,512]{1,0:T(8,128)}, u32[]{:S(2)}, u32[]{:S(2)}) collective-permute-start(f32[192,512]{1,0:T(8,128)} %get-tuple-element.55), channel_id=1, source_target_pairs={{0,2},{2,4},{4,6},{6,0},{1,3},{3,5},{5,7},{7,1},{8,10},{10,12},{12... | collective-permute-start | bytes 1179656 | tf_op jit(solution)/shard_map/ppermute | solution.py:17
  158.8 14.4 %collective-permute-start.24 = (f32[192,512]{1,0:T(8,128)}, f32[192,512]{1,0:T(8,128)S(1)}, u32[]{:S(2)}, u32[]{:S(2)}) collective-permute-start(f32[192,512]{1,0:T(8,128)} %get-tuple-element.66), channel_id=1, source_target_pairs={{0,6},{2,0},{4,2},{6,4},{1,7},{3,1},{5,3},{7,5},{8,14},{10,8},{12,... | collective-permute-start | bytes 1179656 | tf_op jit(solution)/shard_map/ppermute | solution.py:17
  187.7 25.5 %all-to-all-start = ((f32[64,8,512]{2,1,0:T(8,128)}), f32[64,8,512]{2,1,0:T(8,128)S(1)}, u32[]{:S(2)}, u32[]{:S(2)}) async-start(f32[64,8,512]{2,1,0:T(8,128)} %bitcast_add_fusion), calls=%async_computation | async-start | bytes 2097152 | tf_op jit(solution)/shard_map/all_to_all | solution.py:193
  (15 other events, 213.2 us)

commit v5 on v4

--- a/solution.py
+++ b/solution.py
@@ -181,7 +181,7 @@
         panel,
         rows,
         (((0,), (0,)), ((), ())),
-        precision=lax.Precision.HIGHEST,
+        precision=lax.Precision.HIGH,
         preferred_element_type=jnp.float32,
     )
 
@@ -210,7 +210,8 @@
     pattern = expand_local(lmask, block_rows, supernode)
     lmasked = lpanel * pattern
     half = rows_local // 2
-    mine_top, mine_low = to_slabs(lmasked[:half]), to_slabs(lmasked[half:])
+    mine_top = to_slabs(lpanel[:half] * pattern[:half])
+    mine_low = to_slabs(lpanel[half:] * pattern[half:])
     (mine_top,) = fence(mine_top)
     left_top, right_top, mine_low = fence(
         shift(mine_top, "x", 1), shift(mine_top, "x", -1), mine_low

time: 215 us -> 212 us (0.986)
  transfers between devices with their start and end apart: 32 -> 32, of which waited for: 16 -> 16; matrix products, arithmetic and copies ran while one was open for 7% -> 8% of each run, Pallas kernels for 15% -> 16%
where the time goes in v5:
time: 212 us; the launch traced here: 211 us
  starting transfers between devices  69 us (33%)
  waiting for transfers between devices  66.2 us (31%)
  Pallas kernels  45.6 us (22%)
  other arithmetic  19.1 us (9%)
  local copies, waits for them, and re-layouts  4.92 us (2%)
  matrix products  4.39 us (2%)
    ppermute x29, starting transfers between devices, shift(): lax.ppermute(array, axis, [(i, (i + by) % size) for i in range(size)])  60 us
    ppermute x29, waiting for transfers between devices, shift(): lax.ppermute(array, axis, [(i, (i + by) % size) for i in range(size)])  51.5 us
    pallas_call x2, Pallas kernels, far_product(): pl.pallas_call(functools.partial(far_kernel, columns), grid_spec=pltpu.Pr...  25.8 us
    pallas_call x1, Pallas kernels, near_product(): pl.pallas_call(near_kernel, grid_spec=pltpu.PrefetchScalarGridSpec(num_sc...  19.8 us
    all_to_all x1, waiting for transfers between devices, sum_diag(): lax.all_to_all(terms, ('zh', 'x', 'zl', 'y'), 0, 0, tiled=True)  14.7 us
    all_to_all x1, starting transfers between devices, sum_diag(): lax.all_to_all(terms, ('zh', 'x', 'zl', 'y'), 0, 0, tiled=True)  7.59 us
    dot_general x2, matrix products, diag_term(): lax.dot_general(panel, rows, (((0,), (0,)), ((), ())), precision=lax.Prec...  4.39 us
  transfers between devices with their start and end apart: 32, of which 16 were waited for; matrix products, arithmetic and copies ran while one was open for 8% of the time, Pallas kernels for 16%

profile of v5, /device:TPU:0, one launch (start us, length us, event | category | flops | bytes accessed | tf_op | source)
XLA Modules:
  0.0 210.7 jit_solution(1348610309026462031)
XLA Ops:
  4.7 9.3 %collective-permute-start.1 = (f32[96,1024]{1,0:T(8,128)S(1)}, f32[96,1024]{1,0:T(8,128)S(1)}, u32[]{:S(2)}, u32[]{:S(2)}) collective-permute-start(f32[96,1024]{1,0:T(8,128)S(1)} %collective-permute-done.refs_0_), channel_id=1, source_target_pairs={{0,16},{16,32},{32,48},{48,0},{1,17},{17,33},{33,49},{49,1},{2,18}... | collective-permute-start | bytes 1179656 | tf_op jit(solution)/shard_map/ppermute | solution.py:17
  14.0 6.5 %collective-permute-start.2 = (f32[96,1024]{1,0:T(8,128)S(1)}, f32[96,1024]{1,0:T(8,128)S(1)}, u32[]{:S(2)}, u32[]{:S(2)}) collective-permute-start(f32[96,1024]{1,0:T(8,128)S(1)} %collective-permute-done.refs_0_), channel_id=1, source_target_pairs={{0,48},{16,0},{32,16},{48,32},{1,49},{17,1},{33,17},{49,33},{2,50}... | collective-permute-start | bytes 1179656 | tf_op jit(solution)/shard_map/ppermute | solution.py:17
  20.6 10.0 %collective-permute-done.1.refs_4_ = f32[96,1024]{1,0:T(8,128)S(1)} collective-permute-done((f32[96,1024]{1,0:T(8,128)S(1)}, f32[96,1024]{1,0:T(8,128)S(1)}, u32[]{:S(2)}, u32[]{:S(2)}) %collective-permute-start.1) | collective-permute-done | bytes 393248 | tf_op jit(solution)/shard_map/ppermute | solution.py:17
  35.3 4.7 %collective-permute-start.8 = (f32[192,1024]{1,0:T(8,128)}, f32[192,1024]{1,0:T(8,128)S(1)}, u32[]{:S(2)}, u32[]{:S(2)}) collective-permute-start(f32[192,1024]{1,0:T(8,128)} %pad_maximum_fusion.3), channel_id=1, source_target_pairs={{0,64},{64,0},{1,65},{65,1},{2,66},{66,2},{3,67},{67,3},{4,68},{68... | collective-permute-start | bytes 2359304 | tf_op jit(solution)/shard_map/ppermute | solution.py:17
  40.9 3.2 %collective-permute-done.4.refs_5_ = f32[96,1024]{1,0:T(8,128)S(1)} collective-permute-done((f32[96,1024]{1,0:T(8,128)S(1)}, f32[96,1024]{1,0:T(8,128)S(1)}, u32[]{:S(2)}, u32[]{:S(2)}) %collective-permute-start.4) | collective-permute-done | bytes 393248 | tf_op jit(solution)/shard_map/ppermute | solution.py:17
  44.1 3.4 %collective-permute-start.7 = (f32[96,1024]{1,0:T(8,128)S(1)}, f32[96,1024]{1,0:T(8,128)}, u32[]{:S(2)}, u32[]{:S(2)}) collective-permute-start(f32[96,1024]{1,0:T(8,128)S(1)} %collective-permute-done.5.refs_3_), channel_id=1, source_target_pairs={{0,48},{16,0},{32,16},{48,32},{1,49},{17,1},{33,17},{49,33},{2,50}... | collective-permute-start | bytes 1179656 | tf_op jit(solution)/shard_map/ppermute | solution.py:17
  52.8 3.4 %collective-permute-done.7.refs_7_ = f32[96,1024]{1,0:T(8,128)} collective-permute-done((f32[96,1024]{1,0:T(8,128)S(1)}, f32[96,1024]{1,0:T(8,128)}, u32[]{:S(2)}, u32[]{:S(2)}) %collective-permute-start.7) | collective-permute-done | bytes 393248 | tf_op jit(solution)/shard_map/ppermute | solution.py:17
  57.1 2.8 %collective-permute-start.9 = (f32[192,1024]{1,0:T(8,128)S(1)}, f32[192,1024]{1,0:T(8,128)S(1)}, u32[]{:S(2)}, u32[]{:S(2)}) collective-permute-start(f32[192,1024]{1,0:T(8,128)S(1)} %collective-permute-done.8.refs_0_), channel_id=1, source_target_pairs={{0,48},{16,0},{32,16},{48,32},{1,49},{17,1},{33,17},{49,33},{2,50}... | collective-permute-start | bytes 2359304 | tf_op jit(solution)/shard_map/ppermute | solution.py:17
  63.5 19.8 %shard_map.94 = f32[3072,1024]{1,0:T(8,128)} custom-call(s32[5]{0:T(128)S(1)} %stack.23.where, f32[3072,1536]{1,0:T(8,128)} %a_ref.1, f32[96,1024]{1,0:T(8,128)S(1)} %collective-permute-done.refs_0_, f32[96,1024]{1,0:T(8,128)S(1)} %collective-permute-done.3.refs_1_, f32[96,1024]{1,0:T(8,128)S(1)} %collective-permute-done.2.refs_2_, ...), custom_call_target="tpu_custom_call" | custom-call | flops 14495514624 | bytes 22020096 | tf_op jit(solution)/shard_map/pallas_call | solution.py:71
  83.3 12.9 %shard_map.95 = (f32[2,4,192,512]{3,2,1,0:T(8,128)S(1)}, f32[2,4,192,512]{3,2,1,0:T(8,128)S(1)}) custom-call(s32[5]{0:T(128)S(1)} %stack.23.where, f32[2,4,2,192,1536]{4,3,2,1,0:T(8,128)} %bitcast.78, f32[2,4,2,192,1024]{4,3,2,1,0:T(8,128)} %bitcast.80, f32[192,1024]{1,0:T(8,128)S(1)} %collective-permute-done.8.refs_0_, ...), custom_call_target="tpu_custom_call" | custom-call | flops 7247757312 | bytes 22020096 | tf_op jit(solution)/shard_map/pallas_call | solution.py:133
  96.3 12.9 %shard_map.96 = (f32[2,4,192,512]{3,2,1,0:T(8,128)S(1)}, f32[2,4,192,512]{3,2,1,0:T(8,128)S(1)}) custom-call(s32[5]{0:T(128)S(1)} %stack.23.where, f32[2,4,2,192,1536]{4,3,2,1,0:T(8,128)} %bitcast.79, f32[2,4,2,192,1024]{4,3,2,1,0:T(8,128)} %bitcast.81, f32[192,1024]{1,0:T(8,128)S(1)} %collective-permute-done.8.refs_0_, ...), custom_call_target="tpu_custom_call" | custom-call | flops 7247757312 | bytes 22020096 | tf_op jit(solution)/shard_map/pallas_call | solution.py:133
  114.3 4.7 %collective-permute-start.18 = (f32[192,512]{1,0:T(8,128)S(1)}, f32[192,512]{1,0:T(8,128)S(1)}, u32[]{:S(2)}, u32[]{:S(2)}) collective-permute-start(f32[192,512]{1,0:T(8,128)S(1)} %get-tuple-element.58), channel_id=1, source_target_pairs={{0,6},{2,0},{4,2},{6,4},{1,7},{3,1},{5,3},{7,5},{8,14},{10,8},{12,... | collective-permute-start | bytes 1179656 | tf_op jit(solution)/shard_map/ppermute | solution.py:17
  121.0 3.5 %collective-permute-start.26 = (f32[192,512]{1,0:T(8,128)S(1)}, f32[192,512]{1,0:T(8,128)S(1)}, u32[]{:S(2)}, u32[]{:S(2)}) collective-permute-start(f32[192,512]{1,0:T(8,128)S(1)} %get-tuple-element.64), channel_id=1, source_target_pairs={{0,6},{2,0},{4,2},{6,4},{1,7},{3,1},{5,3},{7,5},{8,14},{10,8},{12,... | collective-permute-start | bytes 1179656 | tf_op jit(solution)/shard_map/ppermute | solution.py:17
  124.5 4.5 %collective-permute-done.14 = f32[192,512]{1,0:T(8,128)S(1)} collective-permute-done((f32[192,512]{1,0:T(8,128)S(1)}, f32[192,512]{1,0:T(8,128)S(1)}, u32[]{:S(2)}, u32[]{:S(2)}) %collective-permute-start.14) | collective-permute-done | bytes 393248 | tf_op jit(solution)/shard_map/ppermute | solution.py:17
  129.9 3.3 %collective-permute-start.19 = (f32[192,512]{1,0:T(8,128)S(1)}, f32[192,512]{1,0:T(8,128)S(1)}, u32[]{:S(2)}, u32[]{:S(2)}) collective-permute-start(f32[192,512]{1,0:T(8,128)S(1)} %get-tuple-element.56), channel_id=1, source_target_pairs={{0,6},{2,0},{4,2},{6,4},{1,7},{3,1},{5,3},{7,5},{8,14},{10,8},{12,... | collective-permute-start | bytes 1179656 | tf_op jit(solution)/shard_map/ppermute | solution.py:17
  133.6 3.8 %collective-permute-done.22 = f32[192,512]{1,0:T(8,128)S(1)} collective-permute-done((f32[192,512]{1,0:T(8,128)S(1)}, f32[192,512]{1,0:T(8,128)S(1)}, u32[]{:S(2)}, u32[]{:S(2)}) %collective-permute-start.22) | collective-permute-done | bytes 393248 | tf_op jit(solution)/shard_map/ppermute | solution.py:17
  138.4 3.3 %collective-permute-start.27 = (f32[192,512]{1,0:T(8,128)}, f32[192,512]{1,0:T(8,128)}, u32[]{:S(2)}, u32[]{:S(2)}) collective-permute-start(f32[192,512]{1,0:T(8,128)} %get-tuple-element.62), channel_id=1, source_target_pairs={{0,6},{2,0},{4,2},{6,4},{1,7},{3,1},{5,3},{7,5},{8,14},{10,8},{12,... | collective-permute-start | bytes 1179656 | tf_op jit(solution)/shard_map/ppermute | solution.py:17
  141.7 4.1 %collective-permute-done.17 = f32[192,512]{1,0:T(8,128)S(1)} collective-permute-done((f32[192,512]{1,0:T(8,128)S(1)}, f32[192,512]{1,0:T(8,128)S(1)}, u32[]{:S(2)}, u32[]{:S(2)}) %collective-permute-start.17) | collective-permute-done | bytes 393248 | tf_op jit(solution)/shard_map/ppermute | solution.py:17
  148.0 6.2 %collective-permute-done.25 = f32[192,512]{1,0:T(8,128)S(1)} collective-permute-done((f32[192,512]{1,0:T(8,128)S(1)}, f32[192,512]{1,0:T(8,128)S(1)}, u32[]{:S(2)}, u32[]{:S(2)}) %collective-permute-start.25) | collective-permute-done | bytes 393248 | tf_op jit(solution)/shard_map/ppermute | solution.py:17
  158.8 3.5 %collective-permute-done.16 = f32[192,512]{1,0:T(8,128)} collective-permute-done((f32[192,512]{1,0:T(8,128)}, f32[192,512]{1,0:T(8,128)}, u32[]{:S(2)}, u32[]{:S(2)}) %collective-permute-start.16) | collective-permute-done | bytes 393248 | tf_op jit(solution)/shard_map/ppermute | solution.py:17
  169.9 3.9 %collective-permute-done.23 = f32[192,512]{1,0:T(8,128)S(1)} collective-permute-done((f32[192,512]{1,0:T(8,128)}, f32[192,512]{1,0:T(8,128)S(1)}, u32[]{:S(2)}, u32[]{:S(2)}) %collective-permute-start.23) | collective-permute-done | bytes 393248 | tf_op jit(solution)/shard_map/ppermute | solution.py:17
  178.1 3.0 %collective-permute-done.30 = f32[64,8,512]{2,1,0:T(8,128)} collective-permute-done((f32[64,8,512]{2,1,0:T(8,128)}, f32[64,8,512]{2,1,0:T(8,128)}, u32[]{:S(2)}, u32[]{:S(2)}) %collective-permute-start.30) | collective-permute-done | bytes 1048608 | tf_op jit(solution)/shard_map/ppermute | solution.py:17
  183.6 7.6 %all-to-all-start = ((f32[64,8,512]{2,1,0:T(8,128)}), f32[64,8,512]{2,1,0:T(8,128)S(1)}, u32[]{:S(2)}, u32[]{:S(2)}) async-start(f32[64,8,512]{2,1,0:T(8,128)} %bitcast_add_fusion), calls=%async_computation | async-start | bytes 2097152 | tf_op jit(solution)/shard_map/all_to_all | solution.py:193
  195.3 14.7 %all-to-all-done = f32[64,8,512]{2,1,0:T(8,128)S(1)} async-done(((f32[64,8,512]{2,1,0:T(8,128)}), f32[64,8,512]{2,1,0:T(8,128)S(1)}, u32[]{:S(2)}, u32[]{:S(2)}) %all-to-all-start) | async-done | bytes 1048608 | tf_op jit(solution)/shard_map/all_to_all | solution.py:193
  (88 shorter events, 54.0 us)
Async XLA Ops:
  4.0 16.5 %collective-permute-start.3 = (f32[96,1024]{1,0:T(8,128)S(1)}, f32[96,1024]{1,0:T(8,128)S(1)}, u32[]{:S(2)}, u32[]{:S(2)}) collective-permute-start(f32[96,1024]{1,0:T(8,128)S(1)} %get-tuple-element.67), channel_id=1, source_target_pairs={{0,0},{1,16},{2,32},{3,48},{4,64},{5,80},{6,96},{7,112},{8,1},{9,1... | collective-permute-start | bytes 1179656 | tf_op jit(solution)/shard_map/ppermute | solution.py:31
  4.7 25.8 %collective-permute-start.1 = (f32[96,1024]{1,0:T(8,128)S(1)}, f32[96,1024]{1,0:T(8,128)S(1)}, u32[]{:S(2)}, u32[]{:S(2)}) collective-permute-start(f32[96,1024]{1,0:T(8,128)S(1)} %collective-permute-done.refs_0_), channel_id=1, source_target_pairs={{0,16},{16,32},{32,48},{48,0},{1,17},{17,33},{33,49},{49,1},{2,18}... | collective-permute-start | bytes 1179656 | tf_op jit(solution)/shard_map/ppermute | solution.py:17
  14.0 17.1 %collective-permute-start.2 = (f32[96,1024]{1,0:T(8,128)S(1)}, f32[96,1024]{1,0:T(8,128)S(1)}, u32[]{:S(2)}, u32[]{:S(2)}) collective-permute-start(f32[96,1024]{1,0:T(8,128)S(1)} %collective-permute-done.refs_0_), channel_id=1, source_target_pairs={{0,48},{16,0},{32,16},{48,32},{1,49},{17,1},{33,17},{49,33},{2,50}... | collective-permute-start | bytes 1179656 | tf_op jit(solution)/shard_map/ppermute | solution.py:17
  31.2 13.0 %collective-permute-start.4 = (f32[96,1024]{1,0:T(8,128)S(1)}, f32[96,1024]{1,0:T(8,128)S(1)}, u32[]{:S(2)}, u32[]{:S(2)}) collective-permute-start(f32[96,1024]{1,0:T(8,128)S(1)} %collective-permute-done.3.refs_1_), channel_id=1, source_target_pairs={{0,16},{16,32},{32,48},{48,0},{1,17},{17,33},{33,49},{49,1},{2,18}... | collective-permute-start | bytes 1179656 | tf_op jit(solution)/shard_map/ppermute | solution.py:17
  35.3 21.8 %collective-permute-start.8 = (f32[192,1024]{1,0:T(8,128)}, f32[192,1024]{1,0:T(8,128)S(1)}, u32[]{:S(2)}, u32[]{:S(2)}) collective-permute-start(f32[192,1024]{1,0:T(8,128)} %pad_maximum_fusion.3), channel_id=1, source_target_pairs={{0,64},{64,0},{1,65},{65,1},{2,66},{66,2},{3,67},{67,3},{4,68},{68... | collective-permute-start | bytes 2359304 | tf_op jit(solution)/shard_map/ppermute | solution.py:17
  40.1 12.7 %collective-permute-start.6 = (f32[96,1024]{1,0:T(8,128)S(1)}, f32[96,1024]{1,0:T(8,128)S(1)}, u32[]{:S(2)}, u32[]{:S(2)}) collective-permute-start(f32[96,1024]{1,0:T(8,128)S(1)} %collective-permute-done.1.refs_4_), channel_id=1, source_target_pairs={{0,16},{16,32},{32,48},{48,0},{1,17},{17,33},{33,49},{49,1},{2,18}... | collective-permute-start | bytes 1179656 | tf_op jit(solution)/shard_map/ppermute | solution.py:17
  57.1 26.1 %collective-permute-start.9 = (f32[192,1024]{1,0:T(8,128)S(1)}, f32[192,1024]{1,0:T(8,128)S(1)}, u32[]{:S(2)}, u32[]{:S(2)}) collective-permute-start(f32[192,1024]{1,0:T(8,128)S(1)} %collective-permute-done.8.refs_0_), channel_id=1, source_target_pairs={{0,48},{16,0},{32,16},{48,32},{1,49},{17,1},{33,17},{49,33},{2,50}... | collective-permute-start | bytes 2359304 | tf_op jit(solution)/shard_map/ppermute | solution.py:17
  59.9 23.3 %collective-permute-start.10 = (f32[192,1024]{1,0:T(8,128)S(1)}, f32[192,1024]{1,0:T(8,128)S(1)}, u32[]{:S(2)}, u32[]{:S(2)}) collective-permute-start(f32[192,1024]{1,0:T(8,128)S(1)} %collective-permute-done.8.refs_0_), channel_id=1, source_target_pairs={{0,16},{16,32},{32,48},{48,0},{1,17},{17,33},{33,49},{49,1},{2,18}... | collective-permute-start | bytes 2359304 | tf_op jit(solution)/shard_map/ppermute | solution.py:17
  59.9 23.3 %collective-permute-start.11 = (f32[96,1024]{1,0:T(8,128)S(1)}, f32[96,1024]{1,0:T(8,128)S(1)}, u32[]{:S(2)}, u32[]{:S(2)}) collective-permute-start(f32[96,1024]{1,0:T(8,128)S(1)} %collective-permute-done.6.refs_6_), channel_id=1, source_target_pairs={{0,64},{64,0},{1,65},{65,1},{2,66},{66,2},{3,67},{67,3},{4,68},{68... | collective-permute-start | bytes 1179656 | tf_op jit(solution)/shard_map/ppermute | solution.py:17
  60.8 22.5 %collective-permute-start.12 = (f32[96,1024]{1,0:T(8,128)}, f32[96,1024]{1,0:T(8,128)S(1)}, u32[]{:S(2)}, u32[]{:S(2)}) collective-permute-start(f32[96,1024]{1,0:T(8,128)} %collective-permute-done.7.refs_7_), channel_id=1, source_target_pairs={{0,64},{64,0},{1,65},{65,1},{2,66},{66,2},{3,67},{67,3},{4,68},{68... | collective-permute-start | bytes 1179656 | tf_op jit(solution)/shard_map/ppermute | solution.py:17
  96.2 13.0 %collective-permute-start.13 = (f32[2,4,192,512]{3,2,1,0:T(8,128)S(1)}, f32[2,4,192,512]{3,2,1,0:T(8,128)S(1)}, u32[]{:S(2)}, u32[]{:S(2)}) collective-permute-start(f32[2,4,192,512]{3,2,1,0:T(8,128)S(1)} %get-tuple-element.44), channel_id=1, source_target_pairs={{0,1},{1,0},{2,3},{3,2},{4,5},{5,4},{6,7},{7,6},{8,9},{9,8},{10,11... | collective-permute-start | bytes 9437192 | tf_op jit(solution)/shard_map/ppermute | solution.py:17
  111.5 17.4 %collective-permute-start.14 = (f32[192,512]{1,0:T(8,128)S(1)}, f32[192,512]{1,0:T(8,128)S(1)}, u32[]{:S(2)}, u32[]{:S(2)}) collective-permute-start(f32[192,512]{1,0:T(8,128)S(1)} %get-tuple-element.57), channel_id=1, source_target_pairs={{0,2},{2,4},{4,6},{6,0},{1,3},{3,5},{5,7},{7,1},{8,10},{10,12},{12... | collective-permute-start | bytes 1179656 | tf_op jit(solution)/shard_map/ppermute | solution.py:17
  114.3 14.7 %collective-permute-start.18 = (f32[192,512]{1,0:T(8,128)S(1)}, f32[192,512]{1,0:T(8,128)S(1)}, u32[]{:S(2)}, u32[]{:S(2)}) collective-permute-start(f32[192,512]{1,0:T(8,128)S(1)} %get-tuple-element.58), channel_id=1, source_target_pairs={{0,6},{2,0},{4,2},{6,4},{1,7},{3,1},{5,3},{7,5},{8,14},{10,8},{12,... | collective-permute-start | bytes 1179656 | tf_op jit(solution)/shard_map/ppermute | solution.py:17
  121.0 16.4 %collective-permute-start.22 = (f32[192,512]{1,0:T(8,128)S(1)}, f32[192,512]{1,0:T(8,128)S(1)}, u32[]{:S(2)}, u32[]{:S(2)}) collective-permute-start(f32[192,512]{1,0:T(8,128)S(1)} %get-tuple-element.63), channel_id=1, source_target_pairs={{0,2},{2,4},{4,6},{6,0},{1,3},{3,5},{5,7},{7,1},{8,10},{10,12},{12... | collective-permute-start | bytes 1179656 | tf_op jit(solution)/shard_map/ppermute | solution.py:17
  121.0 16.4 %collective-permute-start.26 = (f32[192,512]{1,0:T(8,128)S(1)}, f32[192,512]{1,0:T(8,128)S(1)}, u32[]{:S(2)}, u32[]{:S(2)}) collective-permute-start(f32[192,512]{1,0:T(8,128)S(1)} %get-tuple-element.64), channel_id=1, source_target_pairs={{0,6},{2,0},{4,2},{6,4},{1,7},{3,1},{5,3},{7,5},{8,14},{10,8},{12,... | collective-permute-start | bytes 1179656 | tf_op jit(solution)/shard_map/ppermute | solution.py:17
  124.5 21.3 %collective-permute-start.17 = (f32[192,512]{1,0:T(8,128)S(1)}, f32[192,512]{1,0:T(8,128)S(1)}, u32[]{:S(2)}, u32[]{:S(2)}) collective-permute-start(f32[192,512]{1,0:T(8,128)S(1)} %get-tuple-element.59), channel_id=1, source_target_pairs={{0,2},{2,4},{4,6},{6,0},{1,3},{3,5},{5,7},{7,1},{8,10},{10,12},{12... | collective-permute-start | bytes 1179656 | tf_op jit(solution)/shard_map/ppermute | solution.py:17
  129.9 18.0 %collective-permute-start.19 = (f32[192,512]{1,0:T(8,128)S(1)}, f32[192,512]{1,0:T(8,128)S(1)}, u32[]{:S(2)}, u32[]{:S(2)}) collective-permute-start(f32[192,512]{1,0:T(8,128)S(1)} %get-tuple-element.56), channel_id=1, source_target_pairs={{0,6},{2,0},{4,2},{6,4},{1,7},{3,1},{5,3},{7,5},{8,14},{10,8},{12,... | collective-permute-start | bytes 1179656 | tf_op jit(solution)/shard_map/ppermute | solution.py:17
  133.1 33.4 %collective-permute-start.29 = (f32[192,1024]{1,0:T(8,128)}, f32[192,1024]{1,0:T(8,128)}, u32[]{:S(2)}, u32[]{:S(2)}) collective-permute-start(f32[192,1024]{1,0:T(8,128)} %mul.26), channel_id=1, source_target_pairs={{0,8},{8,0},{1,9},{9,1},{2,10},{10,2},{3,11},{11,3},{4,12},{12,4},... | collective-permute-start | bytes 2359304 | tf_op jit(solution)/shard_map/ppermute | solution.py:17
  137.4 16.9 %collective-permute-start.25 = (f32[192,512]{1,0:T(8,128)S(1)}, f32[192,512]{1,0:T(8,128)S(1)}, u32[]{:S(2)}, u32[]{:S(2)}) collective-permute-start(f32[192,512]{1,0:T(8,128)S(1)} %get-tuple-element.65), channel_id=1, source_target_pairs={{0,2},{2,4},{4,6},{6,0},{1,3},{3,5},{5,7},{7,1},{8,10},{10,12},{12... | collective-permute-start | bytes 1179656 | tf_op jit(solution)/shard_map/ppermute | solution.py:17
  138.4 17.0 %collective-permute-start.27 = (f32[192,512]{1,0:T(8,128)}, f32[192,512]{1,0:T(8,128)}, u32[]{:S(2)}, u32[]{:S(2)}) collective-permute-start(f32[192,512]{1,0:T(8,128)} %get-tuple-element.62), channel_id=1, source_target_pairs={{0,6},{2,0},{4,2},{6,4},{1,7},{3,1},{5,3},{7,5},{8,14},{10,8},{12,... | collective-permute-start | bytes 1179656 | tf_op jit(solution)/shard_map/ppermute | solution.py:17
  145.8 16.5 %collective-permute-start.16 = (f32[192,512]{1,0:T(8,128)}, f32[192,512]{1,0:T(8,128)}, u32[]{:S(2)}, u32[]{:S(2)}) collective-permute-start(f32[192,512]{1,0:T(8,128)} %get-tuple-element.60), channel_id=1, source_target_pairs={{0,6},{2,0},{4,2},{6,4},{1,7},{3,1},{5,3},{7,5},{8,14},{10,8},{12,... | collective-permute-start | bytes 1179656 | tf_op jit(solution)/shard_map/ppermute | solution.py:17
  147.9 16.4 %collective-permute-start.15 = (f32[192,512]{1,0:T(8,128)}, f32[192,512]{1,0:T(8,128)}, u32[]{:S(2)}, u32[]{:S(2)}) collective-permute-start(f32[192,512]{1,0:T(8,128)} %get-tuple-element.55), channel_id=1, source_target_pairs={{0,2},{2,4},{4,6},{6,0},{1,3},{3,5},{5,7},{7,1},{8,10},{10,12},{12... | collective-permute-start | bytes 1179656 | tf_op jit(solution)/shard_map/ppermute | solution.py:17
  155.5 14.4 %collective-permute-start.24 = (f32[192,512]{1,0:T(8,128)}, f32[192,512]{1,0:T(8,128)S(1)}, u32[]{:S(2)}, u32[]{:S(2)}) collective-permute-start(f32[192,512]{1,0:T(8,128)} %get-tuple-element.66), channel_id=1, source_target_pairs={{0,6},{2,0},{4,2},{6,4},{1,7},{3,1},{5,3},{7,5},{8,14},{10,8},{12,... | collective-permute-start | bytes 1179656 | tf_op jit(solution)/shard_map/ppermute | solution.py:17
  183.6 26.4 %all-to-all-start = ((f32[64,8,512]{2,1,0:T(8,128)}), f32[64,8,512]{2,1,0:T(8,128)S(1)}, u32[]{:S(2)}, u32[]{:S(2)}) async-start(f32[64,8,512]{2,1,0:T(8,128)} %bitcast_add_fusion), calls=%async_computation | async-start | bytes 2097152 | tf_op jit(solution)/shard_map/all_to_all | solution.py:193
  (15 other events, 211.4 us)

commit v6 on v5

--- a/solution.py
+++ b/solution.py
@@ -67,7 +67,7 @@
 def near_product(ainv, pieces, where):
     total, depth = ainv.shape
     width = pieces[0].shape[1]
-    tile = total // 8
+    tile = total // 4
     return pl.pallas_call(
         near_kernel,
         grid_spec=pltpu.PrefetchScalarGridSpec(
@@ -111,7 +111,7 @@
 def far_product(ainv, near, pieces, where, supernode):
     total, depth = ainv.shape
     rows, width = pieces[0].shape[0], pieces[0].shape[1] // 2
-    tiles = 2
+    tiles = 4
 
     def rows_of(half, dz, part, where):
         core = jnp.bitwise_xor(where[4], 1 - half)
@@ -219,7 +219,7 @@
     left_low, right_low = shift(mine_low, "x", 1), shift(mine_low, "x", -1)
     across = shift(jnp.concatenate([mine_top, mine_low]), "zh", 1)
     left_low, right_low = fence(left_low, right_low)
-    top, bottom, across = fence(shift(left_top, "x", 1), shift(right_low, "x", -1), across)
+    top, bottom = fence(shift(left_top, "x", 1), shift(right_low, "x", -1))
     own = (mine_top, mine_low, right_top, right_low, left_top, left_low, top, bottom)
     near = near_product(ainv, own, where)
     near, *others = fence(

time: 212 us -> 208 us (0.981)
  waiting for transfers between devices: 66.2 us -> 63.4 us
  Pallas kernels: 45.6 us -> 43 us
  starting transfers between devices: 69 us -> 71.4 us
    ppermute x29, waiting for transfers between devices: 51.5 us -> 48.6 us  [shift(): lax.ppermute(array, axis, [(i, (i + by) % size) for i in range(size)])]
    pallas_call x2, Pallas kernels: 25.8 us -> 23.1 us  [far_product(): pl.pallas_call(functools.partial(far_kernel, columns), grid_spec=pltpu.Pr...]
  transfers between devices with their start and end apart: 32 -> 32, of which waited for: 16 -> 14; matrix products, arithmetic and copies ran while one was open for 8% -> 8% of each run, Pallas kernels for 16% -> 15%
where the time goes in v6:
time: 208 us
  starting transfers between devices  71.4 us (34%)
  waiting for transfers between devices  63.4 us (30%)
  Pallas kernels  43 us (21%)
  other arithmetic  19.1 us (9%)
  local copies, waits for them, and re-layouts  4.92 us (2%)
  matrix products  4.39 us (2%)
    ppermute x29, starting transfers between devices, shift(): lax.ppermute(array, axis, [(i, (i + by) % size) for i in range(size)])  61.7 us
    ppermute x29, waiting for transfers between devices, shift(): lax.ppermute(array, axis, [(i, (i + by) % size) for i in range(size)])  48.6 us
    pallas_call x2, Pallas kernels, far_product(): pl.pallas_call(functools.partial(far_kernel, columns), grid_spec=pltpu.Pr...  23.1 us
    pallas_call x1, Pallas kernels, near_product(): pl.pallas_call(near_kernel, grid_spec=pltpu.PrefetchScalarGridSpec(num_sc...  19.9 us
    all_to_all x1, waiting for transfers between devices, sum_diag(): lax.all_to_all(terms, ('zh', 'x', 'zl', 'y'), 0, 0, tiled=True)  14.7 us
    all_to_all x1, starting transfers between devices, sum_diag(): lax.all_to_all(terms, ('zh', 'x', 'zl', 'y'), 0, 0, tiled=True)  8.31 us
    dot_general x2, matrix products, diag_term(): lax.dot_general(panel, rows, (((0,), (0,)), ((), ())), precision=lax.Prec...  4.39 us
  transfers between devices with their start and end apart: 32, of which 14 were waited for; matrix products, arithmetic and copies ran while one was open for 8% of the time, Pallas kernels for 15%

profile of v6, /device:TPU:0, one launch (start us, length us, event | category | flops | bytes accessed | tf_op | source)
XLA Modules:
  0.0 207.7 jit_solution(16902617570835948285)
XLA Ops:
  4.7 9.3 %collective-permute-start.1 = (f32[96,1024]{1,0:T(8,128)S(1)}, f32[96,1024]{1,0:T(8,128)S(1)}, u32[]{:S(2)}, u32[]{:S(2)}) collective-permute-start(f32[96,1024]{1,0:T(8,128)S(1)} %collective-permute-done.refs_0_), channel_id=1, source_target_pairs={{0,16},{16,32},{32,48},{48,0},{1,17},{17,33},{33,49},{49,1},{2,18}... | collective-permute-start | bytes 1179656 | tf_op jit(solution)/shard_map/ppermute | solution.py:17
  14.0 6.5 %collective-permute-start.2 = (f32[96,1024]{1,0:T(8,128)S(1)}, f32[96,1024]{1,0:T(8,128)S(1)}, u32[]{:S(2)}, u32[]{:S(2)}) collective-permute-start(f32[96,1024]{1,0:T(8,128)S(1)} %collective-permute-done.refs_0_), channel_id=1, source_target_pairs={{0,48},{16,0},{32,16},{48,32},{1,49},{17,1},{33,17},{49,33},{2,50}... | collective-permute-start | bytes 1179656 | tf_op jit(solution)/shard_map/ppermute | solution.py:17
  20.6 10.0 %collective-permute-done.1.refs_4_ = f32[96,1024]{1,0:T(8,128)S(1)} collective-permute-done((f32[96,1024]{1,0:T(8,128)S(1)}, f32[96,1024]{1,0:T(8,128)S(1)}, u32[]{:S(2)}, u32[]{:S(2)}) %collective-permute-start.1) | collective-permute-done | bytes 393248 | tf_op jit(solution)/shard_map/ppermute | solution.py:17
  35.3 4.7 %collective-permute-start.8 = (f32[192,1024]{1,0:T(8,128)}, f32[192,1024]{1,0:T(8,128)S(1)}, u32[]{:S(2)}, u32[]{:S(2)}) collective-permute-start(f32[192,1024]{1,0:T(8,128)} %pad_maximum_fusion.3), channel_id=1, source_target_pairs={{0,64},{64,0},{1,65},{65,1},{2,66},{66,2},{3,67},{67,3},{4,68},{68... | collective-permute-start | bytes 2359304 | tf_op jit(solution)/shard_map/ppermute | solution.py:17
  40.9 3.2 %collective-permute-done.4.refs_5_ = f32[96,1024]{1,0:T(8,128)S(1)} collective-permute-done((f32[96,1024]{1,0:T(8,128)S(1)}, f32[96,1024]{1,0:T(8,128)S(1)}, u32[]{:S(2)}, u32[]{:S(2)}) %collective-permute-start.4) | collective-permute-done | bytes 393248 | tf_op jit(solution)/shard_map/ppermute | solution.py:17
  44.1 3.4 %collective-permute-start.7 = (f32[96,1024]{1,0:T(8,128)S(1)}, f32[96,1024]{1,0:T(8,128)}, u32[]{:S(2)}, u32[]{:S(2)}) collective-permute-start(f32[96,1024]{1,0:T(8,128)S(1)} %collective-permute-done.5.refs_3_), channel_id=1, source_target_pairs={{0,48},{16,0},{32,16},{48,32},{1,49},{17,1},{33,17},{49,33},{2,50}... | collective-permute-start | bytes 1179656 | tf_op jit(solution)/shard_map/ppermute | solution.py:17
  52.8 3.4 %collective-permute-done.7.refs_7_ = f32[96,1024]{1,0:T(8,128)} collective-permute-done((f32[96,1024]{1,0:T(8,128)S(1)}, f32[96,1024]{1,0:T(8,128)}, u32[]{:S(2)}, u32[]{:S(2)}) %collective-permute-start.7) | collective-permute-done | bytes 393248 | tf_op jit(solution)/shard_map/ppermute | solution.py:17
  59.7 3.8 %collective-permute-start.9 = (f32[192,1024]{1,0:T(8,128)S(1)}, f32[192,1024]{1,0:T(8,128)S(1)}, u32[]{:S(2)}, u32[]{:S(2)}) collective-permute-start(f32[192,1024]{1,0:T(8,128)S(1)} %collective-permute-done.8.refs_0_), channel_id=1, source_target_pairs={{0,48},{16,0},{32,16},{48,32},{1,49},{17,1},{33,17},{49,33},{2,50}... | collective-permute-start | bytes 2359304 | tf_op jit(solution)/shard_map/ppermute | solution.py:17
  63.5 19.9 %shard_map.94 = f32[3072,1024]{1,0:T(8,128)} custom-call(s32[5]{0:T(128)S(1)} %stack.23.where, f32[3072,1536]{1,0:T(8,128)} %a_ref.1, f32[96,1024]{1,0:T(8,128)S(1)} %collective-permute-done.refs_0_, f32[96,1024]{1,0:T(8,128)S(1)} %collective-permute-done.3.refs_1_, f32[96,1024]{1,0:T(8,128)S(1)} %collective-permute-done.2.refs_2_, ...), custom_call_target="tpu_custom_call" | custom-call | flops 14495514624 | bytes 22020096 | tf_op jit(solution)/shard_map/pallas_call | solution.py:71
  83.4 11.6 %shard_map.95 = (f32[2,4,192,512]{3,2,1,0:T(8,128)S(1)}, f32[2,4,192,512]{3,2,1,0:T(8,128)S(1)}) custom-call(s32[5]{0:T(128)S(1)} %stack.23.where, f32[2,4,2,192,1536]{4,3,2,1,0:T(8,128)} %bitcast.78, f32[2,4,2,192,1024]{4,3,2,1,0:T(8,128)} %bitcast.80, f32[192,1024]{1,0:T(8,128)S(1)} %collective-permute-done.8.refs_0_, ...), custom_call_target="tpu_custom_call" | custom-call | flops 7247757312 | bytes 22020096 | tf_op jit(solution)/shard_map/pallas_call | solution.py:133
  95.2 11.6 %shard_map.96 = (f32[2,4,192,512]{3,2,1,0:T(8,128)S(1)}, f32[2,4,192,512]{3,2,1,0:T(8,128)S(1)}) custom-call(s32[5]{0:T(128)S(1)} %stack.23.where, f32[2,4,2,192,1536]{4,3,2,1,0:T(8,128)} %bitcast.79, f32[2,4,2,192,1024]{4,3,2,1,0:T(8,128)} %bitcast.81, f32[192,1024]{1,0:T(8,128)S(1)} %collective-permute-done.8.refs_0_, ...), custom_call_target="tpu_custom_call" | custom-call | flops 7247757312 | bytes 22020096 | tf_op jit(solution)/shard_map/pallas_call | solution.py:133
  111.5 3.8 %collective-permute-start.18 = (f32[192,512]{1,0:T(8,128)S(1)}, f32[192,512]{1,0:T(8,128)S(1)}, u32[]{:S(2)}, u32[]{:S(2)}) collective-permute-start(f32[192,512]{1,0:T(8,128)S(1)} %get-tuple-element.56), channel_id=1, source_target_pairs={{0,6},{2,0},{4,2},{6,4},{1,7},{3,1},{5,3},{7,5},{8,14},{10,8},{12,... | collective-permute-start | bytes 1179656 | tf_op jit(solution)/shard_map/ppermute | solution.py:17
  117.3 3.5 %collective-permute-start.26 = (f32[192,512]{1,0:T(8,128)S(1)}, f32[192,512]{1,0:T(8,128)S(1)}, u32[]{:S(2)}, u32[]{:S(2)}) collective-permute-start(f32[192,512]{1,0:T(8,128)S(1)} %get-tuple-element.62), channel_id=1, source_target_pairs={{0,6},{2,0},{4,2},{6,4},{1,7},{3,1},{5,3},{7,5},{8,14},{10,8},{12,... | collective-permute-start | bytes 1179656 | tf_op jit(solution)/shard_map/ppermute | solution.py:17
  120.8 4.5 %collective-permute-done.14 = f32[192,512]{1,0:T(8,128)S(1)} collective-permute-done((f32[192,512]{1,0:T(8,128)S(1)}, f32[192,512]{1,0:T(8,128)S(1)}, u32[]{:S(2)}, u32[]{:S(2)}) %collective-permute-start.14) | collective-permute-done | bytes 393248 | tf_op jit(solution)/shard_map/ppermute | solution.py:17
  126.2 3.3 %collective-permute-start.19 = (f32[192,512]{1,0:T(8,128)S(1)}, f32[192,512]{1,0:T(8,128)S(1)}, u32[]{:S(2)}, u32[]{:S(2)}) collective-permute-start(f32[192,512]{1,0:T(8,128)S(1)} %get-tuple-element.54), channel_id=1, source_target_pairs={{0,6},{2,0},{4,2},{6,4},{1,7},{3,1},{5,3},{7,5},{8,14},{10,8},{12,... | collective-permute-start | bytes 1179656 | tf_op jit(solution)/shard_map/ppermute | solution.py:17
  130.5 3.2 %collective-permute-done.22 = f32[192,512]{1,0:T(8,128)S(1)} collective-permute-done((f32[192,512]{1,0:T(8,128)S(1)}, f32[192,512]{1,0:T(8,128)S(1)}, u32[]{:S(2)}, u32[]{:S(2)}) %collective-permute-start.22) | collective-permute-done | bytes 393248 | tf_op jit(solution)/shard_map/ppermute | solution.py:17
  134.7 3.3 %collective-permute-start.27 = (f32[192,512]{1,0:T(8,128)}, f32[192,512]{1,0:T(8,128)}, u32[]{:S(2)}, u32[]{:S(2)}) collective-permute-start(f32[192,512]{1,0:T(8,128)} %get-tuple-element.60), channel_id=1, source_target_pairs={{0,6},{2,0},{4,2},{6,4},{1,7},{3,1},{5,3},{7,5},{8,14},{10,8},{12,... | collective-permute-start | bytes 1179656 | tf_op jit(solution)/shard_map/ppermute | solution.py:17
  138.0 4.1 %collective-permute-done.17 = f32[192,512]{1,0:T(8,128)S(1)} collective-permute-done((f32[192,512]{1,0:T(8,128)S(1)}, f32[192,512]{1,0:T(8,128)S(1)}, u32[]{:S(2)}, u32[]{:S(2)}) %collective-permute-start.17) | collective-permute-done | bytes 393248 | tf_op jit(solution)/shard_map/ppermute | solution.py:17
  144.3 6.2 %collective-permute-done.25 = f32[192,512]{1,0:T(8,128)S(1)} collective-permute-done((f32[192,512]{1,0:T(8,128)S(1)}, f32[192,512]{1,0:T(8,128)S(1)}, u32[]{:S(2)}, u32[]{:S(2)}) %collective-permute-start.25) | collective-permute-done | bytes 393248 | tf_op jit(solution)/shard_map/ppermute | solution.py:17
  155.7 3.0 %collective-permute-done.16 = f32[192,512]{1,0:T(8,128)} collective-permute-done((f32[192,512]{1,0:T(8,128)}, f32[192,512]{1,0:T(8,128)}, u32[]{:S(2)}, u32[]{:S(2)}) %collective-permute-start.16) | collective-permute-done | bytes 393248 | tf_op jit(solution)/shard_map/ppermute | solution.py:17
  166.1 3.9 %collective-permute-done.23 = f32[192,512]{1,0:T(8,128)S(1)} collective-permute-done((f32[192,512]{1,0:T(8,128)}, f32[192,512]{1,0:T(8,128)S(1)}, u32[]{:S(2)}, u32[]{:S(2)}) %collective-permute-start.23) | collective-permute-done | bytes 393248 | tf_op jit(solution)/shard_map/ppermute | solution.py:17
  174.4 3.0 %collective-permute-done.30 = f32[64,8,512]{2,1,0:T(8,128)} collective-permute-done((f32[64,8,512]{2,1,0:T(8,128)}, f32[64,8,512]{2,1,0:T(8,128)}, u32[]{:S(2)}, u32[]{:S(2)}) %collective-permute-start.30) | collective-permute-done | bytes 1048608 | tf_op jit(solution)/shard_map/ppermute | solution.py:17
  179.8 8.3 %all-to-all-start = ((f32[64,8,512]{2,1,0:T(8,128)}), f32[64,8,512]{2,1,0:T(8,128)S(1)}, u32[]{:S(2)}, u32[]{:S(2)}) async-start(f32[64,8,512]{2,1,0:T(8,128)} %bitcast_add_fusion), calls=%async_computation | async-start | bytes 2097152 | tf_op jit(solution)/shard_map/all_to_all | solution.py:193
  192.3 14.7 %all-to-all-done = f32[64,8,512]{2,1,0:T(8,128)S(1)} async-done(((f32[64,8,512]{2,1,0:T(8,128)}), f32[64,8,512]{2,1,0:T(8,128)S(1)}, u32[]{:S(2)}, u32[]{:S(2)}) %all-to-all-start) | async-done | bytes 1048608 | tf_op jit(solution)/shard_map/all_to_all | solution.py:193
  (88 shorter events, 54.0 us)
Async XLA Ops:
  4.0 16.5 %collective-permute-start.3 = (f32[96,1024]{1,0:T(8,128)S(1)}, f32[96,1024]{1,0:T(8,128)S(1)}, u32[]{:S(2)}, u32[]{:S(2)}) collective-permute-start(f32[96,1024]{1,0:T(8,128)S(1)} %get-tuple-element.65), channel_id=1, source_target_pairs={{0,0},{1,16},{2,32},{3,48},{4,64},{5,80},{6,96},{7,112},{8,1},{9,1... | collective-permute-start | bytes 1179656 | tf_op jit(solution)/shard_map/ppermute | solution.py:31
  4.7 25.8 %collective-permute-start.1 = (f32[96,1024]{1,0:T(8,128)S(1)}, f32[96,1024]{1,0:T(8,128)S(1)}, u32[]{:S(2)}, u32[]{:S(2)}) collective-permute-start(f32[96,1024]{1,0:T(8,128)S(1)} %collective-permute-done.refs_0_), channel_id=1, source_target_pairs={{0,16},{16,32},{32,48},{48,0},{1,17},{17,33},{33,49},{49,1},{2,18}... | collective-permute-start | bytes 1179656 | tf_op jit(solution)/shard_map/ppermute | solution.py:17
  14.0 17.1 %collective-permute-start.2 = (f32[96,1024]{1,0:T(8,128)S(1)}, f32[96,1024]{1,0:T(8,128)S(1)}, u32[]{:S(2)}, u32[]{:S(2)}) collective-permute-start(f32[96,1024]{1,0:T(8,128)S(1)} %collective-permute-done.refs_0_), channel_id=1, source_target_pairs={{0,48},{16,0},{32,16},{48,32},{1,49},{17,1},{33,17},{49,33},{2,50}... | collective-permute-start | bytes 1179656 | tf_op jit(solution)/shard_map/ppermute | solution.py:17
  31.2 13.0 %collective-permute-start.4 = (f32[96,1024]{1,0:T(8,128)S(1)}, f32[96,1024]{1,0:T(8,128)S(1)}, u32[]{:S(2)}, u32[]{:S(2)}) collective-permute-start(f32[96,1024]{1,0:T(8,128)S(1)} %collective-permute-done.3.refs_1_), channel_id=1, source_target_pairs={{0,16},{16,32},{32,48},{48,0},{1,17},{17,33},{33,49},{49,1},{2,18}... | collective-permute-start | bytes 1179656 | tf_op jit(solution)/shard_map/ppermute | solution.py:17
  35.3 24.3 %collective-permute-start.8 = (f32[192,1024]{1,0:T(8,128)}, f32[192,1024]{1,0:T(8,128)S(1)}, u32[]{:S(2)}, u32[]{:S(2)}) collective-permute-start(f32[192,1024]{1,0:T(8,128)} %pad_maximum_fusion.3), channel_id=1, source_target_pairs={{0,64},{64,0},{1,65},{65,1},{2,66},{66,2},{3,67},{67,3},{4,68},{68... | collective-permute-start | bytes 2359304 | tf_op jit(solution)/shard_map/ppermute | solution.py:17
  40.1 12.7 %collective-permute-start.6 = (f32[96,1024]{1,0:T(8,128)S(1)}, f32[96,1024]{1,0:T(8,128)S(1)}, u32[]{:S(2)}, u32[]{:S(2)}) collective-permute-start(f32[96,1024]{1,0:T(8,128)S(1)} %collective-permute-done.1.refs_4_), channel_id=1, source_target_pairs={{0,16},{16,32},{32,48},{48,0},{1,17},{17,33},{33,49},{49,1},{2,18}... | collective-permute-start | bytes 1179656 | tf_op jit(solution)/shard_map/ppermute | solution.py:17
  44.1 12.0 %collective-permute-start.7 = (f32[96,1024]{1,0:T(8,128)S(1)}, f32[96,1024]{1,0:T(8,128)}, u32[]{:S(2)}, u32[]{:S(2)}) collective-permute-start(f32[96,1024]{1,0:T(8,128)S(1)} %collective-permute-done.5.refs_3_), channel_id=1, source_target_pairs={{0,48},{16,0},{32,16},{48,32},{1,49},{17,1},{33,17},{49,33},{2,50}... | collective-permute-start | bytes 1179656 | tf_op jit(solution)/shard_map/ppermute | solution.py:17
  56.1 27.2 %collective-permute-start.11 = (f32[96,1024]{1,0:T(8,128)S(1)}, f32[96,1024]{1,0:T(8,128)S(1)}, u32[]{:S(2)}, u32[]{:S(2)}) collective-permute-start(f32[96,1024]{1,0:T(8,128)S(1)} %collective-permute-done.6.refs_6_), channel_id=1, source_target_pairs={{0,64},{64,0},{1,65},{65,1},{2,66},{66,2},{3,67},{67,3},{4,68},{68... | collective-permute-start | bytes 1179656 | tf_op jit(solution)/shard_map/ppermute | solution.py:17
  57.1 26.3 %collective-permute-start.12 = (f32[96,1024]{1,0:T(8,128)}, f32[96,1024]{1,0:T(8,128)S(1)}, u32[]{:S(2)}, u32[]{:S(2)}) collective-permute-start(f32[96,1024]{1,0:T(8,128)} %collective-permute-done.7.refs_7_), channel_id=1, source_target_pairs={{0,64},{64,0},{1,65},{65,1},{2,66},{66,2},{3,67},{67,3},{4,68},{68... | collective-permute-start | bytes 1179656 | tf_op jit(solution)/shard_map/ppermute | solution.py:17
  59.7 23.7 %collective-permute-start.9 = (f32[192,1024]{1,0:T(8,128)S(1)}, f32[192,1024]{1,0:T(8,128)S(1)}, u32[]{:S(2)}, u32[]{:S(2)}) collective-permute-start(f32[192,1024]{1,0:T(8,128)S(1)} %collective-permute-done.8.refs_0_), channel_id=1, source_target_pairs={{0,48},{16,0},{32,16},{48,32},{1,49},{17,1},{33,17},{49,33},{2,50}... | collective-permute-start | bytes 2359304 | tf_op jit(solution)/shard_map/ppermute | solution.py:17
  63.5 19.9 %collective-permute-start.10 = (f32[192,1024]{1,0:T(8,128)S(1)}, f32[192,1024]{1,0:T(8,128)S(1)}, u32[]{:S(2)}, u32[]{:S(2)}) collective-permute-start(f32[192,1024]{1,0:T(8,128)S(1)} %collective-permute-done.8.refs_0_), channel_id=1, source_target_pairs={{0,16},{16,32},{32,48},{48,0},{1,17},{17,33},{33,49},{49,1},{2,18}... | collective-permute-start | bytes 2359304 | tf_op jit(solution)/shard_map/ppermute | solution.py:17
  109.1 16.1 %collective-permute-start.14 = (f32[192,512]{1,0:T(8,128)S(1)}, f32[192,512]{1,0:T(8,128)S(1)}, u32[]{:S(2)}, u32[]{:S(2)}) collective-permute-start(f32[192,512]{1,0:T(8,128)S(1)} %get-tuple-element.55), channel_id=1, source_target_pairs={{0,2},{2,4},{4,6},{6,0},{1,3},{3,5},{5,7},{7,1},{8,10},{10,12},{12... | collective-permute-start | bytes 1179656 | tf_op jit(solution)/shard_map/ppermute | solution.py:17
  111.5 13.7 %collective-permute-start.18 = (f32[192,512]{1,0:T(8,128)S(1)}, f32[192,512]{1,0:T(8,128)S(1)}, u32[]{:S(2)}, u32[]{:S(2)}) collective-permute-start(f32[192,512]{1,0:T(8,128)S(1)} %get-tuple-element.56), channel_id=1, source_target_pairs={{0,6},{2,0},{4,2},{6,4},{1,7},{3,1},{5,3},{7,5},{8,14},{10,8},{12,... | collective-permute-start | bytes 1179656 | tf_op jit(solution)/shard_map/ppermute | solution.py:17
  117.3 16.4 %collective-permute-start.22 = (f32[192,512]{1,0:T(8,128)S(1)}, f32[192,512]{1,0:T(8,128)S(1)}, u32[]{:S(2)}, u32[]{:S(2)}) collective-permute-start(f32[192,512]{1,0:T(8,128)S(1)} %get-tuple-element.61), channel_id=1, source_target_pairs={{0,2},{2,4},{4,6},{6,0},{1,3},{3,5},{5,7},{7,1},{8,10},{10,12},{12... | collective-permute-start | bytes 1179656 | tf_op jit(solution)/shard_map/ppermute | solution.py:17
  117.3 16.4 %collective-permute-start.26 = (f32[192,512]{1,0:T(8,128)S(1)}, f32[192,512]{1,0:T(8,128)S(1)}, u32[]{:S(2)}, u32[]{:S(2)}) collective-permute-start(f32[192,512]{1,0:T(8,128)S(1)} %get-tuple-element.62), channel_id=1, source_target_pairs={{0,6},{2,0},{4,2},{6,4},{1,7},{3,1},{5,3},{7,5},{8,14},{10,8},{12,... | collective-permute-start | bytes 1179656 | tf_op jit(solution)/shard_map/ppermute | solution.py:17
  120.8 21.3 %collective-permute-start.17 = (f32[192,512]{1,0:T(8,128)S(1)}, f32[192,512]{1,0:T(8,128)S(1)}, u32[]{:S(2)}, u32[]{:S(2)}) collective-permute-start(f32[192,512]{1,0:T(8,128)S(1)} %get-tuple-element.57), channel_id=1, source_target_pairs={{0,2},{2,4},{4,6},{6,0},{1,3},{3,5},{5,7},{7,1},{8,10},{10,12},{12... | collective-permute-start | bytes 1179656 | tf_op jit(solution)/shard_map/ppermute | solution.py:17
  126.2 18.0 %collective-permute-start.19 = (f32[192,512]{1,0:T(8,128)S(1)}, f32[192,512]{1,0:T(8,128)S(1)}, u32[]{:S(2)}, u32[]{:S(2)}) collective-permute-start(f32[192,512]{1,0:T(8,128)S(1)} %get-tuple-element.54), channel_id=1, source_target_pairs={{0,6},{2,0},{4,2},{6,4},{1,7},{3,1},{5,3},{7,5},{8,14},{10,8},{12,... | collective-permute-start | bytes 1179656 | tf_op jit(solution)/shard_map/ppermute | solution.py:17
  129.4 33.7 %collective-permute-start.29 = (f32[192,1024]{1,0:T(8,128)}, f32[192,1024]{1,0:T(8,128)}, u32[]{:S(2)}, u32[]{:S(2)}) collective-permute-start(f32[192,1024]{1,0:T(8,128)} %mul.26), channel_id=1, source_target_pairs={{0,8},{8,0},{1,9},{9,1},{2,10},{10,2},{3,11},{11,3},{4,12},{12,4},... | collective-permute-start | bytes 2359304 | tf_op jit(solution)/shard_map/ppermute | solution.py:17
  133.7 16.9 %collective-permute-start.25 = (f32[192,512]{1,0:T(8,128)S(1)}, f32[192,512]{1,0:T(8,128)S(1)}, u32[]{:S(2)}, u32[]{:S(2)}) collective-permute-start(f32[192,512]{1,0:T(8,128)S(1)} %get-tuple-element.63), channel_id=1, source_target_pairs={{0,2},{2,4},{4,6},{6,0},{1,3},{3,5},{5,7},{7,1},{8,10},{10,12},{12... | collective-permute-start | bytes 1179656 | tf_op jit(solution)/shard_map/ppermute | solution.py:17
  134.7 17.7 %collective-permute-start.27 = (f32[192,512]{1,0:T(8,128)}, f32[192,512]{1,0:T(8,128)}, u32[]{:S(2)}, u32[]{:S(2)}) collective-permute-start(f32[192,512]{1,0:T(8,128)} %get-tuple-element.60), channel_id=1, source_target_pairs={{0,6},{2,0},{4,2},{6,4},{1,7},{3,1},{5,3},{7,5},{8,14},{10,8},{12,... | collective-permute-start | bytes 1179656 | tf_op jit(solution)/shard_map/ppermute | solution.py:17
  142.1 16.5 %collective-permute-start.16 = (f32[192,512]{1,0:T(8,128)}, f32[192,512]{1,0:T(8,128)}, u32[]{:S(2)}, u32[]{:S(2)}) collective-permute-start(f32[192,512]{1,0:T(8,128)} %get-tuple-element.58), channel_id=1, source_target_pairs={{0,6},{2,0},{4,2},{6,4},{1,7},{3,1},{5,3},{7,5},{8,14},{10,8},{12,... | collective-permute-start | bytes 1179656 | tf_op jit(solution)/shard_map/ppermute | solution.py:17
  144.2 16.4 %collective-permute-start.15 = (f32[192,512]{1,0:T(8,128)}, f32[192,512]{1,0:T(8,128)}, u32[]{:S(2)}, u32[]{:S(2)}) collective-permute-start(f32[192,512]{1,0:T(8,128)} %get-tuple-element.53), channel_id=1, source_target_pairs={{0,2},{2,4},{4,6},{6,0},{1,3},{3,5},{5,7},{7,1},{8,10},{10,12},{12... | collective-permute-start | bytes 1179656 | tf_op jit(solution)/shard_map/ppermute | solution.py:17
  152.4 13.7 %collective-permute-start.24 = (f32[192,512]{1,0:T(8,128)}, f32[192,512]{1,0:T(8,128)S(1)}, u32[]{:S(2)}, u32[]{:S(2)}) collective-permute-start(f32[192,512]{1,0:T(8,128)} %get-tuple-element.64), channel_id=1, source_target_pairs={{0,6},{2,0},{4,2},{6,4},{1,7},{3,1},{5,3},{7,5},{8,14},{10,8},{12,... | collective-permute-start | bytes 1179656 | tf_op jit(solution)/shard_map/ppermute | solution.py:17
  179.8 27.2 %all-to-all-start = ((f32[64,8,512]{2,1,0:T(8,128)}), f32[64,8,512]{2,1,0:T(8,128)S(1)}, u32[]{:S(2)}, u32[]{:S(2)}) async-start(f32[64,8,512]{2,1,0:T(8,128)} %bitcast_add_fusion), calls=%async_computation | async-start | bytes 2097152 | tf_op jit(solution)/shard_map/all_to_all | solution.py:193
  (15 other events, 211.0 us)
